TPU v7x, 128 devices: a whole 4x4x4 slice. The times are simulated.
128 devices in a mesh: section: 2 (over z_hi), seq: 8 (over y, z_lo), tensor: 8 (over x, core).
Axes of the slice: x: 4, y: 4, z: 4 (z_hi: 2, z_lo: 2; z = z_hi * 2 + z_lo), core: 2. Of those that a mesh axis runs over, the one named last changes fastest.
Arguments:
- ends: bfloat16 [2, 1024, 9, 1024], P('section', ('seq', 'tensor')), may hold values from -6 to 6
- w_qkv: bfloat16 [2, 1024, 3072], P('section', 'seq', 'tensor'), may hold values from -0.25 to 0.25
- qv_bias: bfloat16 [2, 32, 64], P('section', 'tensor', 'seq'), may hold values from -2.5 to 2.5
- w_proj: bfloat16 [2, 1024, 1024], P('section', 'tensor', 'seq'), may hold values from -0.1875 to 0.1875
- w_fc1: bfloat16 [2, 1024, 4096], P('section', 'seq', 'tensor'), may hold values from -0.1875 to 0.1875
- fc1_bias: bfloat16 [2, 64, 64], P('section', 'tensor', 'seq'), may hold values from -2.5 to 2.5
- w_fc2: bfloat16 [2, 4096, 1024], P('section', 'tensor', 'seq'), may hold values from -0.09375 to 0.09375
- vectors: float32 [2, 8, 1024], P('section', None, ('seq', 'tensor')), may hold values from -1 to 1.6, as said below
Outputs:
- ends_out: bfloat16 [2, 1024, 9, 1024], P('section', ('seq', 'tensor'))
- grad_qkv: float32 [2, 1024, 3072], P('section', 'seq', 'tensor')
- grad_qv_bias: float32 [2, 32, 64], P('section', 'tensor', 'seq')
- grad_proj: float32 [2, 1024, 1024], P('section', 'tensor', 'seq')
- grad_fc1: float32 [2, 1024, 4096], P('section', 'seq', 'tensor')
- grad_fc1_bias: float32 [2, 64, 64], P('section', 'tensor', 'seq')
- grad_fc2: float32 [2, 4096, 1024], P('section', 'tensor', 'seq')
- grad_vectors: float32 [2, 8, 1024], P('section', None, ('seq', 'tensor'))
Inputs may be any that keep to these rules, and one draw needn't show every extreme that they name: `vectors`: rows 0, 2, 6 and 7 of each layer lie between 0.4 and 1.6.
All inputs are finite; a program needn't handle non-finite values.
Results may differ from a plain program's by a relative error of at most 0.024.
Values may be sent and summed in bfloat16 or wider, within the bound.
No kernel may reach another device: no remote copies, remote signals or barrier semaphores. Data moves between devices by JAX's collectives and lax.ppermute only.
A program may use at most 192 MiB of HBM per device.

v0:
```python
import jax
import jax.numpy as jnp
from jax import lax
from jax.sharding import PartitionSpec as P

LENGTH = 1024
MICRO = 4
MB_IMG = 2


epsilon = 1e-06


def shifted(block, axis, distance):
    devices = range(lax.axis_size(axis))
    route = [(i - distance, i) for i in devices if i - distance in devices]
    return lax.ppermute(block, axis, route)


def layer_norm(row_data, gain_row, shift_row):
    row_mean = jnp.mean(row_data, axis=-1, keepdims=True)
    centred = row_data - row_mean
    row_var = jnp.mean(centred * centred, axis=-1, keepdims=True)
    return centred * lax.rsqrt(row_var + epsilon) * gain_row + shift_row


def gelu_exact(values_in):
    return jax.nn.gelu(values_in, approximate=False)


def fit_slots(array_in, slot_count):
    present = array_in.shape[1]
    if present >= slot_count:
        return array_in
    padding = [(0, 0)] * array_in.ndim
    padding[1] = (0, slot_count - present)
    return jnp.pad(array_in, padding)


def widen_rows(row_data):
    return lax.all_gather(row_data, "tensor", axis=0, tiled=True)


def narrow(values_in, weight_in):

    def term_rows(row_start, row_count):
        return jnp.einsum("qsc,cd->qsd", values_in, weight_in, preferred_element_type=jnp.float32)

    return lax.psum_scatter(
        term_rows(
            jnp.int32(0), values_in.shape[0] // lax.axis_size("tensor") * lax.axis_size("tensor")
        ).astype(jnp.bfloat16),
        "tensor",
        scatter_dimension=0,
        tiled=True,
    ).astype(jnp.float32)


def narrow_back(grads_in, weight_in):

    def term_rows(row_start, row_count):
        return jnp.einsum("qsc,dc->qsd", grads_in, weight_in, preferred_element_type=jnp.float32)

    return lax.psum_scatter(
        term_rows(
            jnp.int32(0), grads_in.shape[0] // lax.axis_size("tensor") * lax.axis_size("tensor")
        ).astype(jnp.bfloat16),
        "tensor",
        scatter_dimension=0,
        tiled=True,
    ).astype(jnp.float32)


def widen_back(grad_rows, used_rows, weight_in):
    piece_rows = lax.all_gather(grad_rows, "tensor", axis=0, tiled=True)
    weight_grad = jnp.einsum(
        "qsc,qsd->cd", used_rows, piece_rows, preferred_element_type=jnp.float32
    )
    piece_grad = jnp.einsum(
        "qsd,cd->qsc", piece_rows, weight_in, preferred_element_type=jnp.float32
    )
    return (weight_grad, piece_grad)


def block_scores(queries, keys_block, score_scale):
    return (
        jnp.einsum("qshe,kshe->qshk", queries, keys_block, preferred_element_type=jnp.float32)
        * score_scale
    )


def on_device(ends, w_qkv, qv_bias, w_proj, w_fc1, fc1_bias, w_fc2, vectors):
    is_first = lax.axis_index("section") == 0
    w_mix, w_out, w_up, w_down, b_mix, b_up = (
        lax.all_gather(w_qkv, "seq", axis=1, tiled=True),
        lax.all_gather(w_proj, "seq", axis=2, tiled=True),
        lax.all_gather(w_fc1, "seq", axis=1, tiled=True),
        lax.all_gather(w_fc2, "seq", axis=2, tiled=True),
        lax.all_gather(qv_bias, "seq", axis=2, tiled=True),
        lax.all_gather(fc1_bias, "seq", axis=2, tiled=True),
    )
    w_mix, w_out, w_up, w_down = (w_mix[0], w_out[0], w_up[0], w_down[0])
    heads_local = b_mix.shape[1] // 2
    head_size = b_mix.shape[2]
    bias_mix = b_mix[0].astype(jnp.float32).reshape(heads_local, 2, head_size)
    bias_up = b_up[0].astype(jnp.float32).reshape(-1)
    params = lax.all_gather(vectors, ("seq", "tensor"), axis=2, tiled=True)[0]
    score_scale = head_size ** (-0.5)
    key_block = min(LENGTH, 256)
    block_total = LENGTH // key_block
    local_rows = ends.shape[1]
    features = ends.shape[3]
    batch_sizes = [MB_IMG + 1] + [MB_IMG] * (MICRO - 1)

    def batch_rows(batch_id, slot_count):
        if 0 <= batch_id < MICRO:
            start_at = sum(batch_sizes[:batch_id])
            return fit_slots(ends[0][:, start_at : start_at + batch_sizes[batch_id]], slot_count)
        return jnp.zeros((local_rows, slot_count, features), ends.dtype)

    stash_map = {}
    forward_results = {}
    backward_results = {}
    inbox_fwd = None
    inbox_back = None
    weight_total = None
    vector_total = jnp.zeros((8, features), jnp.float32)
    for tick_id in range(MICRO + 2):
        if tick_id <= MICRO:
            slot_count = MB_IMG + 1
            own_rows = batch_rows(tick_id, slot_count)
            if inbox_fwd is None:
                received = jnp.zeros_like(own_rows)
            else:
                received = fit_slots(inbox_fwd, slot_count)
            forward_x_low = jnp.where(is_first, own_rows, received)
            x_in = forward_x_low.astype(jnp.float32)
            forward_a_wide = widen_rows(layer_norm(x_in, params[0], params[1]).astype(jnp.bfloat16))
            forward_q_rows = forward_a_wide.shape[0]
            forward_slot_count = forward_a_wide.shape[1]
            mixed_cols = jnp.einsum(
                "qsd,dc->qsc", forward_a_wide, w_mix, preferred_element_type=jnp.float32
            )
            mixed_cols = mixed_cols.reshape(
                forward_q_rows, forward_slot_count, heads_local, 3, head_size
            )
            forward_queries = (mixed_cols[:, :, :, 0] + bias_mix[:, 0]).astype(jnp.bfloat16)
            keys_proj = mixed_cols[:, :, :, 1].astype(jnp.bfloat16)
            values_proj = (mixed_cols[:, :, :, 2] + bias_mix[:, 1]).astype(jnp.bfloat16)
            forward_keys_all = lax.all_gather(keys_proj, "seq", axis=0, tiled=True)
            forward_values_all = lax.all_gather(values_proj, "seq", axis=0, tiled=True)
            run_max = jnp.full(
                (forward_q_rows, forward_slot_count, heads_local), -jnp.inf, jnp.float32
            )
            run_sum = jnp.zeros((forward_q_rows, forward_slot_count, heads_local), jnp.float32)
            for forward_block_id in range(block_total):
                scores = block_scores(
                    forward_queries,
                    forward_keys_all[
                        forward_block_id * key_block : (forward_block_id + 1) * key_block
                    ],
                    score_scale,
                )
                new_max = jnp.maximum(run_max, jnp.max(scores, axis=-1))
                run_sum = run_sum * jnp.exp(run_max - new_max) + jnp.sum(
                    jnp.exp(scores - new_max[..., None]), axis=-1
                )
                run_max = new_max
            forward_log_total = run_max + jnp.log(run_sum)
            forward_summed = jnp.zeros(
                (forward_q_rows, forward_slot_count, heads_local, head_size), jnp.float32
            )
            for forward_block_id in range(block_total):
                forward_chosen = slice(
                    forward_block_id * key_block, (forward_block_id + 1) * key_block
                )
                scores = block_scores(
                    forward_queries, forward_keys_all[forward_chosen], score_scale
                )
                probs_low = jnp.exp(scores - forward_log_total[..., None]).astype(jnp.bfloat16)
                forward_summed = forward_summed + jnp.einsum(
                    "qshk,kshe->qshe",
                    probs_low,
                    forward_values_all[forward_chosen],
                    preferred_element_type=jnp.float32,
                )
            forward_attended = forward_summed.astype(jnp.bfloat16).reshape(
                forward_q_rows, forward_slot_count, heads_local * head_size
            )
            forward_proj_sum = narrow(forward_attended, w_out)
            forward_middle = x_in + params[6] * (forward_proj_sum + params[4])
            forward_a2_wide = widen_rows(
                layer_norm(forward_middle, params[2], params[3]).astype(jnp.bfloat16)
            )
            forward_hidden = (
                jnp.einsum("qsd,df->qsf", forward_a2_wide, w_up, preferred_element_type=jnp.float32)
                + bias_up
            )
            forward_down_sum = narrow(gelu_exact(forward_hidden).astype(jnp.bfloat16), w_down)
            result = (forward_middle + params[7] * (forward_down_sum + params[5])).astype(
                jnp.bfloat16
            )
            forward_stashed = (
                forward_x_low,
                forward_a_wide,
                forward_queries,
                forward_keys_all,
                forward_values_all,
                forward_log_total,
                forward_summed,
                forward_proj_sum,
                forward_middle,
                forward_a2_wide,
                forward_hidden,
                forward_down_sum,
            )
            result, stashed = (result, forward_stashed)
            stash_map[tick_id] = stashed
            forward_results[tick_id] = result
            if tick_id < MICRO:
                inbox_fwd = shifted(result, "section", 1)
        if tick_id >= 1:
            slot_count = MB_IMG + 1
            cot_rows = batch_rows(tick_id - 1, slot_count)
            if inbox_back is None:
                received = jnp.zeros_like(cot_rows)
            else:
                received = fit_slots(inbox_back, slot_count)
            if 2 <= tick_id <= MICRO:
                earlier = [fit_slots(stored, slot_count) for stored in stash_map[tick_id - 2]]
                later = [fit_slots(stored, slot_count) for stored in stash_map[tick_id]]
                stashed = tuple(
                    (
                        jnp.where(is_first, old_one, new_one)
                        for old_one, new_one in zip(earlier, later)
                    )
                )
            elif tick_id <= MICRO:
                stashed = tuple((fit_slots(stored, slot_count) for stored in stash_map[tick_id]))
            else:
                stashed = tuple(
                    (fit_slots(stored, slot_count) for stored in stash_map[tick_id - 2])
                )
            (
                x_low,
                a_wide,
                queries,
                keys_all,
                values_all,
                log_total,
                summed,
                proj_sum,
                middle,
                a2_wide,
                hidden,
                down_sum,
            ) = stashed
            q_rows = a_wide.shape[0]
            backward_slot_count = a_wide.shape[1]
            grad_out = jnp.where(is_first, received, cot_rows).astype(jnp.float32)
            grad_ls2 = jnp.sum(grad_out * (down_sum + params[5]), axis=(0, 1))
            grad_bias2 = jnp.sum(grad_out, axis=(0, 1)) * params[7]
            grad_down_low = (params[7] * grad_out).astype(jnp.bfloat16)
            grad_w_down, grad_act = widen_back(
                grad_down_low, gelu_exact(hidden).astype(jnp.bfloat16), w_down
            )
            grad_hidden = jax.vjp(gelu_exact, hidden)[1](grad_act)[0].astype(jnp.bfloat16)
            grad_b_up = jnp.sum(grad_hidden.astype(jnp.float32), axis=(0, 1))
            grad_w_up = jnp.einsum(
                "qsd,qsf->df", a2_wide, grad_hidden, preferred_element_type=jnp.float32
            )
            grad_norm2 = narrow_back(grad_hidden, w_up)
            norm_pull = jax.vjp(layer_norm, middle, params[2], params[3])[1]
            grad_mid_part, grad_g2, grad_b2 = norm_pull(grad_norm2)
            grad_mid = grad_out + grad_mid_part
            grad_ls1 = jnp.sum(grad_mid * (proj_sum + params[4]), axis=(0, 1))
            grad_bias1 = jnp.sum(grad_mid, axis=(0, 1)) * params[6]
            grad_proj_low = (params[6] * grad_mid).astype(jnp.bfloat16)
            attended = summed.astype(jnp.bfloat16).reshape(
                q_rows, backward_slot_count, heads_local * head_size
            )
            grad_w_out, grad_att = widen_back(grad_proj_low, attended, w_out)
            grad_att_low = grad_att.astype(jnp.bfloat16).reshape(
                q_rows, backward_slot_count, heads_local, head_size
            )
            row_delta = jnp.zeros((q_rows, backward_slot_count, heads_local), jnp.float32)
            for block_id in range(block_total):
                chosen = slice(block_id * key_block, (block_id + 1) * key_block)
                probs = jnp.exp(
                    block_scores(queries, keys_all[chosen], score_scale) - log_total[..., None]
                )
                grad_probs = jnp.einsum(
                    "qshe,kshe->qshk",
                    grad_att_low,
                    values_all[chosen],
                    preferred_element_type=jnp.float32,
                )
                row_delta = row_delta + jnp.sum(probs * grad_probs, axis=-1)
            grad_query = jnp.zeros(
                (q_rows, backward_slot_count, heads_local, head_size), jnp.float32
            )
            key_parts = []
            value_parts = []
            for block_id in range(block_total):
                chosen = slice(block_id * key_block, (block_id + 1) * key_block)
                keys_block = keys_all[chosen]
                probs = jnp.exp(
                    block_scores(queries, keys_block, score_scale) - log_total[..., None]
                )
                value_parts.append(
                    jnp.einsum(
                        "qshk,qshe->kshe",
                        probs.astype(jnp.bfloat16),
                        grad_att_low,
                        preferred_element_type=jnp.float32,
                    )
                )
                grad_probs = jnp.einsum(
                    "qshe,kshe->qshk",
                    grad_att_low,
                    values_all[chosen],
                    preferred_element_type=jnp.float32,
                )
                grad_scores = (probs * (grad_probs - row_delta[..., None])).astype(jnp.bfloat16)
                grad_query = (
                    grad_query
                    + jnp.einsum(
                        "qshk,kshe->qshe",
                        grad_scores,
                        keys_block,
                        preferred_element_type=jnp.float32,
                    )
                    * score_scale
                )
                key_parts.append(
                    jnp.einsum(
                        "qshk,qshe->kshe", grad_scores, queries, preferred_element_type=jnp.float32
                    )
                    * score_scale
                )
            grad_keys = lax.psum_scatter(
                jnp.concatenate(key_parts, axis=0).astype(jnp.bfloat16),
                "seq",
                scatter_dimension=0,
                tiled=True,
            )
            grad_values = lax.psum_scatter(
                jnp.concatenate(value_parts, axis=0).astype(jnp.bfloat16),
                "seq",
                scatter_dimension=0,
                tiled=True,
            )
            grad_q_low = grad_query.astype(jnp.bfloat16)
            grad_b_mix = jnp.stack(
                [
                    jnp.sum(grad_q_low.astype(jnp.float32), axis=(0, 1)),
                    jnp.sum(grad_values.astype(jnp.float32), axis=(0, 1)),
                ],
                axis=1,
            )
            grad_b_mix = grad_b_mix.reshape(2 * heads_local, head_size)
            grad_mixed = jnp.stack([grad_q_low, grad_keys, grad_values], axis=3)
            grad_mixed = grad_mixed.reshape(
                q_rows, backward_slot_count, 3 * heads_local * head_size
            )
            grad_w_mix = jnp.einsum(
                "qsd,qsc->dc", a_wide, grad_mixed, preferred_element_type=jnp.float32
            )
            grad_norm1 = narrow_back(grad_mixed, w_mix)
            norm_pull = jax.vjp(layer_norm, x_low.astype(jnp.float32), params[0], params[1])[1]
            grad_in_part, grad_g1, grad_b1 = norm_pull(grad_norm1)
            grad_input = (grad_mid + grad_in_part).astype(jnp.bfloat16)
            vector_grads = jnp.stack(
                [grad_g1, grad_b1, grad_g2, grad_b2, grad_bias1, grad_bias2, grad_ls1, grad_ls2]
            )
            weight_grads = (
                grad_w_mix,
                grad_w_out,
                grad_w_up,
                grad_w_down,
                grad_b_mix,
                grad_b_up.reshape(-1, head_size),
            )
            grad_input, weight_grads, vector_grads = (grad_input, weight_grads, vector_grads)
            backward_results[tick_id] = grad_input
            vector_total = vector_total + vector_grads
            if weight_total is None:
                weight_total = weight_grads
            else:
                weight_total = tuple(
                    (before + added for before, added in zip(weight_total, weight_grads))
                )
            if tick_id <= MICRO:
                inbox_back = shifted(grad_input, "section", -1)
    weight_total = (
        lax.psum_scatter(
            weight_total[0].astype(jnp.bfloat16), "seq", scatter_dimension=0, tiled=True
        ).astype(jnp.float32),
        lax.psum_scatter(
            weight_total[1].astype(jnp.bfloat16), "seq", scatter_dimension=1, tiled=True
        ).astype(jnp.float32),
        lax.psum_scatter(
            weight_total[2].astype(jnp.bfloat16), "seq", scatter_dimension=0, tiled=True
        ).astype(jnp.float32),
        lax.psum_scatter(
            weight_total[3].astype(jnp.bfloat16), "seq", scatter_dimension=1, tiled=True
        ).astype(jnp.float32),
        lax.psum_scatter(
            weight_total[4].astype(jnp.bfloat16), "seq", scatter_dimension=1, tiled=True
        ).astype(jnp.float32),
        lax.psum_scatter(
            weight_total[5].astype(jnp.bfloat16), "seq", scatter_dimension=1, tiled=True
        ).astype(jnp.float32),
    )
    vector_shard = lax.psum_scatter(
        vector_total, ("seq", "tensor"), scatter_dimension=1, tiled=True
    )
    pieces = []
    for batch_id in range(MICRO):
        count_now = batch_sizes[batch_id]
        later_out = forward_results[batch_id + 1][:, :count_now]
        back_out = backward_results[batch_id + 2][:, :count_now]
        pieces.append(jnp.where(is_first, back_out, later_out))
    ends_out = jnp.concatenate(pieces, axis=1)[None]
    return (
        ends_out,
        weight_total[0][None],
        weight_total[4][None],
        weight_total[1][None],
        weight_total[2][None],
        weight_total[5][None],
        weight_total[3][None],
        vector_shard[None],
    )


def solution(mesh):
    placed = (
        P("section", ("seq", "tensor"), None, None),
        P("section", "seq", "tensor"),
        P("section", "tensor", "seq"),
        P("section", "tensor", "seq"),
        P("section", "seq", "tensor"),
        P("section", "tensor", "seq"),
        P("section", "tensor", "seq"),
        P("section", None, ("seq", "tensor")),
    )
    return jax.shard_map(
        on_device,
        mesh=mesh,
        in_specs=placed,
        out_specs=(
            P("section", ("seq", "tensor"), None, None),
            P("section", "seq", "tensor"),
            P("section", "tensor", "seq"),
            P("section", "tensor", "seq"),
            P("section", "seq", "tensor"),
            P("section", "tensor", "seq"),
            P("section", "tensor", "seq"),
            P("section", None, ("seq", "tensor")),
        ),
        check_vma=False,
    )
```

profile of v0, /device:TPU:0, one launch (start us, length us, event | category | flops | bytes accessed | tf_op | source)
XLA Modules:
  0.0 2478.0 jit_solution(5662271258107209305)
XLA Ops:
  8.1 30.3 %all_gather.113 = bf16[1,1024,384]{2,1,0:T(8,128)(2,1)S(1)} all-gather(bf16[1,128,384]{2,1,0:T(8,128)(2,1)} %param.9), channel_id=1, replica_groups=mesh['section'=2,'seq'=8,'tensor'=8] {'seq'}, dimensions={1}, use_global_device_ids=true | all-gather | bytes 884736 | tf_op jit(solution)/shard_map/all_gather | solution.py:95
  38.7 83.9 %all_gather.111 = f32[1,8,1024]{1,0,2:T(1,128)S(1)} all-gather(f32[1,8,16]{1,0,2:T(1,128)S(1)} %copy.498), channel_id=1, replica_groups=mesh['section'=2,'seq'=8,'tensor'=8] {'seq','tensor'}, dimensions={2}, use_global_device_ids=true | all-gather | bytes 33280 | tf_op jit(solution)/shard_map/all_gather | solution.py:107
  122.7 25.9 %slice_reduce_fusion.3 = (f32[1024]{0:T(1024)S(1)}, f32[1024]{0:T(1024)S(1)}, f32[1024]{0:T(1024)S(1)}, f32[1024]{0:T(1024)S(1)}, f32[1024]{0:T(1024)S(1)}, /*in...) fusion(f32[1,8,1024]{1,0,2:T(1,128)S(1)} %all_gather.111), kind=kLoop, calls=%fused_computation.634 | loop fusion | bytes 65536 | tf_op jit(solution)/shard_map/slice | solution.py:200
  162.6 28.1 %all_gather.114 = bf16[1,4,64]{1,0,2:T(2,128)(2,1)S(1)} all-gather(bf16[1,4,8]{1,0,2:T(2,128)(2,1)S(1)} %copy.500), channel_id=1, replica_groups=mesh['section'=2,'seq'=8,'tensor'=8] {'seq'}, dimensions={2}, use_global_device_ids=true | all-gather | bytes 576 | tf_op jit(solution)/shard_map/all_gather | solution.py:99
  191.4 26.0 %all-gather = bf16[1024,3,2,1,64]{0,4,3,2,1:T(8,128)(2,1)S(1)} all-gather(bf16[128,3,2,1,64]{0,4,3,2,1:T(8,128)(2,1)S(1)} %slice.988), channel_id=2, replica_groups=mesh['section'=2,'seq'=8,'tensor'=8] {'seq'}, dimensions={0}, use_global_device_ids=true | all-gather | bytes 884736 | tf_op jit(solution)/shard_map/all_gather | solution.py:150
  218.9 26.2 %all_gather.115 = bf16[1024,3,2,64]{0,3,2,1:T(8,128)(2,1)S(1)} all-gather(bf16[128,3,2,64]{0,3,2,1:T(8,128)(2,1)S(1)} %get-tuple-element.199), channel_id=1, replica_groups=mesh['section'=2,'seq'=8,'tensor'=8] {'seq'}, dimensions={0}, use_global_device_ids=true | all-gather | bytes 884736 | tf_op jit(solution)/shard_map/all_gather | solution.py:151
  246.9 24.2 all_gather.117
  273.8 28.3 %all_gather.120 = bf16[1,8,64]{1,0,2:T(2,128)(2,1)S(1)} all-gather(bf16[1,8,8]{1,0,2:T(2,128)(2,1)S(1)} %copy.507), channel_id=1, replica_groups=mesh['section'=2,'seq'=8,'tensor'=8] {'seq'}, dimensions={2}, use_global_device_ids=true | all-gather | bytes 1152 | tf_op jit(solution)/shard_map/all_gather | solution.py:100
  323.3 30.9 %all-gather.10.cloned.1.call-done = bf16[1,512,1024]{2,1,0:T(8,128)(2,1)} async-done(((bf16[1,512,128]{2,1,0:T(8,128)(2,1)}), bf16[1,512,1024]{2,1,0:T(8,128)(2,1)}) %all-gather.10.cloned.1.call-update) | async-done | bytes 1048592 | tf_op jit(solution)/shard_map/all_gather | solution.py:98
  358.9 33.9 %reduce-scatter.66.cloned.1.call-done = bf16[16,3,1024]{2,0,1:T(8,128)(2,1)} async-done(((bf16[128,3,1024]{2,0,1:T(8,128)(2,1)}), bf16[16,3,1024]{2,0,1:T(8,128)(2,1)}) %reduce-scatter.66.cloned.1.call-update) | async-done | bytes 98320 | tf_op jit(solution)/shard_map/reduce_scatter | solution.py:49
  417.6 27.4 %all-gather.1 = bf16[1024,3,2,1,64]{0,4,3,2,1:T(8,128)(2,1)S(1)} all-gather(bf16[128,3,2,1,64]{0,4,3,2,1:T(8,128)(2,1)S(1)} %slice.987), channel_id=3, replica_groups=mesh['section'=2,'seq'=8,'tensor'=8] {'seq'}, dimensions={0}, use_global_device_ids=true | all-gather | bytes 884736 | tf_op jit(solution)/shard_map/all_gather | solution.py:150
  446.4 26.6 %all_gather.123 = bf16[1024,3,2,64]{0,3,2,1:T(8,128)(2,1)S(1)} all-gather(bf16[128,3,2,64]{0,3,2,1:T(8,128)(2,1)S(1)} %get-tuple-element.198), channel_id=1, replica_groups=mesh['section'=2,'seq'=8,'tensor'=8] {'seq'}, dimensions={0}, use_global_device_ids=true | all-gather | bytes 884736 | tf_op jit(solution)/shard_map/all_gather | solution.py:151
  476.1 31.2 %reduce-scatter.68.cloned.1.call-done = bf16[16,3,1024]{2,0,1:T(8,128)(2,1)} async-done(((bf16[128,3,1024]{2,0,1:T(8,128)(2,1)}), bf16[16,3,1024]{2,0,1:T(8,128)(2,1)}) %reduce-scatter.68.cloned.1.call-update) | async-done | bytes 98320 | tf_op jit(solution)/shard_map/reduce_scatter | solution.py:49
  532.3 31.3 %reduce-scatter.74.cloned.1.call-done = bf16[16,3,1024]{2,0,1:T(8,128)(2,1)} async-done(((bf16[128,3,1024]{2,0,1:T(8,128)(2,1)}), bf16[16,3,1024]{2,0,1:T(8,128)(2,1)}) %reduce-scatter.74.cloned.1.call-update) | async-done | bytes 98320 | tf_op jit(solution)/shard_map/reduce_scatter | solution.py:49
  589.4 27.6 %all-gather.2 = bf16[1024,3,2,1,64]{0,4,3,2,1:T(8,128)(2,1)S(1)} all-gather(bf16[128,3,2,1,64]{0,4,3,2,1:T(8,128)(2,1)S(1)} %slice.986), channel_id=4, replica_groups=mesh['section'=2,'seq'=8,'tensor'=8] {'seq'}, dimensions={0}, use_global_device_ids=true | all-gather | bytes 884736 | tf_op jit(solution)/shard_map/all_gather | solution.py:150
  618.5 26.9 %all_gather.129 = bf16[1024,3,2,64]{0,3,2,1:T(8,128)(2,1)S(1)} all-gather(bf16[128,3,2,64]{0,3,2,1:T(8,128)(2,1)S(1)} %fusion.564), channel_id=1, replica_groups=mesh['section'=2,'seq'=8,'tensor'=8] {'seq'}, dimensions={0}, use_global_device_ids=true | all-gather | bytes 884736 | tf_op jit(solution)/shard_map/all_gather | solution.py:151
  649.0 30.7 %reduce-scatter.76.cloned.1.call-done = bf16[16,3,1024]{2,0,1:T(8,128)(2,1)} async-done(((bf16[128,3,1024]{2,0,1:T(8,128)(2,1)}), bf16[16,3,1024]{2,0,1:T(8,128)(2,1)}) %reduce-scatter.76.cloned.1.call-update) | async-done | bytes 98320 | tf_op jit(solution)/shard_map/reduce_scatter | solution.py:49
  702.9 31.2 %reduce-scatter.82.cloned.1.call-done = bf16[16,3,1024]{2,0,1:T(8,128)(2,1)} async-done(((bf16[128,3,1024]{2,0,1:T(8,128)(2,1)}), bf16[16,3,1024]{2,0,1:T(8,128)(2,1)}) %reduce-scatter.82.cloned.1.call-update) | async-done | bytes 98320 | tf_op jit(solution)/shard_map/reduce_scatter | solution.py:49
  759.6 27.6 %all-gather.3 = bf16[1024,3,2,1,64]{0,4,3,2,1:T(8,128)(2,1)S(1)} all-gather(bf16[128,3,2,1,64]{0,4,3,2,1:T(8,128)(2,1)S(1)} %slice.985), channel_id=5, replica_groups=mesh['section'=2,'seq'=8,'tensor'=8] {'seq'}, dimensions={0}, use_global_device_ids=true | all-gather | bytes 884736 | tf_op jit(solution)/shard_map/all_gather | solution.py:150
  788.6 26.8 %all_gather.135 = bf16[1024,3,2,64]{0,3,2,1:T(8,128)(2,1)S(1)} all-gather(bf16[128,3,2,64]{0,3,2,1:T(8,128)(2,1)S(1)} %fusion.552), channel_id=1, replica_groups=mesh['section'=2,'seq'=8,'tensor'=8] {'seq'}, dimensions={0}, use_global_device_ids=true | all-gather | bytes 884736 | tf_op jit(solution)/shard_map/all_gather | solution.py:151
  852.6 31.3 %reduce-scatter.70.cloned.1.call-done = bf16[16,3,1024]{2,0,1:T(8,128)(2,1)} async-done(((bf16[128,3,1024]{2,0,1:T(8,128)(2,1)}), bf16[16,3,1024]{2,0,1:T(8,128)(2,1)}) %reduce-scatter.70.cloned.1.call-update) | async-done | bytes 98320 | tf_op jit(solution)/shard_map/reduce_scatter | solution.py:64
  911.9 31.2 %reduce-scatter.90.cloned.1.call-done = bf16[16,3,1024]{2,0,1:T(8,128)(2,1)} async-done(((bf16[128,3,1024]{2,0,1:T(8,128)(2,1)}), bf16[16,3,1024]{2,0,1:T(8,128)(2,1)}) %reduce-scatter.90.cloned.1.call-update) | async-done | bytes 98320 | tf_op jit(solution)/shard_map/reduce_scatter | solution.py:49
  967.0 27.4 %all-gather.4 = bf16[1024,3,2,1,64]{0,4,3,2,1:T(8,128)(2,1)S(1)} all-gather(bf16[128,3,2,1,64]{0,4,3,2,1:T(8,128)(2,1)S(1)} %slice.984), channel_id=6, replica_groups=mesh['section'=2,'seq'=8,'tensor'=8] {'seq'}, dimensions={0}, use_global_device_ids=true | all-gather | bytes 884736 | tf_op jit(solution)/shard_map/all_gather | solution.py:150
  995.8 26.7 %all_gather.141 = bf16[1024,3,2,64]{0,3,2,1:T(8,128)(2,1)S(1)} all-gather(bf16[128,3,2,64]{0,3,2,1:T(8,128)(2,1)S(1)} %fusion.544), channel_id=1, replica_groups=mesh['section'=2,'seq'=8,'tensor'=8] {'seq'}, dimensions={0}, use_global_device_ids=true | all-gather | bytes 884736 | tf_op jit(solution)/shard_map/all_gather | solution.py:151
  1026.6 31.4 %reduce-scatter.92.cloned.1.call-done = bf16[16,3,1024]{2,0,1:T(8,128)(2,1)} async-done(((bf16[128,3,1024]{2,0,1:T(8,128)(2,1)}), bf16[16,3,1024]{2,0,1:T(8,128)(2,1)}) %reduce-scatter.92.cloned.1.call-update) | async-done | bytes 98320 | tf_op jit(solution)/shard_map/reduce_scatter | solution.py:49
  1097.3 24.5 reduce-scatter.110.cloned.1.call-done
  1122.8 38.5 %reduce-scatter.108.cloned.1.call-done = bf16[128,384]{1,0:T(8,128)(2,1)} async-done(((bf16[1024,384]{1,0:T(8,128)(2,1)}), bf16[128,384]{1,0:T(8,128)(2,1)}) %reduce-scatter.108.cloned.1.call-update) | async-done | bytes 98320
  1231.8 25.8 %reduce-scatter.78.cloned.1.call-done = bf16[16,3,1024]{2,0,1:T(8,128)(2,1)} async-done(((bf16[128,3,1024]{2,0,1:T(8,128)(2,1)}), bf16[16,3,1024]{2,0,1:T(8,128)(2,1)}) %reduce-scatter.78.cloned.1.call-update) | async-done | bytes 98320 | tf_op jit(solution)/shard_map/reduce_scatter | solution.py:64
  1299.1 26.4 %reduce-scatter.114.cloned.1.call-done = bf16[128,384]{1,0:T(8,128)(2,1)} async-done(((bf16[1024,384]{1,0:T(8,128)(2,1)}), bf16[128,384]{1,0:T(8,128)(2,1)}) %reduce-scatter.114.cloned.1.call-update) | async-done | bytes 98320
  1326.6 38.5 %reduce-scatter.112.cloned.1.call-done = bf16[128,384]{1,0:T(8,128)(2,1)} async-done(((bf16[1024,384]{1,0:T(8,128)(2,1)}), bf16[128,384]{1,0:T(8,128)(2,1)}) %reduce-scatter.112.cloned.1.call-update) | async-done | bytes 98320
  1368.5 30.0 %reduce-scatter.80.cloned.1.call-done = bf16[16,3,1024]{2,0,1:T(8,128)(2,1)} async-done(((bf16[128,3,1024]{2,0,1:T(8,128)(2,1)}), bf16[16,3,1024]{2,0,1:T(8,128)(2,1)}) %reduce-scatter.80.cloned.1.call-update) | async-done | bytes 98320 | tf_op jit(solution)/shard_map/reduce_scatter | solution.py:64
  1433.8 26.3 %reduce-scatter.86.cloned.1.call-done = bf16[16,3,1024]{2,0,1:T(8,128)(2,1)} async-done(((bf16[128,3,1024]{2,0,1:T(8,128)(2,1)}), bf16[16,3,1024]{2,0,1:T(8,128)(2,1)}) %reduce-scatter.86.cloned.1.call-update) | async-done | bytes 98320 | tf_op jit(solution)/shard_map/reduce_scatter | solution.py:64
  1501.3 26.4 %reduce-scatter.118.cloned.1.call-done = bf16[128,384]{1,0:T(8,128)(2,1)} async-done(((bf16[1024,384]{1,0:T(8,128)(2,1)}), bf16[128,384]{1,0:T(8,128)(2,1)}) %reduce-scatter.118.cloned.1.call-update) | async-done | bytes 98320
  1528.8 38.4 %reduce-scatter.116.cloned.1.call-done = bf16[128,384]{1,0:T(8,128)(2,1)} async-done(((bf16[1024,384]{1,0:T(8,128)(2,1)}), bf16[128,384]{1,0:T(8,128)(2,1)}) %reduce-scatter.116.cloned.1.call-update) | async-done | bytes 98320
  1570.6 29.8 %reduce-scatter.88.cloned.1.call-done = bf16[16,3,1024]{2,0,1:T(8,128)(2,1)} async-done(((bf16[128,3,1024]{2,0,1:T(8,128)(2,1)}), bf16[16,3,1024]{2,0,1:T(8,128)(2,1)}) %reduce-scatter.88.cloned.1.call-update) | async-done | bytes 98320 | tf_op jit(solution)/shard_map/reduce_scatter | solution.py:64
  1631.2 29.6 %reduce-scatter.94.cloned.1.call-done = bf16[16,3,1024]{2,0,1:T(8,128)(2,1)} async-done(((bf16[128,3,1024]{2,0,1:T(8,128)(2,1)}), bf16[16,3,1024]{2,0,1:T(8,128)(2,1)}) %reduce-scatter.94.cloned.1.call-update) | async-done | bytes 98320 | tf_op jit(solution)/shard_map/reduce_scatter | solution.py:64
  1701.7 26.3 %reduce-scatter.122.cloned.1.call-done = bf16[128,384]{1,0:T(8,128)(2,1)} async-done(((bf16[1024,384]{1,0:T(8,128)(2,1)}), bf16[128,384]{1,0:T(8,128)(2,1)}) %reduce-scatter.122.cloned.1.call-update) | async-done | bytes 98320
  1729.0 38.6 %reduce-scatter.120.cloned.1.call-done = bf16[128,384]{1,0:T(8,128)(2,1)} async-done(((bf16[1024,384]{1,0:T(8,128)(2,1)}), bf16[128,384]{1,0:T(8,128)(2,1)}) %reduce-scatter.120.cloned.1.call-update) | async-done | bytes 98320
  1775.8 25.2 %reduce-scatter.96.cloned.1.call-done = bf16[16,3,1024]{2,0,1:T(8,128)(2,1)} async-done(((bf16[128,3,1024]{2,0,1:T(8,128)(2,1)}), bf16[16,3,1024]{2,0,1:T(8,128)(2,1)}) %reduce-scatter.96.cloned.1.call-update) | async-done | bytes 98320 | tf_op jit(solution)/shard_map/reduce_scatter | solution.py:64
  1808.7 24.9 %reduce-scatter.102.cloned.1.call-done = bf16[16,3,1024]{2,0,1:T(8,128)(2,1)} async-done(((bf16[128,3,1024]{2,0,1:T(8,128)(2,1)}), bf16[16,3,1024]{2,0,1:T(8,128)(2,1)}) %reduce-scatter.102.cloned.1.call-update) | async-done | bytes 98320 | tf_op jit(solution)/shard_map/reduce_scatter | solution.py:49
  1866.9 18.8 reduce-scatter.98.cloned.1.call-done
  1954.3 37.5 %reduce-scatter.124.cloned.1.call-done = bf16[128,384]{1,0:T(8,128)(2,1)} async-done(((bf16[1024,384]{1,0:T(8,128)(2,1)}), bf16[128,384]{1,0:T(8,128)(2,1)}) %reduce-scatter.124.cloned.1.call-update) | async-done | bytes 98320
  1999.1 31.5 %reduce-scatter.128.cloned.1.call-done = bf16[128,128]{1,0:T(8,128)(2,1)} async-done(((bf16[1024,128]{1,0:T(8,128)(2,1)}), bf16[128,128]{1,0:T(8,128)(2,1)}) %reduce-scatter.128.cloned.1.call-update) | async-done | bytes 32784
  2031.5 39.6 %reduce-scatter.130.cloned.1.call-done = bf16[128,512]{1,0:T(8,128)(2,1)} async-done(((bf16[1024,512]{1,0:T(8,128)(2,1)}), bf16[128,512]{1,0:T(8,128)(2,1)}) %reduce-scatter.130.cloned.1.call-update) | async-done | bytes 131088
  2072.8 39.0 %reduce-scatter.106.cloned.1.call-done = bf16[128,512]{1,0:T(8,128)(2,1)} async-done(((bf16[1024,512]{1,0:T(8,128)(2,1)}), bf16[128,512]{1,0:T(8,128)(2,1)}) %reduce-scatter.106.cloned.1.call-update) | async-done | bytes 131088 | tf_op jit(solution)/shard_map/reduce_scatter | solution.py:402
  2118.6 17.4 all-reduce.5
  2147.8 36.3 %reduce-scatter.104.cloned.1.call-done = bf16[128,384]{1,0:T(8,128)(2,1)} async-done(((bf16[1024,384]{1,0:T(8,128)(2,1)}), bf16[128,384]{1,0:T(8,128)(2,1)}) %reduce-scatter.104.cloned.1.call-update) | async-done | bytes 98320 | tf_op jit(solution)/shard_map/reduce_scatter | solution.py:396
  2186.5 282.5 %reduce-scatter.132.cloned.1.call-done = f32[16,8]{1,0:T(8,128)} async-done(((f32[1024,8]{1,0:T(8,128)}), f32[16,8]{1,0:T(8,128)}) %reduce-scatter.132.cloned.1.call-update) | async-done | bytes 528
  (1356 shorter events, 731.3 us)
Async XLA Ops:
  8.0 295.5 %reduce-scatter.64.cloned.1.call-start = ((), (), s32[]{:S(2)}) async-start(), calls=%async_computation.35 | async-start | bytes 884736 | tf_op jit(solution)/shard_map/reduce_scatter | solution.py:49
  190.8 397.9 %copy-start.285 = (f32[2,1,64]{2,1,0:T(1,128)}, f32[2,1,64]{2,1,0:T(1,128)S(1)}, u32[]{:S(2)}) copy-start(f32[2,1,64]{2,1,0:T(1,128)S(1)} %get-tuple-element.269) | copy-start | bytes 1540
  190.8 567.9 %copy-start.283 = (f32[2,1,64]{2,1,0:T(1,128)}, f32[2,1,64]{2,1,0:T(1,128)S(1)}, u32[]{:S(2)}) copy-start(f32[2,1,64]{2,1,0:T(1,128)S(1)} %get-tuple-element.268) | copy-start | bytes 1540
  272.5 47.7 %all-gather.8.cloned.1.call-start = ((), (), s32[]{:S(2)}) async-start(), calls=%async_computation.36 | async-start | bytes 1179648 | tf_op jit(solution)/shard_map/all_gather | solution.py:97
  273.0 81.3 %all-gather.10.cloned.1.call-start = ((), (), s32[]{:S(2)}) async-start(), calls=%async_computation.37 | async-start | bytes 1179648 | tf_op jit(solution)/shard_map/all_gather | solution.py:98
  273.6 119.2 %reduce-scatter.66.cloned.1.call-start = ((), (), s32[]{:S(2)}) async-start(), calls=%async_computation.38 | async-start | bytes 884736 | tf_op jit(solution)/shard_map/reduce_scatter | solution.py:49
  358.9 148.4 %reduce-scatter.68.cloned.1.call-start = ((), (), s32[]{:S(2)}) async-start(), calls=%async_computation.39 | async-start | bytes 884736 | tf_op jit(solution)/shard_map/reduce_scatter | solution.py:49
  394.5 7.3 collective-permute-start
  476.0 87.6 %reduce-scatter.74.cloned.1.call-start = ((), (), s32[]{:S(2)}) async-start(), calls=%async_computation.42 | async-start | bytes 884736 | tf_op jit(solution)/shard_map/reduce_scatter | solution.py:49
  532.3 147.4 %reduce-scatter.76.cloned.1.call-start = ((), (), s32[]{:S(2)}) async-start(), calls=%async_computation.43 | async-start | bytes 884736 | tf_op jit(solution)/shard_map/reduce_scatter | solution.py:49
  564.6 7.3 collective-permute-start.2
  574.0 160.2 %copy-start.44 = (bf16[16,3,1024]{2,0,1:T(8,128)(2,1)}, bf16[16,3,1024]{2,0,1:T(8,128)(2,1)S(1)}, u32[]{:S(2)}) copy-start(bf16[16,3,1024]{2,0,1:T(8,128)(2,1)S(1)} %get-tuple-element.156) | copy-start | bytes 294916
  648.9 85.2 %reduce-scatter.82.cloned.1.call-start = ((), (), s32[]{:S(2)}) async-start(), calls=%async_computation.46 | async-start | bytes 884736 | tf_op jit(solution)/shard_map/reduce_scatter | solution.py:49
  702.9 148.1 %reduce-scatter.84.cloned.1.call-start = ((), (), s32[]{:S(2)}) async-start(), calls=%async_computation.47 | async-start | bytes 884736 | tf_op jit(solution)/shard_map/reduce_scatter | solution.py:49
  735.2 7.2 collective-permute-start.4
  820.0 63.9 %reduce-scatter.70.cloned.1.call-start = ((), (), s32[]{:S(2)}) async-start(), calls=%async_computation.40 | async-start | bytes 884736 | tf_op jit(solution)/shard_map/reduce_scatter | solution.py:64
  839.5 103.5 %reduce-scatter.90.cloned.1.call-start = ((), (), s32[]{:S(2)}) async-start(), calls=%async_computation.50 | async-start | bytes 884736 | tf_op jit(solution)/shard_map/reduce_scatter | solution.py:49
  911.8 146.2 %reduce-scatter.92.cloned.1.call-start = ((), (), s32[]{:S(2)}) async-start(), calls=%async_computation.51 | async-start | bytes 884736 | tf_op jit(solution)/shard_map/reduce_scatter | solution.py:49
  944.1 7.2 collective-permute-start.6
  1026.6 95.2 %reduce-scatter.110.cloned.1.call-start = ((), (), s32[]{:S(2)}) async-start(), calls=%async_computation.60 | async-start | bytes 884736
  1083.4 78.0 %reduce-scatter.108.cloned.1.call-start = ((), (), s32[]{:S(2)}) async-start(), calls=%async_computation.59 | async-start | bytes 884736
  1093.0 102.5 %reduce-scatter.72.cloned.1.call-start = ((), (), s32[]{:S(2)}) async-start(), calls=%async_computation.41 | async-start | bytes 884736 | tf_op jit(solution)/shard_map/reduce_scatter | solution.py:64
  1164.9 92.7 %reduce-scatter.78.cloned.1.call-start = ((), (), s32[]{:S(2)}) async-start(), calls=%async_computation.44 | async-start | bytes 884736 | tf_op jit(solution)/shard_map/reduce_scatter | solution.py:64
  1200.7 8.1 collective-permute-start.1
  1227.6 97.9 %reduce-scatter.114.cloned.1.call-start = ((), (), s32[]{:S(2)}) async-start(), calls=%async_computation.62 | async-start | bytes 884736
  1287.2 77.8 %reduce-scatter.112.cloned.1.call-start = ((), (), s32[]{:S(2)}) async-start(), calls=%async_computation.61 | async-start | bytes 884736
  1295.5 103.0 %reduce-scatter.80.cloned.1.call-start = ((), (), s32[]{:S(2)}) async-start(), calls=%async_computation.45 | async-start | bytes 884736 | tf_op jit(solution)/shard_map/reduce_scatter | solution.py:64
  1368.4 91.7 %reduce-scatter.86.cloned.1.call-start = ((), (), s32[]{:S(2)}) async-start(), calls=%async_computation.48 | async-start | bytes 884736 | tf_op jit(solution)/shard_map/reduce_scatter | solution.py:64
  1403.7 8.0 collective-permute-start.3
  1430.5 97.3 %reduce-scatter.118.cloned.1.call-start = ((), (), s32[]{:S(2)}) async-start(), calls=%async_computation.64 | async-start | bytes 884736
  1489.4 77.8 %reduce-scatter.116.cloned.1.call-start = ((), (), s32[]{:S(2)}) async-start(), calls=%async_computation.63 | async-start | bytes 884736
  1497.7 102.7 %reduce-scatter.88.cloned.1.call-start = ((), (), s32[]{:S(2)}) async-start(), calls=%async_computation.49 | async-start | bytes 884736 | tf_op jit(solution)/shard_map/reduce_scatter | solution.py:64
  1570.5 90.2 %reduce-scatter.94.cloned.1.call-start = ((), (), s32[]{:S(2)}) async-start(), calls=%async_computation.52 | async-start | bytes 884736 | tf_op jit(solution)/shard_map/reduce_scatter | solution.py:64
  1605.0 8.0 collective-permute-start.5
  1631.1 96.9 %reduce-scatter.122.cloned.1.call-start = ((), (), s32[]{:S(2)}) async-start(), calls=%async_computation.66 | async-start | bytes 884736
  1689.7 78.0 %reduce-scatter.120.cloned.1.call-start = ((), (), s32[]{:S(2)}) async-start(), calls=%async_computation.65 | async-start | bytes 884736
  1698.0 103.0 %reduce-scatter.96.cloned.1.call-start = ((), (), s32[]{:S(2)}) async-start(), calls=%async_computation.53 | async-start | bytes 884736 | tf_op jit(solution)/shard_map/reduce_scatter | solution.py:64
  1771.0 62.6 %reduce-scatter.102.cloned.1.call-start = ((), (), s32[]{:S(2)}) async-start(), calls=%async_computation.56 | async-start | bytes 884736 | tf_op jit(solution)/shard_map/reduce_scatter | solution.py:49
  1775.8 110.0 %reduce-scatter.98.cloned.1.call-start = ((), (), s32[]{:S(2)}) async-start(), calls=%async_computation.54 | async-start | bytes 884736 | tf_op jit(solution)/shard_map/reduce_scatter | solution.py:64
  1805.4 28.2 %collective-permute-start.7 = (bf16[16,3,1024]{2,0,1:T(8,128)(2,1)S(1)}, bf16[16,3,1024]{2,0,1:T(8,128)(2,1)S(1)}, u32[]{:S(2)}, u32[]{:S(2)}) collective-permute-start(bf16[16,3,1024]{2,0,1:T(8,128)(2,1)S(1)} %add_convert_fusion.5), channel_id=1, source_target_pairs={{64,0},{65,1},{66,2},{67,3},{68,4},{69,5},{70,6},{71,7},{72,8},{73... | collective-permute-start | bytes 294920 | tf_op jit(solution)/shard_map/ppermute | solution.py:17
  1854.4 98.9 %reduce-scatter.126.cloned.1.call-start = ((), (), s32[]{:S(2)}) async-start(), calls=%async_computation.68 | async-start | bytes 884736
  1914.1 77.7 %reduce-scatter.124.cloned.1.call-start = ((), (), s32[]{:S(2)}) async-start(), calls=%async_computation.67 | async-start | bytes 884736
  1920.4 110.2 %reduce-scatter.128.cloned.1.call-start = ((), (), s32[]{:S(2)}) async-start(), calls=%async_computation.69 | async-start | bytes 294912
  1929.0 142.1 %reduce-scatter.130.cloned.1.call-start = ((), (), s32[]{:S(2)}) async-start(), calls=%async_computation.70 | async-start | bytes 1179648
  1935.2 176.6 %reduce-scatter.106.cloned.1.call-start = ((), (), s32[]{:S(2)}) async-start(), calls=%async_computation.58 | async-start | bytes 1179648 | tf_op jit(solution)/shard_map/reduce_scatter | solution.py:402
  1947.2 197.1 %reduce-scatter.100.cloned.1.call-start = ((), (), s32[]{:S(2)}) async-start(), calls=%async_computation.55 | async-start | bytes 884736 | tf_op jit(solution)/shard_map/reduce_scatter | solution.py:64
  1994.8 189.3 %reduce-scatter.104.cloned.1.call-start = ((), (), s32[]{:S(2)}) async-start(), calls=%async_computation.57 | async-start | bytes 884736 | tf_op jit(solution)/shard_map/reduce_scatter | solution.py:396
  2117.7 351.3 %reduce-scatter.132.cloned.1.call-start = ((), (), s32[]{:S(2)}) async-start(), calls=%async_computation.71 | async-start | bytes 532480
  (393 other events, 4594.7 us)
Sparse Core Ops, SparseCore 0:
  272.6 30.9 reduce-scatter.63
  359.0 33.8 reduce-scatter.65
  476.2 31.0 reduce-scatter.67
  532.4 31.1 reduce-scatter.73
  649.1 30.6 reduce-scatter.75
  703.0 31.1 reduce-scatter.81
  820.2 30.7 reduce-scatter.83
  853.5 30.3 reduce-scatter.69
  911.9 31.0 reduce-scatter.89
  1026.7 31.3 reduce-scatter.91
  1165.0 30.4 reduce-scatter.71
  1227.7 29.8 reduce-scatter.77
  1368.5 29.9 reduce-scatter.79
  1430.6 29.3 reduce-scatter.85
  1570.7 29.7 reduce-scatter.87
  1631.2 29.4 reduce-scatter.93
  1771.1 29.8 reduce-scatter.95
  1803.4 30.1 reduce-scatter.101
  1854.6 31.1 reduce-scatter.97
Sparse Core Ops, SparseCore 1:
  274.6 38.2 all-gather.7
  314.3 39.9 all-gather.9
  1083.5 38.3 reduce-scatter.109
  1124.3 37.0 reduce-scatter.107
  1287.3 38.2 reduce-scatter.113
  1328.1 36.9 reduce-scatter.111
  1489.5 38.2 reduce-scatter.117
  1530.2 37.0 reduce-scatter.115
  1689.8 38.2 reduce-scatter.121
  1730.5 37.0 reduce-scatter.119
  1914.2 38.2 reduce-scatter.125
  1954.8 36.9 reduce-scatter.123
  1994.8 35.8 reduce-scatter.127
  2033.0 38.0 reduce-scatter.129
  2073.5 38.3 reduce-scatter.105
  2114.2 30.1 reduce-scatter.99
  2146.9 37.3 reduce-scatter.103
  2186.5 282.4 reduce-scatter.131
where the time goes:
time: 2490 us; the launch traced here: 2480 us
  waiting for transfers between devices  1280 us (51%)
  blocking collectives  754 us (30%)
  matrix products  177 us (7%)
  other arithmetic  125 us (5%)
  local copies, waits for them, and re-layouts  93.6 us (4%)
  starting transfers between devices  28.1 us (1%)
    unnamed x50, waiting for transfers between devices  650 us
    reduce_scatter x10, waiting for transfers between devices, narrow(): lax.psum_scatter(term_rows(jnp.int32(0), values_in.shape[0] // lax.axis_s...  259 us
    reduce_scatter x10, waiting for transfers between devices, narrow_back(): lax.psum_scatter(term_rows(jnp.int32(0), grads_in.shape[0] // lax.axis_si...  239 us
    all_gather x10, blocking collectives, widen_rows(): return lax.all_gather(row_data, 'tensor', axis=0, tiled=True)  137 us
    all_gather x5, blocking collectives, on_device(): forward_keys_all = lax.all_gather(keys_proj, 'seq', axis=0, tiled=True)  136 us
    all_gather x10, blocking collectives, widen_back(): piece_rows = lax.all_gather(grad_rows, 'tensor', axis=0, tiled=True)  136 us
    all_gather x5, blocking collectives, on_device(): forward_values_all = lax.all_gather(values_proj, 'seq', axis=0, tiled=True)  133 us
    all_gather x1, blocking collectives, on_device(): params = lax.all_gather(vectors, ('seq', 'tensor'), axis=2, tiled=True)[0]  83.9 us
  transfers between devices with their start and end apart: 45, of which 42 were waited for; matrix products, arithmetic and copies ran while one was open for 6% of the time, Pallas kernels for 0%

commit v1 on v0

v1 whole, which is shorter than its diff:
```python
import jax
import jax.numpy as jnp
from jax import lax
from jax.experimental import pallas as pl
from jax.experimental.pallas import tpu as pltpu
from jax.sharding import PartitionSpec as P

SS = ("section", "seq")
EPS = 1e-6
F32 = jnp.float32
BF = jnp.bfloat16
D = 1024
HEAD = 64
TOK = 128
GROUPS = [0, 1, 2, 3, 4, None, None, None, 5, 6, 7, 8, None, None, None, None]
SLOT = [GROUPS.index(i) for i in range(9)]


def move_x(v, d):
    return lax.ppermute(v, "tensor", [(i, (i + 2 * d) % 8) for i in range(8)])


def move_core(v):
    return lax.ppermute(v, "tensor", [(i, i ^ 1) for i in range(8)])


def joint(y, z):
    return (z // 2) * 8 + y * 2 + z % 2


def move_yz(v, dy, dz):
    return lax.ppermute(
        v,
        SS,
        [
            (joint(y, z), joint((y + dy) % 4, (z + dz) % 4))
            for y in range(4)
            for z in range(4)
        ],
    )


def move_section(v):
    return lax.ppermute(v, "section", [(0, 1), (1, 0)])


def widen(v):
    return jnp.concatenate([v, move_x(v, 1), move_x(v, -1), move_x(v, 2)], 0)


def narrow(v):
    k = v.shape[0] // 4
    far = move_x(v[3 * k :].astype(BF), 2)
    back = move_x(v[k : 2 * k].astype(BF), -1)
    ahead = move_x(v[2 * k : 3 * k].astype(BF), 1)
    return v[:k].astype(F32) + back.astype(F32) + ahead.astype(F32) + far.astype(F32)


def dot(a, b, dims, out=F32):
    return lax.dot_general(a, b, (dims, ((), ())), preferred_element_type=F32).astype(out)


def attend_kernel(q_ref, k0_ref, v0_ref, k1_ref, v1_ref, o_ref, lse_ref):
    rows = q_ref.shape[0]
    lane = lax.broadcasted_iota(jnp.int32, (rows, 128), 1)
    k = jnp.concatenate([k0_ref[...], k1_ref[...]], 0)
    v = jnp.concatenate([v0_ref[...], v1_ref[...]], 0)
    q = q_ref[...] * jnp.asarray(0.125, BF)
    zero = jnp.zeros_like(q)
    outs = []
    for h in range(2):
        mine = (lane < HEAD) if h == 0 else (lane >= HEAD)
        qh = jnp.where(mine, q, zero)
        s = lax.dot_general(k, qh, (((1,), (1,)), ((), ())), preferred_element_type=F32)
        top = jnp.max(s, axis=0, keepdims=True)
        p = jnp.exp(s - top)
        total = jnp.sum(p, axis=0, keepdims=True)
        o = lax.dot_general(v, p.astype(BF), (((0,), (0,)), ((), ())), preferred_element_type=F32)
        outs.append(o * (1.0 / total))
        lse_ref[0, h : h + 1, :] = top + jnp.log(total)
    sub = lax.broadcasted_iota(jnp.int32, outs[0].shape, 0)
    o_ref[...] = jnp.where(sub < HEAD, outs[0], outs[1]).T.astype(BF)


def attend(q, k0, v0, k1, v1):
    rows = 256
    n = q.shape[0]
    near = pl.BlockSpec((n, 128), lambda p, r: (0, p))
    away = pl.BlockSpec((n, 128), lambda p, r: (0, 1 - p))
    here = pl.BlockSpec((rows, 128), lambda p, r: (r, p))
    return pl.pallas_call(
        attend_kernel,
        grid=(2, n // rows),
        in_specs=[here, near, near, away, away],
        out_specs=[here, pl.BlockSpec((1, 8, rows), lambda p, r: (p, 0, r))],
        out_shape=[
            jax.ShapeDtypeStruct((n, 256), BF),
            jax.ShapeDtypeStruct((2, 8, n), F32),
        ],
        compiler_params=pltpu.CompilerParams(vmem_limit_bytes=40 * 2**20),
        cost_estimate=pl.CostEstimate(
            flops=4 * 4 * n * 2 * n * 256, bytes_accessed=12 * n * 256, transcendentals=8 * n * n
        ),
        name="attend",
    )(q, k0, v0, k1, v1)


def attend_back_kernel(
    q_ref, k0_ref, v0_ref, k1_ref, v1_ref, do_ref, lse_ref,
    dq_ref, dk0_ref, dv0_ref, dk1_ref, dv1_ref, dk_acc, dv_acc,
):
    r = pl.program_id(1)
    rows = q_ref.shape[0]
    n = k0_ref.shape[0]
    lane = lax.broadcasted_iota(jnp.int32, (rows, 128), 1)
    k = jnp.concatenate([k0_ref[...], k1_ref[...]], 0)
    v = jnp.concatenate([v0_ref[...], v1_ref[...]], 0)
    q = q_ref[...] * jnp.asarray(0.125, BF)
    do = do_ref[...]
    zero = jnp.zeros_like(q)
    dqs = []
    dk = jnp.zeros((2 * n, 128), F32)
    dv = jnp.zeros((2 * n, 128), F32)
    for h in range(2):
        mine = (lane < HEAD) if h == 0 else (lane >= HEAD)
        qh = jnp.where(mine, q, zero)
        doh = jnp.where(mine, do, zero)
        s = lax.dot_general(k, qh, (((1,), (1,)), ((), ())), preferred_element_type=F32)
        p = jnp.exp(s - lse_ref[0, h : h + 1, :])
        dv = dv + jnp.dot(p.astype(BF), doh, preferred_element_type=F32)
        dp = lax.dot_general(v, doh, (((1,), (1,)), ((), ())), preferred_element_type=F32)
        delta = jnp.sum(p * dp, axis=0, keepdims=True)
        ds = (p * (dp - delta)).astype(BF)
        dk = dk + jnp.dot(ds, qh, preferred_element_type=F32)
        dqs.append(
            lax.dot_general(k, ds, (((0,), (0,)), ((), ())), preferred_element_type=F32)
        )
    sub = lax.broadcasted_iota(jnp.int32, dqs[0].shape, 0)
    dq_ref[...] = (jnp.where(sub < HEAD, dqs[0], dqs[1]) * 0.125).T.astype(BF)

    @pl.when(r == 0)
    def _():
        dk_acc[...] = dk
        dv_acc[...] = dv

    @pl.when(r > 0)
    def _():
        dk_acc[...] += dk
        dv_acc[...] += dv

    @pl.when(r == pl.num_programs(1) - 1)
    def _():
        dk0_ref[...] = dk_acc[:n]
        dv0_ref[...] = dv_acc[:n]
        dk1_ref[...] = dk_acc[n:].astype(BF)
        dv1_ref[...] = dv_acc[n:].astype(BF)


def attend_back(q, k0, v0, k1, v1, do, lse):
    rows = 256
    n = q.shape[0]
    near = pl.BlockSpec((n, 128), lambda p, r: (0, p))
    away = pl.BlockSpec((n, 128), lambda p, r: (0, 1 - p))
    here = pl.BlockSpec((rows, 128), lambda p, r: (r, p))
    shape = jax.ShapeDtypeStruct
    return pl.pallas_call(
        attend_back_kernel,
        grid=(2, n // rows),
        in_specs=[
            here, near, near, away, away, here,
            pl.BlockSpec((1, 8, rows), lambda p, r: (p, 0, r)),
        ],
        out_specs=[here, near, near, away, away],
        out_shape=[
            shape((n, 256), BF), shape((n, 256), F32), shape((n, 256), F32),
            shape((n, 256), BF), shape((n, 256), BF),
        ],
        scratch_shapes=[pltpu.VMEM((2 * n, 128), F32), pltpu.VMEM((2 * n, 128), F32)],
        compiler_params=pltpu.CompilerParams(vmem_limit_bytes=48 * 2**20),
        cost_estimate=pl.CostEstimate(
            flops=4 * 10 * n * 2 * n * 256, bytes_accessed=26 * n * 256, transcendentals=8 * n * n
        ),
        name="attend_back",
    )(q, k0, v0, k1, v1, do, lse)


def norm_parts(v):
    mean = jnp.mean(v, axis=-1, keepdims=True)
    centred = v - mean
    scale = lax.rsqrt(jnp.mean(centred * centred, axis=-1, keepdims=True) + EPS)
    return centred * scale, scale


def norm(v, gain, shift):
    return norm_parts(v)[0] * gain + shift


def norm_back(v, gain, grad):
    unit, scale = norm_parts(v)
    inner = grad * gain
    part = scale * (
        inner
        - jnp.mean(inner, axis=-1, keepdims=True)
        - unit * jnp.mean(inner * unit, axis=-1, keepdims=True)
    )
    return part, jnp.sum(grad * unit, 0), jnp.sum(grad, 0)


def gelu(v):
    return jax.nn.gelu(v, approximate=False)


def gather_weights(shard, y, z):
    rows, cols = shard.shape
    along_z = jnp.zeros((4, rows, cols), shard.dtype)
    for d in range(4):
        piece = move_yz(shard, 0, d) if d else shard
        along_z = lax.dynamic_update_slice(along_z, piece[None], ((z - d) % 4, 0, 0))
    out = []
    for layer in range(2):
        block = along_z[2 * layer : 2 * layer + 2]
        whole = jnp.zeros((4, 2, rows, cols), shard.dtype)
        for d in range(4):
            piece = move_yz(block, d, 0) if d else block
            whole = lax.dynamic_update_slice(whole, piece[None], ((y - d) % 4, 0, 0, 0))
        whole = whole.reshape(8 * rows, cols)
        out.append((whole, move_core(whole)))
    return out


def forward(x, w, p):
    wq, wo, wu, wd = w
    qkv_bias, up_bias, par = p
    a = norm(x, par[0], par[1]).astype(BF)
    a_wide = widen(a)
    qkv = (dot(a_wide, wq, ((1,), (0,))) + qkv_bias).astype(BF)
    q = jnp.concatenate([qkv[:, 0:128], qkv[:, 384:512]], 1)
    k = jnp.concatenate([qkv[:, 128:256], qkv[:, 512:640]], 1)
    v = jnp.concatenate([qkv[:, 256:384], qkv[:, 640:768]], 1)
    kv = move_core(jnp.concatenate([k, v], 1))
    k1, v1 = kv[:, :256], kv[:, 256:]
    o, lse = attend(q, k, v, k1, v1)
    z = narrow(dot(o, wo, ((1,), (1,)))) + par[4]
    x1 = x + par[6] * z
    a2 = norm(x1, par[2], par[3]).astype(BF)
    a2_wide = widen(a2)
    u = dot(a2_wide, wu, ((1,), (0,))) + up_bias
    gl = gelu(u).astype(BF)
    m = narrow(dot(gl, wd, ((1,), (1,)))) + par[5]
    x2 = x1 + par[7] * m
    return x2, (x, a_wide, q, k, v, k1, v1, o, lse, z, x1, a2_wide, u, gl, m)


def backward(dy, kept, w, p):
    wq, wo, wu, wd = w
    _, _, par = p
    x, a_wide, q, k, v, k1, v1, o, lse, z, x1, a2_wide, u, gl, m = kept
    ds2 = jnp.sum(dy * m, 0)
    dc2 = par[7] * jnp.sum(dy, 0)
    dm = widen((par[7] * dy).astype(BF))
    g_down = dot(dm, gl, ((0,), (0,)))
    dgl = dot(dm, wd, ((1,), (0,)))
    du = jax.vjp(gelu, u)[1](dgl)[0].astype(BF)
    g_up_bias = jnp.sum(du.astype(F32), 0)
    g_up = dot(a2_wide, du, ((0,), (0,)))
    da2 = narrow(dot(du, wu, ((1,), (1,))))
    part, dg2, db2 = norm_back(x1, par[2], da2)
    dx1 = dy + part
    ds1 = jnp.sum(dx1 * z, 0)
    dco = par[6] * jnp.sum(dx1, 0)
    dz = widen((par[6] * dx1).astype(BF))
    g_out = dot(dz, o, ((0,), (0,)))
    do = dot(dz, wo, ((1,), (0,)), BF)
    dq, dk0, dv0, dk1, dv1 = attend_back(q, k, v, k1, v1, do, lse)
    dkv = move_core(jnp.concatenate([dk1, dv1], 1))
    dk = (dk0 + dkv[:, :256].astype(F32)).astype(BF)
    dv = (dv0 + dkv[:, 256:].astype(F32)).astype(BF)
    dqkv = jnp.concatenate(
        [dq[:, :128], dk[:, :128], dv[:, :128], dq[:, 128:], dk[:, 128:], dv[:, 128:]], 1
    )
    g_qkv_bias = jnp.sum(dqkv.astype(F32), 0)
    g_qkv = dot(a_wide, dqkv, ((0,), (0,)))
    da = narrow(dot(dqkv, wq, ((1,), (1,))))
    part, dg1, db1 = norm_back(x, par[0], da)
    dx = dx1 + part
    vec = jnp.stack([dg1, db1, dg2, db2, dco, dc2, ds1, ds2])
    return dx, (g_qkv, g_out, g_up, g_down), (g_qkv_bias, g_up_bias), vec


def scatter_grad(g, seq):
    cols = g.shape[1] // 2
    both = (g[:, :cols] + move_core(g[:, cols:].astype(BF)).astype(F32)).astype(BF)
    rows = both.shape[0] // 8
    total = None
    for d in range(8):
        piece = lax.dynamic_slice(both, (((seq + d) % 8) * rows, 0), (rows, cols))
        if d:
            piece = lax.ppermute(piece, "seq", [(j, (j + d) % 8) for j in range(5)])
        total = piece.astype(F32) if total is None else total + piece.astype(F32)
    return total


def on_device(ends, w_qkv, qv_bias, w_proj, w_fc1, fc1_bias, w_fc2, vectors):
    sec = lax.axis_index("section")
    seq = lax.axis_index("seq")
    ten = lax.axis_index("tensor")
    first = sec == 0
    core = ten % 2
    y = seq // 2
    z = sec * 2 + seq % 2

    by_image = jnp.transpose(ends[0], (1, 0, 2))
    blank = jnp.zeros(by_image.shape[1:], BF)
    send = jnp.stack([blank if g is None else by_image[g] for g in GROUPS])
    got = lax.all_to_all(send, SS, 0, 0, tiled=True)
    x = got[:8].reshape(TOK, D).astype(F32)
    cot = got[8:].reshape(TOK, D).astype(F32)

    flat = jnp.concatenate(
        [
            vectors[0].reshape(-1),
            qv_bias[0].astype(F32).reshape(-1),
            fc1_bias[0].astype(F32).reshape(-1),
            jnp.zeros((32,), F32),
        ]
    ).reshape(2, 128)
    flat = lax.all_to_all(jnp.broadcast_to(flat[None], (8, 2, 128)), "tensor", 0, 0, tiled=True)
    flat = flat.reshape(1, 16, 128)
    flat = lax.all_to_all(jnp.broadcast_to(flat, (16, 16, 128)), SS, 0, 0, tiled=True)
    flat = flat.reshape(2, 8, 8, 256)
    pars = []
    for layer in range(2):
        f = flat[layer]
        par = f[:, :, :128].reshape(8, 8, 8, 16)
        par = jnp.transpose(par, (2, 0, 1, 3)).reshape(8, D)
        sides_q, sides_u = [], []
        for owner in (ten, ten ^ 1):
            b = lax.dynamic_slice(f, (0, owner, 0), (8, 1, 256))[:, 0]
            bq = b[:, 128:160].reshape(8, 2, 2, 8)
            bq = jnp.transpose(bq, (2, 1, 0, 3)).reshape(2, 128)
            sides_q += [bq[0], jnp.zeros((128,), F32), bq[1]]
            bu = b[:, 160:224].reshape(8, 8, 8)
            sides_u.append(jnp.transpose(bu, (1, 0, 2)).reshape(512))
        pars.append((jnp.concatenate(sides_q), jnp.concatenate(sides_u), par))

    own_qkv = jnp.transpose(w_qkv[0].reshape(128, 2, 3, HEAD), (0, 2, 1, 3)).reshape(128, 384)
    near = jnp.concatenate([own_qkv, w_proj[0].T], 1)
    far = jnp.concatenate([w_fc1[0], w_fc2[0].T], 1)
    near = gather_weights(near, y, z)
    far = gather_weights(far, y, z)
    weights = []
    for layer in range(2):
        a, b = near[layer]
        c, d = far[layer]
        weights.append(
            (
                jnp.concatenate([a[:, :384], b[:, :384]], 1),
                jnp.concatenate([a[:, 384:], b[:, 384:]], 1),
                jnp.concatenate([c[:, :512], d[:, :512]], 1),
                jnp.concatenate([c[:, 512:], d[:, 512:]], 1),
            )
        )

    x2, kept0 = forward(x, weights[0], pars[0])
    y0 = x2.astype(BF).astype(F32)
    x2, kept1 = forward(y0, weights[1], pars[1])
    y1 = x2.astype(BF)
    dx, g1, b1, v1 = backward(cot, kept1, weights[1], pars[1])
    dx, g0, b0, v0 = backward(dx.astype(BF).astype(F32), kept0, weights[0], pars[0])
    dx = dx.astype(BF)

    back = jnp.concatenate([dx.reshape(8, 16, D), y1.reshape(8, 16, D)], 0)
    back = lax.all_to_all(back, SS, 0, 0, tiled=True)
    ends_out = jnp.transpose(jnp.stack([back[s] for s in SLOT]), (1, 0, 2))

    grads = []
    for a, b in zip(g0, g1):
        r0, r1 = scatter_grad(a, seq), scatter_grad(b, seq)
        other = move_section(jnp.where(first, r1, r0).astype(BF)).astype(F32)
        grads.append(jnp.where(first, r0, r1) + other)
    g_qkv, g_out, g_up, g_down = grads
    g_qkv = jnp.transpose(g_qkv.reshape(128, 3, 2, HEAD), (0, 2, 1, 3)).reshape(128, 384)

    vec = jnp.stack([v0, v1]).reshape(2, 8, 8, 8, 16)
    vec = jnp.transpose(vec, (3, 0, 2, 1, 4)).reshape(8, 2, 8, 128)
    sides = []
    for side in range(2):
        rows = []
        for gq, gu in (b0, b1):
            gq = gq[384 * side : 384 * side + 384]
            gq = jnp.stack([gq[:128], gq[256:]]).reshape(2, 2, 8, 8)
            gq = jnp.transpose(gq, (2, 1, 0, 3)).reshape(8, 32)
            gu = gu[512 * side : 512 * side + 512].reshape(8, 8, 8)
            gu = jnp.transpose(gu, (1, 0, 2)).reshape(8, 64)
            rows.append(jnp.concatenate([gq, gu, jnp.zeros((8, 32), F32)], 1))
        sides.append(jnp.stack(rows))
    who = jnp.arange(8)[:, None, None, None]
    bias = jnp.where(who == ten, sides[0][None], jnp.where(who == (ten ^ 1), sides[1][None], 0.0))
    small = jnp.concatenate([vec, bias], -1).reshape(8, 32, 128)
    small = lax.all_to_all(small, "tensor", 0, 0, tiled=True)
    small = jnp.sum(small, 0).reshape(16, 2, 128)
    small = lax.all_to_all(small, SS, 0, 0, tiled=True)
    small = jnp.sum(small, 0)
    g_vec = small[0].reshape(8, 16)
    g_qvb = small[1, :32].reshape(4, 8)
    g_upb = small[1, 32:96].reshape(8, 8)
    return (
        ends_out[None],
        g_qkv[None],
        g_qvb[None],
        g_out.T[None],
        g_up[None],
        g_upb[None],
        g_down.T[None],
        g_vec[None],
    )


def solution(mesh):
    placed = (
        P("section", ("seq", "tensor"), None, None),
        P("section", "seq", "tensor"),
        P("section", "tensor", "seq"),
        P("section", "tensor", "seq"),
        P("section", "seq", "tensor"),
        P("section", "tensor", "seq"),
        P("section", "tensor", "seq"),
        P("section", None, ("seq", "tensor")),
    )
    return jax.shard_map(
        on_device, mesh=mesh, in_specs=placed, out_specs=placed, check_vma=False
    )
```

time: 2490 us -> 704 us (0.28)
  waiting for transfers between devices: 1280 us -> 150 us
  blocking collectives: 754 us -> 0 us
  starting transfers between devices: 28.1 us -> 291 us
  matrix products: 177 us -> 58.8 us
  other arithmetic: 125 us -> 47.3 us
  Pallas kernels: 0 us -> 31.3 us
    all_gather x35 -> x0, blocking collectives: 737 us -> none  [the longest x10 137 us: widen_rows(): return lax.all_gather(row_data, 'tensor', axis=0, tiled=True)]
    unnamed x50 -> x0, waiting for transfers between devices: 650 us -> none
    reduce_scatter x22 -> x0, waiting for transfers between devices: 573 us -> none  [the longest x10 259 us: narrow(): lax.psum_scatter(term_rows(jnp.int32(0), values_in.shape[0] // lax.axis_s...]
    ppermute x8 -> x142, starting transfers between devices: 25.5 us -> 261 us  [the longest x56 153 us: scatter_grad(): piece = lax.ppermute(piece, 'seq', [(j, (j + d) % 8) for j in range(5)])]
    dot_general x192 -> x24, matrix products: 177 us -> 58.8 us  [dot(): lax.dot_general(a, b, (dims, ((), ())), preferred_element_type=F32)]
    ppermute x8 -> x142, waiting for transfers between devices: 23.6 us -> 130 us  [the longest x48 94.7 us: move_x(): return lax.ppermute(v, 'tensor', [(i, (i + 2 * d) % 8) for i in range(8)])]
    reduce_sum x67 -> x19, other arithmetic: 56.5 us -> 16 us  [the longest x4 5.96 us: norm_back(): return (part, jnp.sum(grad * unit, 0), jnp.sum(grad, 0))]
    unnamed x822 -> x421, local copies, waits for them, and re-layouts: 63.5 us -> 24.2 us
  transfers between devices with their start and end apart: 45 -> 148, of which waited for: 42 -> 41; matrix products, arithmetic and copies ran while one was open for 6% -> 26% of each run, Pallas kernels for 0% -> 5%
where the time goes in v1:
time: 704 us; the launch traced here: 690 us
  starting transfers between devices  291 us (41%)
  waiting for transfers between devices  150 us (21%)
  local copies, waits for them, and re-layouts  106 us (15%)
  matrix products  58.8 us (8%)
  other arithmetic  47.3 us (7%)
  Pallas kernels  31.3 us (4%)
    ppermute x56, starting transfers between devices, scatter_grad(): piece = lax.ppermute(piece, 'seq', [(j, (j + d) % 8) for j in range(5)])  153 us
    ppermute x48, waiting for transfers between devices, move_x(): return lax.ppermute(v, 'tensor', [(i, (i + 2 * d) % 8) for i in range(8)])  94.7 us
    ppermute x48, starting transfers between devices, move_x(): return lax.ppermute(v, 'tensor', [(i, (i + 2 * d) % 8) for i in range(8)])  59.5 us
    dot_general x24, matrix products, dot(): lax.dot_general(a, b, (dims, ((), ())), preferred_element_type=F32)  58.8 us
    ppermute x18, starting transfers between devices, move_yz(): lax.ppermute(v, SS, [(joint(y, z), joint((y + dy) % 4, (z + dz) % 4)) for...  36.8 us
    ppermute x18, waiting for transfers between devices, move_yz(): lax.ppermute(v, SS, [(joint(y, z), joint((y + dy) % 4, (z + dz) % 4)) for...  27.7 us
    unnamed x421, local copies, waits for them, and re-layouts  24.2 us
    pallas_call x2, Pallas kernels, attend_back(): pl.pallas_call(attend_back_kernel, grid=(2, n // rows), in_specs=[here, n...  17.6 us
  transfers between devices with their start and end apart: 148, of which 41 were waited for; matrix products, arithmetic and copies ran while one was open for 26% of the time, Pallas kernels for 5%

profile of v1, /device:TPU:0, one launch (start us, length us, event | category | flops | bytes accessed | tf_op | source)
XLA Modules:
  0.0 690.4 jit_solution(764772836935373002)
XLA Ops:
  2.5 4.0 collective-permute-start.4
  16.3 4.3 all-to-all-start.1
  26.6 7.1 %all-to-all-start.2 = ((f32[16,16,128]{2,1,0:T(8,128)}), f32[16,16,128]{2,1,0:T(8,128)S(1)}, u32[]{:S(2)}, u32[]{:S(2)}) async-start(f32[16,16,128]{2,1,0:T(8,128)} %broadcast_in_dim.178), calls=%async_computation.2 | async-start | bytes 262144 | tf_op jit(solution)/shard_map/all_to_all | solution.py:329
  34.6 7.0 %all-to-all-done.2 = f32[16,16,128]{2,1,0:T(8,128)S(1)} async-done(((f32[16,16,128]{2,1,0:T(8,128)}), f32[16,16,128]{2,1,0:T(8,128)S(1)}, u32[]{:S(2)}, u32[]{:S(2)}) %all-to-all-start.2) | async-done | bytes 131104 | tf_op jit(solution)/shard_map/all_to_all | solution.py:329
  41.5 3.6 all-to-all-start
  76.5 6.1 collective-permute-done.8
  82.9 5.6 collective-permute-done.30
  93.6 5.9 collective-permute-done.20
  110.6 8.3 %collective-permute-done.22 = bf16[2,128,1024]{2,1,0:T(8,128)(2,1)S(1)} collective-permute-done((bf16[2,128,1024]{2,1,0:T(8,128)(2,1)}, bf16[2,128,1024]{2,1,0:T(8,128)(2,1)S(1)}, u32[]{:S(2)}, u32[]{:S(2)}) %collective-permute-start.22) | collective-permute-done | bytes 524320 | tf_op jit(solution)/shard_map/ppermute | solution.py:32
  120.2 6.8 attend.2
  131.9 9.7 %collective-permute-done.11 = bf16[128,1024]{1,0:T(8,128)(2,1)S(1)} collective-permute-done((bf16[128,1024]{1,0:T(8,128)(2,1)S(1)}, bf16[128,1024]{1,0:T(8,128)(2,1)S(1)}, u32[]{:S(2)}, u32[]{:S(2)}) %collective-permute-start.11) | collective-permute-done | bytes 262176 | tf_op jit(solution)/shard_map/ppermute | solution.py:20
  150.6 6.9 collective-permute-done.16
  162.1 7.4 %multiply_convert_fusion.1 = (bf16[512,1024]{1,0:T(8,128)(2,1)S(1)}, f32[512,1024]{1,0:T(8,128)}, f32[512,1024]{1,0:T(8,128)}) fusion(f32[1024]{0:T(1024)S(1)} %pad_maximum_fusion.68, bf16[1024,512]{1,0:T(8,128)(2,1)S(1)} %get-tuple-element.145, bf16[1024,512]{1,0:T(8,128)(2,1)S(1)} %get-tuple-element.143, ...), kind=kOutput, calls=%fused_computation.37 | convolution fusion | flops 1116733440 | bytes 8392704 | tf_op jit(solution)/shard_map/dot_general | solution.py:60
  186.0 3.9 collective-permute-done.25
  211.4 6.8 attend.3
  226.8 11.5 %collective-permute-done.35 = bf16[128,1024]{1,0:T(8,128)(2,1)S(1)} collective-permute-done((bf16[128,1024]{1,0:T(8,128)(2,1)S(1)}, bf16[128,1024]{1,0:T(8,128)(2,1)S(1)}, u32[]{:S(2)}, u32[]{:S(2)}) %collective-permute-start.35) | collective-permute-done | bytes 262176 | tf_op jit(solution)/shard_map/ppermute | solution.py:20
  238.3 3.7 collective-permute-start.46
  245.7 8.5 %collective-permute-done.40 = bf16[128,1024]{1,0:T(8,128)(2,1)S(1)} collective-permute-done((bf16[128,1024]{1,0:T(8,128)(2,1)S(1)}, bf16[128,1024]{1,0:T(8,128)(2,1)S(1)}, u32[]{:S(2)}, u32[]{:S(2)}) %collective-permute-start.40) | collective-permute-done | bytes 262176 | tf_op jit(solution)/shard_map/ppermute | solution.py:20
  258.4 6.5 multiply_convert_fusion
  277.4 3.8 collective-permute-start.48
  318.0 8.8 %attend_back.2 = (bf16[512,256]{1,0:T(8,128)(2,1)S(1)}, f32[512,256]{1,0:T(8,128)S(1)}, f32[512,256]{1,0:T(8,128)S(1)}, bf16[512,256]{1,0:T(8,128)(2,1)S(1)}, bf16[512,256]{1,0:T(8,128)(2,1)S(1)}) custom-call(bf16[512,256]{1,0:T(8,128)(2,1)S(1)} %pad_maximum_fusion.45.q_ref, bf16[512,256]{1,0:T(8,128)(2,1)S(1)} %pad_maximum_fusion.46.k0_ref, ...), custom_call_target="tpu_custom_call" | custom-call | flops 5368709120 | bytes 3407872 | tf_op jit(solution)/shard_map/attend_back/pallas_call | solution.py:166
  333.3 3.8 fusion.160
  351.8 3.7 collective-permute-done.57
  355.5 4.3 collective-permute-done.56
  368.5 5.3 collective-permute-done.60
  379.1 6.1 convert_reduce_fusion.1
  401.3 4.0 collective-permute-done.62
  410.3 8.1 %collective-permute-done.66 = bf16[128,1024]{1,0:T(8,128)(2,1)S(1)} collective-permute-done((bf16[128,1024]{1,0:T(8,128)(2,1)S(1)}, bf16[128,1024]{1,0:T(8,128)(2,1)S(1)}, u32[]{:S(2)}, u32[]{:S(2)}) %collective-permute-start.66) | collective-permute-done | bytes 262176 | tf_op jit(solution)/shard_map/ppermute | solution.py:20
  429.2 7.1 %collective-permute-start.103 = (bf16[128,128]{1,0:T(8,128)(2,1)S(1)}, bf16[128,128]{1,0:T(8,128)(2,1)S(1)}, u32[]{:S(2)}, u32[]{:S(2)}) collective-permute-start(bf16[128,128]{1,0:T(8,128)(2,1)S(1)} %copy-done.122), channel_id=1, source_target_pairs={{0,32},{8,40},{16,48},{24,56},{32,0},{1,33},{9,41},{17,49},{25,57}... | collective-permute-start | bytes 98312 | tf_op jit(solution)/shard_map/ppermute | solution.py:298
  440.2 4.0 collective-permute-start.92
  448.1 8.8 %attend_back.3 = (bf16[512,256]{1,0:T(8,128)(2,1)S(1)}, f32[512,256]{1,0:T(8,128)S(1)}, f32[512,256]{1,0:T(8,128)S(1)}, bf16[512,256]{1,0:T(8,128)(2,1)S(1)}, bf16[512,256]{1,0:T(8,128)(2,1)S(1)}) custom-call(bf16[512,256]{1,0:T(8,128)(2,1)S(1)} %pad_maximum_fusion.41.q_ref, bf16[512,256]{1,0:T(8,128)(2,1)S(1)} %pad_maximum_fusion.42.k0_ref, ...), custom_call_target="tpu_custom_call" | custom-call | flops 5368709120 | bytes 3407872 | tf_op jit(solution)/shard_map/attend_back/pallas_call | solution.py:166
  458.8 6.9 collective-permute-start.95
  468.4 4.7 collective-permute-start.134
  491.6 6.8 collective-permute-start.137
  507.6 4.0 collective-permute-start.117
  518.5 6.9 collective-permute-start.120
  530.0 4.0 collective-permute-start.109
  536.0 3.9 collective-permute-start.126
  546.5 6.9 collective-permute-start.129
  562.5 7.0 %collective-permute-start.112 = (bf16[128,512]{1,0:T(8,128)(2,1)S(1)}, bf16[128,512]{1,0:T(8,128)(2,1)S(1)}, u32[]{:S(2)}, u32[]{:S(2)}) collective-permute-start(bf16[128,512]{1,0:T(8,128)(2,1)S(1)} %copy-done.95), channel_id=1, source_target_pairs={{0,32},{8,40},{16,48},{24,56},{32,0},{1,33},{9,41},{17,49},{25,57}... | collective-permute-start | bytes 393224 | tf_op jit(solution)/shard_map/ppermute | solution.py:298
  583.1 3.5 collective-permute-start.68
  595.8 4.0 collective-permute-start.83
  621.1 5.7 all-to-all-done.4
  627.5 8.7 %all-to-all-start.5 = ((f32[16,2,128]{2,1,0:T(2,128)}), f32[16,2,128]{2,1,0:T(2,128)S(1)}, u32[]{:S(2)}, u32[]{:S(2)}) async-start(f32[16,2,128]{2,1,0:T(2,128)} %bitcast.77), calls=%async_computation.5 | async-start | bytes 32768 | tf_op jit(solution)/shard_map/all_to_all | solution.py:402
  637.1 6.7 all-to-all-done.5
  643.8 3.6 all-to-all-start.3
  648.1 5.4 collective-permute-start.86
  669.9 6.9 collective-permute-start.78
  (1016 shorter events, 398.0 us)
Async XLA Ops:
  2.5 49.6 %collective-permute-start.4 = (bf16[128,512]{0,1:T(8,128)(2,1)S(1)}, bf16[128,512]{0,1:T(8,128)(2,1)}, u32[]{:S(2)}, u32[]{:S(2)}) collective-permute-start(bf16[128,512]{0,1:T(8,128)(2,1)S(1)} %get-tuple-element.263), channel_id=1, source_target_pairs={{0,64},{8,72},{64,0},{72,8},{16,80},{24,88},{80,16},{88,24},{32,96... | collective-permute-start | bytes 393224 | tf_op jit(solution)/shard_map/ppermute | solution.py:32
  6.5 49.7 %collective-permute-start.3 = (bf16[128,512]{0,1:T(8,128)(2,1)S(1)}, bf16[128,512]{0,1:T(8,128)(2,1)}, u32[]{:S(2)}, u32[]{:S(2)}) collective-permute-start(bf16[128,512]{0,1:T(8,128)(2,1)S(1)} %get-tuple-element.263), channel_id=1, source_target_pairs={{0,8},{8,64},{64,72},{72,0},{16,24},{24,80},{80,88},{88,16},{32,40... | collective-permute-start | bytes 393224 | tf_op jit(solution)/shard_map/ppermute | solution.py:32
  7.6 49.7 %collective-permute-start.5 = (bf16[128,512]{0,1:T(8,128)(2,1)S(1)}, bf16[128,512]{0,1:T(8,128)(2,1)S(1)}, u32[]{:S(2)}, u32[]{:S(2)}) collective-permute-start(bf16[128,512]{0,1:T(8,128)(2,1)S(1)} %get-tuple-element.263), channel_id=1, source_target_pairs={{0,72},{8,0},{64,8},{72,64},{16,88},{24,16},{80,24},{88,80},{32,10... | collective-permute-start | bytes 393224 | tf_op jit(solution)/shard_map/ppermute | solution.py:32
  12.5 54.8 %collective-permute-start.18 = (bf16[128,1024]{1,0:T(8,128)(2,1)}, bf16[128,1024]{1,0:T(8,128)(2,1)S(1)}, u32[]{:S(2)}, u32[]{:S(2)}) collective-permute-start(bf16[128,1024]{1,0:T(8,128)(2,1)} %pad_maximum_fusion.44), channel_id=1, source_target_pairs={{0,64},{8,72},{64,0},{72,8},{16,80},{24,88},{80,16},{88,24},{32,96... | collective-permute-start | bytes 786440 | tf_op jit(solution)/shard_map/ppermute | solution.py:32
  12.5 51.1 %collective-permute-start.17 = (bf16[128,1024]{1,0:T(8,128)(2,1)}, bf16[128,1024]{1,0:T(8,128)(2,1)}, u32[]{:S(2)}, u32[]{:S(2)}) collective-permute-start(bf16[128,1024]{1,0:T(8,128)(2,1)} %pad_maximum_fusion.44), channel_id=1, source_target_pairs={{0,8},{8,64},{64,72},{72,0},{16,24},{24,80},{80,88},{88,16},{32,40... | collective-permute-start | bytes 786440 | tf_op jit(solution)/shard_map/ppermute | solution.py:32
  41.5 47.7 %all-to-all-start = ((bf16[16,16,1024]{2,1,0:T(8,128)(2,1)}), bf16[16,16,1024]{2,1,0:T(8,128)(2,1)S(1)}, u32[]{:S(2)}, u32[]{:S(2)}) async-start(bf16[16,16,1024]{2,1,0:T(8,128)(2,1)} %constant_dynamic-update-slice_fusion), calls=%async_computation | async-start | bytes 1048576 | tf_op jit(solution)/shard_map/all_to_all | solution.py:315
  58.2 18.2 %collective-permute-start.7 = (bf16[2,128,512]{2,1,0:T(8,128)(2,1)S(1)}, bf16[2,128,512]{2,1,0:T(8,128)(2,1)S(1)}, u32[]{:S(2)}, u32[]{:S(2)}) collective-permute-start(bf16[2,128,512]{2,1,0:T(8,128)(2,1)S(1)} %get-tuple-element.235), channel_id=1, source_target_pairs={{0,32},{8,40},{64,96},{72,104},{16,48},{24,56},{80,112},{88,120},{... | collective-permute-start | bytes 786440 | tf_op jit(solution)/shard_map/ppermute | solution.py:32
  63.6 19.0 %collective-permute-start.8 = (bf16[2,128,512]{2,1,0:T(8,128)(2,1)S(1)}, bf16[2,128,512]{2,1,0:T(8,128)(2,1)S(1)}, u32[]{:S(2)}, u32[]{:S(2)}) collective-permute-start(bf16[2,128,512]{2,1,0:T(8,128)(2,1)S(1)} %get-tuple-element.235), channel_id=1, source_target_pairs={{0,48},{8,56},{64,112},{72,120},{16,0},{24,8},{80,64},{88,72},{32,... | collective-permute-start | bytes 786440 | tf_op jit(solution)/shard_map/ppermute | solution.py:32
  67.4 21.1 %collective-permute-start.30 = (bf16[2,128,512]{2,1,0:T(8,128)(2,1)}, bf16[2,128,512]{2,1,0:T(8,128)(2,1)S(1)}, u32[]{:S(2)}, u32[]{:S(2)}) collective-permute-start(bf16[2,128,512]{2,1,0:T(8,128)(2,1)} %get-tuple-element.236), channel_id=1, source_target_pairs={{0,16},{8,24},{64,80},{72,88},{16,32},{24,40},{80,96},{88,104},{32... | collective-permute-start | bytes 786440 | tf_op jit(solution)/shard_map/ppermute | solution.py:32
  69.5 32.0 %collective-permute-start.21 = (bf16[2,128,1024]{2,1,0:T(8,128)(2,1)}, bf16[2,128,1024]{2,1,0:T(8,128)(2,1)}, u32[]{:S(2)}, u32[]{:S(2)}) collective-permute-start(bf16[2,128,1024]{2,1,0:T(8,128)(2,1)} %get-tuple-element.190), channel_id=1, source_target_pairs={{0,32},{8,40},{64,96},{72,104},{16,48},{24,56},{80,112},{88,120},{... | collective-permute-start | bytes 1572872 | tf_op jit(solution)/shard_map/ppermute | solution.py:32
  73.7 25.8 %collective-permute-start.20 = (bf16[2,128,1024]{2,1,0:T(8,128)(2,1)}, bf16[2,128,1024]{2,1,0:T(8,128)(2,1)S(1)}, u32[]{:S(2)}, u32[]{:S(2)}) collective-permute-start(bf16[2,128,1024]{2,1,0:T(8,128)(2,1)} %get-tuple-element.190), channel_id=1, source_target_pairs={{0,16},{8,24},{64,80},{72,88},{16,32},{24,40},{80,96},{88,104},{32... | collective-permute-start | bytes 1572872 | tf_op jit(solution)/shard_map/ppermute | solution.py:32
  82.8 22.7 %collective-permute-start.9 = (bf16[1024,512]{1,0:T(8,128)(2,1)S(1)}, bf16[1024,512]{1,0:T(8,128)(2,1)}, u32[]{:S(2)}, u32[]{:S(2)}) collective-permute-start(bf16[1024,512]{1,0:T(8,128)(2,1)S(1)} %bitcast.242), channel_id=1, source_target_pairs={{0,1},{1,0},{2,3},{3,2},{4,5},{5,4},{6,7},{7,6},{8,9},{9,8},{10,11... | collective-permute-start | bytes 3145736 | tf_op jit(solution)/shard_map/ppermute | solution.py:24
  90.0 19.1 %collective-permute-start.2 = (bf16[128,1024]{1,0:T(8,128)(2,1)S(1)}, bf16[128,1024]{1,0:T(8,128)(2,1)S(1)}, u32[]{:S(2)}, u32[]{:S(2)}) collective-permute-start(bf16[128,1024]{1,0:T(8,128)(2,1)S(1)} %fusion.75), channel_id=1, source_target_pairs={{0,4},{1,5},{2,6},{3,7},{4,0},{5,1},{6,2},{7,3},{8,12},{9,13},{10,... | collective-permute-start | bytes 786440 | tf_op jit(solution)/shard_map/ppermute | solution.py:20
  101.5 73.7 %collective-permute-start.31 = (bf16[2,128,512]{2,1,0:T(8,128)(2,1)}, bf16[2,128,512]{2,1,0:T(8,128)(2,1)S(1)}, u32[]{:S(2)}, u32[]{:S(2)}) collective-permute-start(bf16[2,128,512]{2,1,0:T(8,128)(2,1)} %get-tuple-element.236), channel_id=1, source_target_pairs={{0,32},{8,40},{64,96},{72,104},{16,48},{24,56},{80,112},{88,120},{... | collective-permute-start | bytes 786440 | tf_op jit(solution)/shard_map/ppermute | solution.py:32
  118.9 30.6 %collective-permute-start.23 = (bf16[1024,1024]{1,0:T(8,128)(2,1)S(1)}, bf16[1024,1024]{1,0:T(8,128)(2,1)S(1)}, u32[]{:S(2)}, u32[]{:S(2)}) collective-permute-start(bf16[1024,1024]{1,0:T(8,128)(2,1)S(1)} %bitcast.238), channel_id=1, source_target_pairs={{0,1},{1,0},{2,3},{3,2},{4,5},{5,4},{6,7},{7,6},{8,9},{9,8},{10,11... | collective-permute-start | bytes 6291464 | tf_op jit(solution)/shard_map/ppermute | solution.py:24
  141.6 35.2 %collective-permute-start.32 = (bf16[2,128,512]{2,1,0:T(8,128)(2,1)}, bf16[2,128,512]{2,1,0:T(8,128)(2,1)S(1)}, u32[]{:S(2)}, u32[]{:S(2)}) collective-permute-start(bf16[2,128,512]{2,1,0:T(8,128)(2,1)} %get-tuple-element.236), channel_id=1, source_target_pairs={{0,48},{8,56},{64,112},{72,120},{16,0},{24,8},{80,64},{88,72},{32,... | collective-permute-start | bytes 786440 | tf_op jit(solution)/shard_map/ppermute | solution.py:32
  157.5 39.1 %collective-permute-start.42 = (bf16[2,128,1024]{2,1,0:T(8,128)(2,1)}, bf16[2,128,1024]{2,1,0:T(8,128)(2,1)}, u32[]{:S(2)}, u32[]{:S(2)}) collective-permute-start(bf16[2,128,1024]{2,1,0:T(8,128)(2,1)} %get-tuple-element.189), channel_id=1, source_target_pairs={{0,32},{8,40},{64,96},{72,104},{16,48},{24,56},{80,112},{88,120},{... | collective-permute-start | bytes 1572872 | tf_op jit(solution)/shard_map/ppermute | solution.py:32
  211.0 33.4 %collective-permute-start.44 = (bf16[1024,1024]{1,0:T(8,128)(2,1)}, bf16[1024,1024]{1,0:T(8,128)(2,1)S(1)}, u32[]{:S(2)}, u32[]{:S(2)}) collective-permute-start(bf16[1024,1024]{1,0:T(8,128)(2,1)} %bitcast.50), channel_id=1, source_target_pairs={{0,1},{1,0},{2,3},{3,2},{4,5},{5,4},{6,7},{7,6},{8,9},{9,8},{10,11... | collective-permute-start | bytes 6291464 | tf_op jit(solution)/shard_map/ppermute | solution.py:24
  218.8 19.5 %collective-permute-start.35 = (bf16[128,1024]{1,0:T(8,128)(2,1)S(1)}, bf16[128,1024]{1,0:T(8,128)(2,1)S(1)}, u32[]{:S(2)}, u32[]{:S(2)}) collective-permute-start(bf16[128,1024]{1,0:T(8,128)(2,1)S(1)} %get-tuple-element.191), channel_id=1, source_target_pairs={{0,6},{1,7},{2,0},{3,1},{4,2},{5,3},{6,4},{7,5},{8,14},{9,15},{10,... | collective-permute-start | bytes 786440 | tf_op jit(solution)/shard_map/ppermute | solution.py:20
  220.8 21.2 %collective-permute-start.37 = (bf16[128,1024]{1,0:T(8,128)(2,1)S(1)}, bf16[128,1024]{1,0:T(8,128)(2,1)S(1)}, u32[]{:S(2)}, u32[]{:S(2)}) collective-permute-start(bf16[128,1024]{1,0:T(8,128)(2,1)S(1)} %get-tuple-element.192), channel_id=1, source_target_pairs={{0,4},{1,5},{2,6},{3,7},{4,0},{5,1},{6,2},{7,3},{8,12},{9,13},{10,... | collective-permute-start | bytes 786440 | tf_op jit(solution)/shard_map/ppermute | solution.py:20
  222.2 19.8 %collective-permute-start.36 = (bf16[128,1024]{1,0:T(8,128)(2,1)S(1)}, bf16[128,1024]{1,0:T(8,128)(2,1)S(1)}, u32[]{:S(2)}, u32[]{:S(2)}) collective-permute-start(bf16[128,1024]{1,0:T(8,128)(2,1)S(1)} %get-tuple-element.193), channel_id=1, source_target_pairs={{0,2},{1,3},{2,4},{3,5},{4,6},{5,7},{6,0},{7,1},{8,10},{9,11},{10,... | collective-permute-start | bytes 786440 | tf_op jit(solution)/shard_map/ppermute | solution.py:20
  224.2 40.7 %collective-permute-start.47 = (bf16[128,1024]{1,0:T(8,128)(2,1)S(1)}, bf16[128,1024]{1,0:T(8,128)(2,1)S(1)}, u32[]{:S(2)}, u32[]{:S(2)}) collective-permute-start(bf16[128,1024]{1,0:T(8,128)(2,1)S(1)} %copy-done.81), channel_id=1, source_target_pairs={{0,4},{1,5},{2,6},{3,7},{4,0},{5,1},{6,2},{7,3},{8,12},{9,13},{10,... | collective-permute-start | bytes 786440 | tf_op jit(solution)/shard_map/ppermute | solution.py:20
  238.3 26.7 %collective-permute-start.46 = (bf16[128,1024]{1,0:T(8,128)(2,1)S(1)}, bf16[128,1024]{1,0:T(8,128)(2,1)S(1)}, u32[]{:S(2)}, u32[]{:S(2)}) collective-permute-start(bf16[128,1024]{1,0:T(8,128)(2,1)S(1)} %copy-done.81), channel_id=1, source_target_pairs={{0,6},{1,7},{2,0},{3,1},{4,2},{5,3},{6,4},{7,5},{8,14},{9,15},{10,... | collective-permute-start | bytes 786440 | tf_op jit(solution)/shard_map/ppermute | solution.py:20
  286.6 57.4 %collective-permute-start.133 = (bf16[1024,512]{1,0:T(8,128)(2,1)}, bf16[1024,512]{1,0:T(8,128)(2,1)}, u32[]{:S(2)}, u32[]{:S(2)}) collective-permute-start(bf16[1024,512]{1,0:T(8,128)(2,1)} %slice.1087), channel_id=1, source_target_pairs={{0,1},{1,0},{2,3},{3,2},{4,5},{5,4},{6,7},{7,6},{8,9},{9,8},{10,11... | collective-permute-start | bytes 3145736 | tf_op jit(solution)/shard_map/ppermute | solution.py:24
  306.4 40.9 %collective-permute-start.116 = (bf16[1024,512]{1,0:T(8,128)(2,1)}, bf16[1024,512]{1,0:T(8,128)(2,1)}, u32[]{:S(2)}, u32[]{:S(2)}) collective-permute-start(bf16[1024,512]{1,0:T(8,128)(2,1)} %slice.1089), channel_id=1, source_target_pairs={{0,1},{1,0},{2,3},{3,2},{4,5},{5,4},{6,7},{7,6},{8,9},{9,8},{10,11... | collective-permute-start | bytes 3145736 | tf_op jit(solution)/shard_map/ppermute | solution.py:24
  328.3 108.9 %collective-permute-start.100 = (bf16[128,128]{1,0:T(8,128)(2,1)}, bf16[128,128]{1,0:T(8,128)(2,1)}, u32[]{:S(2)}, u32[]{:S(2)}) collective-permute-start(bf16[128,128]{1,0:T(8,128)(2,1)} %get-tuple-element.237), channel_id=1, source_target_pairs={{0,8},{8,16},{16,24},{24,32},{32,40},{1,9},{9,17},{17,25},{25,33},... | collective-permute-start | bytes 98312 | tf_op jit(solution)/shard_map/ppermute | solution.py:298
  330.2 108.4 %collective-permute-start.106 = (bf16[128,128]{1,0:T(8,128)(2,1)}, bf16[128,128]{1,0:T(8,128)(2,1)}, u32[]{:S(2)}, u32[]{:S(2)}) collective-permute-start(bf16[128,128]{1,0:T(8,128)(2,1)} %get-tuple-element.238), channel_id=1, source_target_pairs={{0,56},{8,0},{16,8},{24,16},{32,24},{1,57},{9,1},{17,9},{25,17},{3... | collective-permute-start | bytes 98312 | tf_op jit(solution)/shard_map/ppermute | solution.py:298
  418.4 21.5 %collective-permute-start.105 = (bf16[128,128]{1,0:T(8,128)(2,1)}, bf16[128,128]{1,0:T(8,128)(2,1)}, u32[]{:S(2)}, u32[]{:S(2)}) collective-permute-start(bf16[128,128]{1,0:T(8,128)(2,1)} %get-tuple-element.239), channel_id=1, source_target_pairs={{0,48},{8,56},{16,0},{24,8},{32,16},{1,49},{9,57},{17,1},{25,9},{3... | collective-permute-start | bytes 98312 | tf_op jit(solution)/shard_map/ppermute | solution.py:298
  420.7 19.5 %collective-permute-start.104 = (bf16[128,128]{1,0:T(8,128)(2,1)}, bf16[128,128]{1,0:T(8,128)(2,1)}, u32[]{:S(2)}, u32[]{:S(2)}) collective-permute-start(bf16[128,128]{1,0:T(8,128)(2,1)} %get-tuple-element.240), channel_id=1, source_target_pairs={{0,40},{8,48},{16,56},{24,0},{32,8},{1,41},{9,49},{17,57},{25,1},{... | collective-permute-start | bytes 98312 | tf_op jit(solution)/shard_map/ppermute | solution.py:298
  438.6 18.3 %collective-permute-start.101 = (bf16[128,128]{1,0:T(8,128)(2,1)S(1)}, bf16[128,128]{1,0:T(8,128)(2,1)S(1)}, u32[]{:S(2)}, u32[]{:S(2)}) collective-permute-start(bf16[128,128]{1,0:T(8,128)(2,1)S(1)} %copy-done.120), channel_id=1, source_target_pairs={{0,16},{8,24},{16,32},{24,40},{32,48},{1,17},{9,25},{17,33},{25,41... | collective-permute-start | bytes 98312 | tf_op jit(solution)/shard_map/ppermute | solution.py:298
  439.9 44.9 %collective-permute-start.108 = (bf16[1024,512]{1,0:T(8,128)(2,1)}, bf16[1024,512]{1,0:T(8,128)(2,1)}, u32[]{:S(2)}, u32[]{:S(2)}) collective-permute-start(bf16[1024,512]{1,0:T(8,128)(2,1)} %slice.1090), channel_id=1, source_target_pairs={{0,1},{1,0},{2,3},{3,2},{4,5},{5,4},{6,7},{7,6},{8,9},{9,8},{10,11... | collective-permute-start | bytes 3145736 | tf_op jit(solution)/shard_map/ppermute | solution.py:24
  440.2 18.6 %collective-permute-start.92 = (bf16[128,128]{1,0:T(8,128)(2,1)S(1)}, bf16[128,128]{1,0:T(8,128)(2,1)S(1)}, u32[]{:S(2)}, u32[]{:S(2)}) collective-permute-start(bf16[128,128]{1,0:T(8,128)(2,1)S(1)} %get-tuple-element.244), channel_id=1, source_target_pairs={{0,8},{8,16},{16,24},{24,32},{32,40},{1,9},{9,17},{17,25},{25,33},... | collective-permute-start | bytes 98312 | tf_op jit(solution)/shard_map/ppermute | solution.py:298
  444.2 21.5 %collective-permute-start.98 = (bf16[128,128]{1,0:T(8,128)(2,1)S(1)}, bf16[128,128]{1,0:T(8,128)(2,1)S(1)}, u32[]{:S(2)}, u32[]{:S(2)}) collective-permute-start(bf16[128,128]{1,0:T(8,128)(2,1)S(1)} %get-tuple-element.245), channel_id=1, source_target_pairs={{0,56},{8,0},{16,8},{24,16},{32,24},{1,57},{9,1},{17,9},{25,17},{3... | collective-permute-start | bytes 98312 | tf_op jit(solution)/shard_map/ppermute | solution.py:298
  446.1 20.9 %collective-permute-start.97 = (bf16[128,128]{1,0:T(8,128)(2,1)S(1)}, bf16[128,128]{1,0:T(8,128)(2,1)S(1)}, u32[]{:S(2)}, u32[]{:S(2)}) collective-permute-start(bf16[128,128]{1,0:T(8,128)(2,1)S(1)} %get-tuple-element.246), channel_id=1, source_target_pairs={{0,48},{8,56},{16,0},{24,8},{32,16},{1,49},{9,57},{17,1},{25,9},{3... | collective-permute-start | bytes 98312 | tf_op jit(solution)/shard_map/ppermute | solution.py:298
  468.4 36.5 %collective-permute-start.134 = (bf16[128,512]{1,0:T(8,128)(2,1)}, bf16[128,512]{1,0:T(8,128)(2,1)}, u32[]{:S(2)}, u32[]{:S(2)}) collective-permute-start(bf16[128,512]{1,0:T(8,128)(2,1)} %get-tuple-element.146), channel_id=1, source_target_pairs={{0,8},{8,16},{16,24},{24,32},{32,40},{1,9},{9,17},{17,25},{25,33},... | collective-permute-start | bytes 393224 | tf_op jit(solution)/shard_map/ppermute | solution.py:298
  473.0 33.3 %collective-permute-start.140 = (bf16[128,512]{1,0:T(8,128)(2,1)}, bf16[128,512]{1,0:T(8,128)(2,1)}, u32[]{:S(2)}, u32[]{:S(2)}) collective-permute-start(bf16[128,512]{1,0:T(8,128)(2,1)} %get-tuple-element.147), channel_id=1, source_target_pairs={{0,56},{8,0},{16,8},{24,16},{32,24},{1,57},{9,1},{17,9},{25,17},{3... | collective-permute-start | bytes 393224 | tf_op jit(solution)/shard_map/ppermute | solution.py:298
  482.1 25.5 %collective-permute-start.139 = (bf16[128,512]{1,0:T(8,128)(2,1)}, bf16[128,512]{1,0:T(8,128)(2,1)}, u32[]{:S(2)}, u32[]{:S(2)}) collective-permute-start(bf16[128,512]{1,0:T(8,128)(2,1)} %get-tuple-element.148), channel_id=1, source_target_pairs={{0,48},{8,56},{16,0},{24,8},{32,16},{1,49},{9,57},{17,1},{25,9},{3... | collective-permute-start | bytes 393224 | tf_op jit(solution)/shard_map/ppermute | solution.py:298
  488.3 24.4 %collective-permute-start.138 = (bf16[128,512]{1,0:T(8,128)(2,1)}, bf16[128,512]{1,0:T(8,128)(2,1)}, u32[]{:S(2)}, u32[]{:S(2)}) collective-permute-start(bf16[128,512]{1,0:T(8,128)(2,1)} %get-tuple-element.149), channel_id=1, source_target_pairs={{0,40},{8,48},{16,56},{24,0},{32,8},{1,41},{9,49},{17,57},{25,1},{... | collective-permute-start | bytes 393224 | tf_op jit(solution)/shard_map/ppermute | solution.py:298
  491.6 23.0 %collective-permute-start.137 = (bf16[128,512]{1,0:T(8,128)(2,1)}, bf16[128,512]{1,0:T(8,128)(2,1)}, u32[]{:S(2)}, u32[]{:S(2)}) collective-permute-start(bf16[128,512]{1,0:T(8,128)(2,1)} %get-tuple-element.150), channel_id=1, source_target_pairs={{0,32},{8,40},{16,48},{24,56},{32,0},{1,33},{9,41},{17,49},{25,57}... | collective-permute-start | bytes 393224 | tf_op jit(solution)/shard_map/ppermute | solution.py:298
  576.5 19.3 %collective-permute-start.73 = (bf16[128,1024]{1,0:T(8,128)(2,1)}, bf16[128,1024]{1,0:T(8,128)(2,1)}, u32[]{:S(2)}, u32[]{:S(2)}) collective-permute-start(bf16[128,1024]{1,0:T(8,128)(2,1)} %get-tuple-element.187), channel_id=1, source_target_pairs={{0,4},{1,5},{2,6},{3,7},{4,0},{5,1},{6,2},{7,3},{8,12},{9,13},{10,... | collective-permute-start | bytes 786440 | tf_op jit(solution)/shard_map/ppermute | solution.py:20
  576.5 23.4 %collective-permute-start.72 = (bf16[128,1024]{1,0:T(8,128)(2,1)}, bf16[128,1024]{1,0:T(8,128)(2,1)}, u32[]{:S(2)}, u32[]{:S(2)}) collective-permute-start(bf16[128,1024]{1,0:T(8,128)(2,1)} %get-tuple-element.188), channel_id=1, source_target_pairs={{0,2},{1,3},{2,4},{3,5},{4,6},{5,7},{6,0},{7,1},{8,10},{9,11},{10,... | collective-permute-start | bytes 786440 | tf_op jit(solution)/shard_map/ppermute | solution.py:20
  583.1 18.6 %collective-permute-start.68 = (bf16[128,1024]{1,0:T(8,128)(2,1)}, bf16[128,1024]{1,0:T(8,128)(2,1)}, u32[]{:S(2)}, u32[]{:S(2)}) collective-permute-start(bf16[128,1024]{1,0:T(8,128)(2,1)} %get-tuple-element.174), channel_id=1, source_target_pairs={{0,6},{1,7},{2,0},{3,1},{4,2},{5,3},{6,4},{7,5},{8,14},{9,15},{10,... | collective-permute-start | bytes 786440 | tf_op jit(solution)/shard_map/ppermute | solution.py:20
  595.8 59.7 %collective-permute-start.83 = (bf16[128,384]{0,1:T(8,128)(2,1)}, bf16[128,384]{0,1:T(8,128)(2,1)}, u32[]{:S(2)}, u32[]{:S(2)}) collective-permute-start(bf16[128,384]{0,1:T(8,128)(2,1)} %get-tuple-element.200), channel_id=1, source_target_pairs={{0,8},{8,16},{16,24},{24,32},{32,40},{1,9},{9,17},{17,25},{25,33},... | collective-permute-start | bytes 294920 | tf_op jit(solution)/shard_map/ppermute | solution.py:298
  599.8 59.1 %collective-permute-start.89 = (bf16[128,384]{0,1:T(8,128)(2,1)}, bf16[128,384]{0,1:T(8,128)(2,1)}, u32[]{:S(2)}, u32[]{:S(2)}) collective-permute-start(bf16[128,384]{0,1:T(8,128)(2,1)} %get-tuple-element.201), channel_id=1, source_target_pairs={{0,56},{8,0},{16,8},{24,16},{32,24},{1,57},{9,1},{17,9},{25,17},{3... | collective-permute-start | bytes 294920 | tf_op jit(solution)/shard_map/ppermute | solution.py:298
  601.8 58.5 %collective-permute-start.88 = (bf16[128,384]{0,1:T(8,128)(2,1)}, bf16[128,384]{0,1:T(8,128)(2,1)}, u32[]{:S(2)}, u32[]{:S(2)}) collective-permute-start(bf16[128,384]{0,1:T(8,128)(2,1)} %get-tuple-element.202), channel_id=1, source_target_pairs={{0,48},{8,56},{16,0},{24,8},{32,16},{1,49},{9,57},{17,1},{25,9},{3... | collective-permute-start | bytes 294920 | tf_op jit(solution)/shard_map/ppermute | solution.py:298
  603.7 59.7 %collective-permute-start.87 = (bf16[128,384]{0,1:T(8,128)(2,1)}, bf16[128,384]{0,1:T(8,128)(2,1)}, u32[]{:S(2)}, u32[]{:S(2)}) collective-permute-start(bf16[128,384]{0,1:T(8,128)(2,1)} %get-tuple-element.203), channel_id=1, source_target_pairs={{0,40},{8,48},{16,56},{24,0},{32,8},{1,41},{9,49},{17,57},{25,1},{... | collective-permute-start | bytes 294920 | tf_op jit(solution)/shard_map/ppermute | solution.py:298
  605.6 42.4 %collective-permute-start.74 = (bf16[1024,384]{0,1:T(8,128)(2,1)}, bf16[1024,384]{0,1:T(8,128)(2,1)}, u32[]{:S(2)}, u32[]{:S(2)}) collective-permute-start(bf16[1024,384]{0,1:T(8,128)(2,1)} %slice.1092), channel_id=1, source_target_pairs={{0,1},{1,0},{2,3},{3,2},{4,5},{5,4},{6,7},{7,6},{8,9},{9,8},{10,11... | collective-permute-start | bytes 2359304 | tf_op jit(solution)/shard_map/ppermute | solution.py:24
  643.8 36.4 %all-to-all-start.3 = ((bf16[16,16,1024]{2,1,0:T(8,128)(2,1)}), bf16[16,16,1024]{2,1,0:T(8,128)(2,1)S(1)}, u32[]{:S(2)}, u32[]{:S(2)}) async-start(bf16[16,16,1024]{2,1,0:T(8,128)(2,1)} %pad_maximum_fusion.36), calls=%async_computation.3 | async-start | bytes 1048576 | tf_op jit(solution)/shard_map/all_to_all | solution.py:373
  (289 other events, 4336.6 us)

commit v2 on v1

v2 whole, which is shorter than its diff:
```python
import jax
import jax.numpy as jnp
from jax import lax
from jax.experimental import pallas as pl
from jax.experimental.pallas import tpu as pltpu
from jax.sharding import PartitionSpec as P

SS = ("section", "seq")
EPS = 1e-6
F32 = jnp.float32
BF = jnp.bfloat16
D = 1024
HEAD = 64
TOK = 128
GROUPS = [0, 1, 2, 3, 4, None, None, None, 5, 6, 7, 8, None, None, None, None]
SLOT = [GROUPS.index(i) for i in range(9)]


def move_x(v, d):
    return lax.ppermute(v, "tensor", [(i, (i + 2 * d) % 8) for i in range(8)])


def move_core(v):
    return lax.ppermute(v, "tensor", [(i, i ^ 1) for i in range(8)])


def move_section(v):
    return lax.ppermute(v, "section", [(0, 1), (1, 0)])


def widen(v):
    return v, move_x(v, 1), move_x(v, -1), move_x(v, 2)


def narrow(parts):
    own, back, ahead, far = parts
    return own, move_x(back, -1), move_x(ahead, 1), move_x(far, 2)


def dot(a, b, dims, out=F32):
    return lax.dot_general(a, b, (dims, ((), ())), preferred_element_type=F32).astype(out)


NN = ((1,), (0,))
NT = ((1,), (1,))
TN = ((0,), (0,))


def entire(a):
    zeros = (0,) * len(a.shape)
    return pl.BlockSpec(a.shape, lambda i: zeros, pipeline_mode=pl.Buffered(1))


def part(width, k):
    return pl.BlockSpec((1024, width), lambda i: (0, k), pipeline_mode=pl.Buffered(1))


def whole(kernel, out_shape, *args, name, cols=None):
    return pl.pallas_call(
        kernel,
        grid=(1,),
        out_shape=out_shape,
        in_specs=[entire(a) for a in args] if cols is None else [
            entire(a) if a.shape[1:] != (512,) or a.shape[0] != 1024 else part(*cols) for a in args
        ],
        out_specs=jax.tree.map(entire, out_shape),
        compiler_params=pltpu.CompilerParams(vmem_limit_bytes=60 * 2**20),
        cost_estimate=pl.CostEstimate(flops=0, bytes_accessed=4096, transcendentals=0),
        name=name,
    )(*args)


def out(shape, dtype):
    return jax.ShapeDtypeStruct(shape, dtype)


def row(p_ref, r):
    return jnp.concatenate([p_ref[q, r : r + 1, :] for q in range(8)], axis=1)


def bias_rows(p_ref, side):
    return sum(p_ref[q, 8 + 8 * side : 16 + 8 * side, :] for q in range(8))


def unit_of(v):
    centred = v - jnp.mean(v, axis=-1, keepdims=True)
    scale = lax.rsqrt(jnp.mean(centred * centred, axis=-1, keepdims=True) + EPS)
    return centred * scale, scale


def norm_back(v, gain, grad):
    unit, scale = unit_of(v)
    inner = grad * gain
    part = scale * (
        inner
        - jnp.mean(inner, axis=-1, keepdims=True)
        - unit * jnp.mean(inner * unit, axis=-1, keepdims=True)
    )
    return part, jnp.sum(grad * unit, 0, keepdims=True), jnp.sum(grad, 0, keepdims=True)


def total(own, back, ahead, far):
    return own[...] + back[...].astype(F32) + ahead[...].astype(F32) + far[...].astype(F32)


def start_kernel(x_ref, p_ref, a_ref):
    unit, _ = unit_of(x_ref[...].astype(F32))
    a_ref[...] = (unit * row(p_ref, 0) + row(p_ref, 1)).astype(BF)


def qkv_kernel(a0, a1, a2, a3, w0, w1, p_ref, o_ref, a_ref):
    join_rows((a0, a1, a2, a3), a_ref)
    mix_rows((a0, a1, a2, a3), w0, w1, p_ref, o_ref)


def mix_rows(pieces, w0, w1, p_ref, o_ref):
    for side, w in enumerate((w0, w1)):
        b = bias_rows(p_ref, side)
        b = jnp.concatenate([b[0:1], b[1:2], b[2:3]], axis=1)
        for i, a in enumerate(pieces):
            o_ref[128 * i : 128 * i + 128, 384 * side : 384 * side + 384] = (
                jnp.dot(a[...], w[...], preferred_element_type=F32) + b
            ).astype(BF)


def join_rows(pieces, ref):
    for i, piece in enumerate(pieces):
        ref[128 * i : 128 * i + 128, :] = piece[...]


def first_qkv_kernel(x0, x1, x2, x3, w0, w1, p_ref, o_ref, a_ref):
    pieces = [a_ref.at[128 * i : 128 * i + 128] for i in range(4)]
    for x, a in zip((x0, x1, x2, x3), pieces):
        start_kernel(x, p_ref, a)
    mix_rows(pieces, w0, w1, p_ref, o_ref)


def spread(left, own_ref, others):
    own_ref[...] = left(0)
    for i, ref in enumerate(others):
        ref[...] = left(i + 1).astype(BF)


def spread_out():
    return [out((TOK, D), F32)] + [out((TOK, D), BF)] * 3


def pair_kernel(l0, l1, w0, w1, own, back, ahead, far):
    def left(i):
        at = slice(128 * i, 128 * i + 128)
        return dot(l0[at, :], w0[...], NT) + dot(l1[at, :], w1[...], NT)

    spread(left, own, (back, ahead, far))


def proj_kernel(o, w0, w1, own, back, ahead, far):
    w = jnp.concatenate([w0[...], w1[...]], axis=1)
    spread(lambda i: dot(o[128 * i : 128 * i + 128, :], w, NT), own, (back, ahead, far))


def mixed_kernel(g, w0, w1, own, back, ahead, far):
    w = jnp.concatenate([w0[...], w1[...]], axis=1)
    spread(lambda i: dot(g[128 * i : 128 * i + 128, :], w, NT), own, (back, ahead, far))


def middle_kernel(own, back, ahead, far, x_ref, p_ref, z_ref, x1_ref, a2_ref):
    z = total(own, back, ahead, far) + row(p_ref, 4)
    x1 = x_ref[...].astype(F32) + row(p_ref, 6) * z
    unit, _ = unit_of(x1)
    z_ref[...] = z
    x1_ref[...] = x1
    a2_ref[...] = (unit * row(p_ref, 2) + row(p_ref, 3)).astype(BF)


def up_kernel(a0, a1, a2, a3, w0, w1, p_ref, act0, act1, slope0, slope1, a_ref):
    join_rows((a0, a1, a2, a3), a_ref)
    for side, (w, act, slope) in enumerate(((w0, act0, slope0), (w1, act1, slope1))):
        b = bias_rows(p_ref, side)
        b = jnp.concatenate([b[3:4], b[4:5], b[5:6], b[6:7]], axis=1)
        for i, a in enumerate((a0, a1, a2, a3)):
            at = slice(128 * i, 128 * i + 128)
            u = jnp.dot(a[...], w[...], preferred_element_type=F32) + b
            half = 0.5 * (1.0 + lax.erf(u * (0.5**0.5)))
            act[at, :] = (u * half).astype(BF)
            slope[at, :] = (half + u * jnp.exp(-0.5 * u * u) * 0.3989422804014327).astype(BF)


def mlp_kernel(
    a0, a1, a2, a3, u0, u1, d0, d1, p_ref, act0, act1, slope0, slope1, a_ref, own, back, ahead, far
):
    up_kernel(a0, a1, a2, a3, u0, u1, p_ref, act0, act1, slope0, slope1, a_ref)
    pair_kernel(act0, act1, d0, d1, own, back, ahead, far)


def mlp_back_kernel(
    d0, d1, d2, d3, w0, w1, u0, u1, s0, s1, du0, du1, sums, d_ref, own, back, ahead, far
):
    join_rows((d0, d1, d2, d3), d_ref)
    du_kernel(d0, d1, d2, d3, w0, w1, s0, s1, du0, du1, sums)
    pair_kernel(du0, du1, u0, u1, own, back, ahead, far)


def end_kernel(own, back, ahead, far, x1_ref, p_ref, m_ref, y_ref):
    m = total(own, back, ahead, far) + row(p_ref, 5)
    m_ref[...] = m
    y_ref[...] = (x1_ref[...] + row(p_ref, 7) * m).astype(BF)


def end_next_kernel(own, back, ahead, far, x1_ref, p_ref, next_ref, m_ref, y_ref, a_ref):
    end_kernel(own, back, ahead, far, x1_ref, p_ref, m_ref, y_ref)
    start_kernel(y_ref, next_ref, a_ref)


def turn_kernel(*refs):
    scale = row(refs[4], 7)
    for dy, dm in zip(refs[:4], refs[5:]):
        dm[...] = (scale * dy[...].astype(F32)).astype(BF)


def du_kernel(d0, d1, d2, d3, w0, w1, s0, s1, du0, du1, sums_ref):
    for side, (w, slope, du_ref) in enumerate(((w0, s0, du0), (w1, s1, du1))):
        acc = jnp.zeros((1, 512), F32)
        for i, d in enumerate((d0, d1, d2, d3)):
            at = slice(128 * i, 128 * i + 128)
            du = (jnp.dot(d[...], w[...], preferred_element_type=F32) * slope[at, :].astype(F32)).astype(BF)
            du_ref[at, :] = du
            acc = acc + jnp.sum(du.astype(F32), 0, keepdims=True)
        for k in range(4):
            sums_ref[side, k : k + 1, :] = acc[:, 128 * k : 128 * k + 128]
        sums_ref[side, 4:, :] = jnp.zeros((4, 128), F32)


def middle_back_kernel(own, back, ahead, far, x1_ref, dy_ref, z_ref, p_ref, dx1_ref, dz_ref, rows_ref):
    part, dg, db = norm_back(x1_ref[...], row(p_ref, 2), total(own, back, ahead, far))
    dx1 = dy_ref[...].astype(F32) + part
    scale = row(p_ref, 6)
    dx1_ref[...] = dx1
    dz_ref[...] = (scale * dx1).astype(BF)
    rows_ref[0:1, :] = dg
    rows_ref[1:2, :] = db
    rows_ref[2:3, :] = scale * jnp.sum(dx1, 0, keepdims=True)
    rows_ref[3:4, :] = jnp.sum(dx1 * z_ref[...], 0, keepdims=True)


def do_kernel(d0, d1, d2, d3, w0, w1, o_ref, d_ref):
    join_rows((d0, d1, d2, d3), d_ref)
    w = jnp.concatenate([w0[...], w1[...]], axis=1)
    for i, d in enumerate((d0, d1, d2, d3)):
        o_ref[128 * i : 128 * i + 128, :] = jnp.dot(d[...], w, preferred_element_type=F32).astype(BF)


def pack_out(out_ref, ends, vec, bias_ref):
    for q in range(8):
        for k in range(8):
            out_ref[q, 16 * k : 16 * k + 16, :] = ends[16 * q : 16 * q + 16, 128 * k : 128 * k + 128]
        part = [v[:, 128 * q : 128 * q + 128] for v in vec]
        part = jnp.concatenate(part + [bias_ref[0], bias_ref[1]], axis=0)
        high = part.astype(BF).astype(F32)
        out_ref[q, 128:176, :] = jnp.concatenate([high, part - high], axis=0).astype(BF)


def first_back(da, x_ref, dx1_ref, p_ref, dy_ref, m_ref, mid_ref):
    part, dg, db = norm_back(x_ref[...].astype(F32), row(p_ref, 0), total(*da))
    dy = dy_ref[...].astype(F32)
    vec = [
        dg, db, mid_ref[0:1, :], mid_ref[1:2, :], mid_ref[2:3, :],
        row(p_ref, 7) * jnp.sum(dy, 0, keepdims=True),
        mid_ref[3:4, :],
        jnp.sum(dy * m_ref[...], 0, keepdims=True),
    ]
    return (dx1_ref[...] + part).astype(BF), vec


def last_back_kernel(own, back, ahead, far, x, dx1, p, dy, m, mid, bias, out_ref):
    dx, vec = first_back((own, back, ahead, far), x, dx1, p, dy, m, mid)
    pack_out(out_ref, dx, vec, bias)


def next_back_kernel(
    own, back, ahead, far, x, dx1, p, dy, m, mid, bias, y_ref, next_ref, out_ref, dx_ref, dm_ref
):
    dx, vec = first_back((own, back, ahead, far), x, dx1, p, dy, m, mid)
    dx_ref[...] = dx
    dm_ref[...] = (row(next_ref, 7) * dx.astype(F32)).astype(BF)
    pack_out(out_ref, y_ref[...], vec, bias)


def attend_kernel(q_ref, k0_ref, v0_ref, k1_ref, v1_ref, o_ref, lse_ref):
    rows = q_ref.shape[0]
    lane = lax.broadcasted_iota(jnp.int32, (rows, 128), 1)
    k = jnp.concatenate([k0_ref[...], k1_ref[...]], 0)
    v = jnp.concatenate([v0_ref[...], v1_ref[...]], 0)
    q = q_ref[...] * jnp.asarray(0.125, BF)
    zero = jnp.zeros_like(q)
    outs = []
    for h in range(2):
        mine = (lane < HEAD) if h == 0 else (lane >= HEAD)
        qh = jnp.where(mine, q, zero)
        s = lax.dot_general(k, qh, (((1,), (1,)), ((), ())), preferred_element_type=F32)
        top = jnp.max(s, axis=0, keepdims=True)
        p = jnp.exp(s - top)
        total = jnp.sum(p, axis=0, keepdims=True)
        o = lax.dot_general(v, p.astype(BF), (((0,), (0,)), ((), ())), preferred_element_type=F32)
        outs.append(o * (1.0 / total))
        lse_ref[0, h : h + 1, :] = top + jnp.log(total)
    sub = lax.broadcasted_iota(jnp.int32, outs[0].shape, 0)
    o_ref[...] = jnp.where(sub < HEAD, outs[0], outs[1]).T.astype(BF)


def column(rows, part, swap=False, tall=False):
    if swap:
        return pl.BlockSpec((rows, 128), lambda p, r: (0, 3 * (1 - p) + part))
    if tall:
        return pl.BlockSpec((rows, 128), lambda p, r: (0, 3 * p + part))
    return pl.BlockSpec((rows, 128), lambda p, r: (r, 3 * p + part))


def attend(qkv, away):
    rows = 256
    n = qkv.shape[0]
    return pl.pallas_call(
        attend_kernel,
        grid=(2, n // rows),
        in_specs=[
            column(rows, 0),
            column(n, 1, tall=True), column(n, 2, tall=True),
            column(n, 1, swap=True), column(n, 2, swap=True),
        ],
        out_specs=[
            pl.BlockSpec((rows, 128), lambda p, r: (r, p)),
            pl.BlockSpec((1, 8, rows), lambda p, r: (p, 0, r)),
        ],
        out_shape=[
            jax.ShapeDtypeStruct((n, 256), BF),
            jax.ShapeDtypeStruct((2, 8, n), F32),
        ],
        compiler_params=pltpu.CompilerParams(vmem_limit_bytes=60 * 2**20),
        cost_estimate=pl.CostEstimate(flops=0, bytes_accessed=4096, transcendentals=0),
        name="attend",
    )(qkv, qkv, qkv, away, away)


def attend_back_kernel(
    q_ref, k0_ref, v0_ref, k1_ref, v1_ref, do_ref, lse_ref,
    dq_ref, near_ref, far_ref, dk_acc, dv_acc,
):
    r = pl.program_id(1)
    rows = q_ref.shape[0]
    n = k0_ref.shape[0]
    lane = lax.broadcasted_iota(jnp.int32, (rows, 128), 1)
    k = jnp.concatenate([k0_ref[...], k1_ref[...]], 0)
    v = jnp.concatenate([v0_ref[...], v1_ref[...]], 0)
    q = q_ref[...] * jnp.asarray(0.125, BF)
    do = do_ref[...]
    zero = jnp.zeros_like(q)
    dqs = []
    dk = jnp.zeros((2 * n, 128), F32)
    dv = jnp.zeros((2 * n, 128), F32)
    for h in range(2):
        mine = (lane < HEAD) if h == 0 else (lane >= HEAD)
        qh = jnp.where(mine, q, zero)
        doh = jnp.where(mine, do, zero)
        s = lax.dot_general(k, qh, (((1,), (1,)), ((), ())), preferred_element_type=F32)
        p = jnp.exp(s - lse_ref[0, h : h + 1, :])
        dv = dv + jnp.dot(p.astype(BF), doh, preferred_element_type=F32)
        dp = lax.dot_general(v, doh, (((1,), (1,)), ((), ())), preferred_element_type=F32)
        delta = jnp.sum(p * dp, axis=0, keepdims=True)
        ds = (p * (dp - delta)).astype(BF)
        dk = dk + jnp.dot(ds, qh, preferred_element_type=F32)
        dqs.append(
            lax.dot_general(k, ds, (((0,), (0,)), ((), ())), preferred_element_type=F32)
        )
    sub = lax.broadcasted_iota(jnp.int32, dqs[0].shape, 0)
    dq_ref[...] = (jnp.where(sub < HEAD, dqs[0], dqs[1]) * 0.125).T.astype(BF)

    @pl.when(r == 0)
    def _():
        dk_acc[...] = dk
        dv_acc[...] = dv

    @pl.when(r > 0)
    def _():
        dk_acc[...] += dk
        dv_acc[...] += dv

    @pl.when(r == pl.num_programs(1) - 1)
    def _():
        near_ref[:, :128] = dk_acc[:n]
        near_ref[:, 128:] = dv_acc[:n]
        far_ref[:, :128] = dk_acc[n:].astype(BF)
        far_ref[:, 128:] = dv_acc[n:].astype(BF)


def attend_back(qkv, away, do, lse):
    rows = 256
    n = qkv.shape[0]
    here = pl.BlockSpec((rows, 128), lambda p, r: (r, p))
    shape = jax.ShapeDtypeStruct
    return pl.pallas_call(
        attend_back_kernel,
        grid=(2, n // rows),
        in_specs=[
            column(rows, 0),
            column(n, 1, tall=True), column(n, 2, tall=True),
            column(n, 1, swap=True), column(n, 2, swap=True),
            here,
            pl.BlockSpec((1, 8, rows), lambda p, r: (p, 0, r)),
        ],
        out_specs=[
            here,
            pl.BlockSpec((n, 256), lambda p, r: (0, p)),
            pl.BlockSpec((n, 256), lambda p, r: (0, 1 - p)),
        ],
        out_shape=[shape((n, 256), BF), shape((n, 512), F32), shape((n, 512), BF)],
        scratch_shapes=[pltpu.VMEM((2 * n, 128), F32), pltpu.VMEM((2 * n, 128), F32)],
        compiler_params=pltpu.CompilerParams(vmem_limit_bytes=60 * 2**20),
        cost_estimate=pl.CostEstimate(flops=0, bytes_accessed=4096, transcendentals=0),
        name="attend_back",
    )(qkv, qkv, qkv, away, away, do, lse)


def join_da_kernel(dq, near, far_in, up, w0, w1, dqkv, sums, own, back, ahead, far):
    join_kernel(dq, near, far_in, up, dqkv, sums)
    mixed_kernel(dqkv, w0, w1, own, back, ahead, far)


def join_kernel(dq_ref, near_ref, far_ref, up_ref, out_ref, sums_ref):
    for p in range(2):
        dkv = (near_ref[:, 256 * p : 256 * p + 256] + far_ref[:, 256 * p : 256 * p + 256].astype(F32)).astype(BF)
        dq = dq_ref[:, 128 * p : 128 * p + 128]
        out_ref[:, 384 * p : 384 * p + 128] = dq
        out_ref[:, 384 * p + 128 : 384 * p + 384] = dkv
        sums_ref[p, 0:1, :] = jnp.sum(dq.astype(F32), 0, keepdims=True)
        kv = jnp.sum(dkv.astype(F32), 0, keepdims=True)
        sums_ref[p, 1:2, :] = kv[:, :128]
        sums_ref[p, 2:3, :] = kv[:, 128:]
        sums_ref[p, 3:7, :] = up_ref[p, 0:4, :]
        sums_ref[p, 7:8, :] = jnp.zeros((1, 128), F32)


MM = 2 * 512 * 1024 * 1024


def after(value, *events):
    return lax.optimization_barrier((value, *events))[0]


def gather(shard, *events):
    full = after(jnp.broadcast_to(shard[None], (8, 128, 512)), *events)
    return lax.all_to_all(full, "seq", 0, 0, tiled=True).reshape(1024, 512)


def gather_slow(shard, *events):
    return lax.all_gather(after(shard, *events), "seq", axis=0, tiled=True)


def scatter_slow(g):
    return lax.psum_scatter(g, "seq", scatter_dimension=0, tiled=True)


def sides(full):
    return full, move_core(full)


def scatter(g, *events):
    return lax.all_to_all(after(g, *events), "seq", 0, 0, tiled=True).reshape(8, 128, -1)


def add_up(blocks):
    return jnp.sum(blocks.astype(F32), 0)


def core_sum(own, other):
    return (own + move_core(other).astype(F32)).astype(BF)


def hold(parts, *events):
    return (*parts[:-1], after(parts[-1], *events))


def mix(a_wide, near, p):
    return whole(qkv_kernel, [out((512, 768), BF), all_rows()], *a_wide, *near, p, name="qkv", cols=(384, 0))


def mix_first(x_wide, near, p):
    shapes = [out((512, 768), BF), all_rows()]
    return whole(first_qkv_kernel, shapes, *x_wide, *near, p, name="first_qkv", cols=(384, 0))


def proj(o, near):
    return whole(proj_kernel, spread_out(), o, *near, name="proj", cols=(128, 3))


def middle(z, x, p):
    return whole(
        middle_kernel, [out((TOK, D), F32)] * 2 + [out((TOK, D), BF)], *z, x, p, name="middle"
    )


def all_rows():
    return out((512, D), BF)


def act_out():
    return [out((512, 512), BF)] * 4 + [all_rows()]


def mlp_back(dm_wide, act, w):
    _, up, down = w
    *du, sums, dm_all, own, back, ahead, far = whole(
        mlp_back_kernel,
        [out((512, 512), BF)] * 2 + [out((2, 8, 128), F32), all_rows()] + spread_out(),
        *dm_wide, *down, *up, *act[2:4], name="mlp_back",
    )
    return du, sums, dm_all, (own, back, ahead, far)


def middle_back(da2, x1, dy, z, p):
    return whole(
        middle_back_kernel, [out((TOK, D), F32), out((TOK, D), BF), out((4, D), F32)],
        *da2, x1, dy, z, p, name="middle_back",
    )


def pair_grad(rows, left, right):
    return core_sum(dot(rows, left, TN), dot(rows, right, TN, BF))


def near_grad(a_all, dqkv, dz_all, o):
    own = jnp.concatenate([dot(a_all, dqkv[:, :384], TN), dot(dz_all, o[:, :128], TN)], 1)
    other = jnp.concatenate(
        [dot(a_all, dqkv[:, 384:], TN, BF), dot(dz_all, o[:, 128:], TN, BF)], 1
    )
    return core_sum(own, other)


def back_to(dz_wide, near):
    return whole(do_kernel, [out((512, 256), BF), all_rows()], *dz_wide, *near, name="do", cols=(128, 3))


def join_da(dq, nearby, far, up_sums, near):
    dqkv, sums, *da = whole(
        join_da_kernel,
        [out((512, 768), BF), out((2, 8, 128), F32)] + spread_out(),
        dq, nearby, far, up_sums, *near, name="join_da", cols=(384, 0),
    )
    return dqkv, sums, da


def on_device(ends, w_qkv, qv_bias, w_proj, w_fc1, fc1_bias, w_fc2, vectors):
    sec = lax.axis_index("section")
    seq = lax.axis_index("seq")
    ten = lax.axis_index("tensor")
    first = sec == 0

    lane = jnp.arange(128)[None, :]
    vec = jnp.where(lane // 16 == ten, jnp.tile(vectors[0], (1, 8)), 0.0)
    here = (jnp.arange(8) == seq).astype(F32)[None, :, None]
    qv = qv_bias[0].astype(F32).reshape(2, 2, 8)
    qv = jnp.stack([qv[:, 0], jnp.zeros((2, 8), F32), qv[:, 1]])
    qv = (qv.reshape(6, 1, 8) * here).reshape(3, 128)
    fb = (fc1_bias[0].astype(F32)[:, None, :] * here).reshape(4, 128)
    bias = jnp.concatenate([qv, fb, jnp.zeros((1, 128), F32)], 0)
    both = move_core(jnp.concatenate([vec, bias], 0))
    small = jnp.concatenate([vec + both[:8], bias, both[8:]], 0)
    high = lax.reduce_precision(small, 8, 7)
    mid = lax.reduce_precision(small - high, 8, 7)
    parts = jnp.concatenate([high, mid, small - high - mid, jnp.zeros((8, 128), F32)], 0).astype(BF)

    by_image = jnp.transpose(ends[0].reshape(16, 9, 8, 128), (1, 2, 0, 3)).reshape(9, 128, 128)
    blank = jnp.zeros((128, 128), BF)
    send = jnp.stack([blank if g is None else by_image[g] for g in GROUPS])
    send = jnp.concatenate([send, jnp.broadcast_to(parts[None], (16, 80, 128))], 1)
    got = lax.all_to_all(send, SS, 0, 0, tiled=True)
    x, cot = (
        jnp.transpose(v.reshape(8, 8, 16, 128), (0, 2, 1, 3)).reshape(TOK, D)
        for v in (got[:8, :128], got[8:, :128])
    )
    small = got[:, 128:].astype(F32)
    small = small[:, :24] + small[:, 24:48] + small[:, 48:72]
    vec = small[:, :8]
    vec = vec + move_x(vec, 1) + move_x(vec, -1) + move_x(vec, 2)
    pars = jnp.concatenate([vec, small[:, 8:]], 1)
    p0, p1 = pars[:8], pars[8:]

    own_qkv = jnp.transpose(w_qkv[0].reshape(128, 2, 3, HEAD), (0, 2, 1, 3)).reshape(128, 384)
    shard = jnp.concatenate([own_qkv, w_proj[0].T, w_fc1[0], w_fc2[0].T], 1)
    moved = move_section(shard)
    shards = jnp.where(first, shard, moved), jnp.where(first, moved, shard)
    shards = [[v[:, 512 * k : 512 * k + 512] for v in shards] for k in range(3)]

    def to_owner(a, b):
        other = move_section(jnp.where(first, b, a).astype(BF)).astype(F32)
        return jnp.where(first, a, b) + other

    near0 = gather(shards[0][0], got)
    x_wide0 = widen(x)
    cot_wide = widen(after(cot, *x_wide0))
    near0 = sides(after(near0, p0, *x_wide0))
    qkv0, a_all0 = mix_first(x_wide0, near0, p0)
    away0 = move_core(qkv0)
    up0 = gather(shards[1][0], near0[0], p0)
    o0, lse0 = attend(qkv0, away0)
    dm_wide1 = whole(turn_kernel, [out((TOK, D), BF)] * 4, *cot_wide, p1, name="turn")
    z = proj(o0, near0)
    down0 = gather(shards[2][0], up0, z[3])
    near1 = gather_slow(shards[0][1], z[3])
    up0 = sides(after(up0, z[3], *cot_wide))
    z0, x10, a2 = middle(narrow(z), x, p0)
    down0 = sides(after(down0, x10))
    a2_wide0 = widen(a2)
    *act0, o_, b_, a_, f_ = whole(
        mlp_kernel, act_out() + spread_out(), *a2_wide0, *up0, *down0, p0,
        name="mlp",
    )
    near1 = sides(after(near1, f_))
    up1 = gather_slow(shards[1][1], f_)
    m0, y0, a = whole(
        end_next_kernel, [out((TOK, D), F32), out((TOK, D), BF), out((TOK, D), BF)],
        *narrow((o_, b_, a_, f_)), x10, p0, p1, name="end_next",
    )
    a_wide1 = widen(a)
    qkv1, a_all1 = mix(a_wide1, near1, p1)
    away1 = move_core(qkv1)
    down1 = gather_slow(shards[2][1], qkv1)
    o1, lse1 = attend(qkv1, away1)
    up1 = sides(after(up1, o1))
    z1, x11, a2 = middle(narrow(proj(o1, near1)), y0, p1)
    a2_wide1 = widen(a2)
    down1 = sides(after(down1, x11))
    act1 = whole(up_kernel, act_out(), *a2_wide1, *up1, p1, name="up")

    w1, w0 = (near1, up1, down1), (near0, up0, down0)
    du, up_sums, dm_all, da2 = mlp_back(dm_wide1, act1, w1)
    g_down1 = pair_grad(dm_all, after(act1[0], da2[3]), after(act1[1], da2[3]))
    dx1, dz, mid = middle_back(hold(narrow(da2), g_down1), x11, cot, z1, p1)
    g_down1 = scatter_slow(g_down1)
    dz_wide = widen(dz)
    g_up1 = pair_grad(act1[4], after(du[0], dz), after(du[1], dz))
    m_parts = whole(
        pair_kernel, spread_out(), after(act1[0], da2[3]), act1[1], *down1, name="down"
    )
    dz_wide = hold(dz_wide, g_up1, m_parts[3])
    do, dz_all = back_to(dz_wide, near1)
    m_parts = narrow(lax.optimization_barrier((*m_parts, do))[:4])
    dq, nearby, far = attend_back(qkv1, away1, do, lse1)
    g_up1 = scatter_slow(g_up1)
    dqkv, sums, da = join_da(dq, nearby, after(move_core(far), g_down1, *m_parts), up_sums, near1)
    m1, y1 = whole(
        end_kernel, [out((TOK, D), F32), out((TOK, D), BF)], *m_parts, x11, p1, name="end"
    )
    g_near1 = near_grad(a_all1, dqkv, dz_all, after(o1, da[3]))
    send1, dx, dm0 = whole(
        next_back_kernel,
        [out((8, 176, 128), BF), out((TOK, D), BF), out((TOK, D), BF)],
        *hold(narrow(da), g_near1), y0, dx1, p1, cot, m1, mid, sums, y1, p0, name="next_back",
    )
    g_near1 = scatter_slow(g_near1)
    dm_wide0 = hold(widen(dm0), g_up1)
    du, up_sums, dm_all, da2 = mlp_back(dm_wide0, act0, w0)
    g_down0 = pair_grad(dm_all, after(act0[0], da2[3]), after(act0[1], da2[3]))
    dx1, dz, mid = middle_back(hold(narrow(da2), g_down0, g_near1), x10, dx, z0, p0)
    dz_wide = widen(dz)
    g_up0 = pair_grad(act0[4], after(du[0], dz), after(du[1], dz))
    dz_wide = hold(dz_wide, g_up0)
    do, dz_all = back_to(dz_wide, near0)
    g_pair0 = scatter(jnp.concatenate([g_up0, g_down0], 1), do)
    dq, nearby, far = attend_back(qkv0, away0, do, lse0)
    dqkv, sums, da = join_da(dq, nearby, move_core(far), up_sums, near0)
    da = narrow(da)
    g_near0 = add_up(scatter(near_grad(a_all0, dqkv, dz_all, after(o0, da[0])), da[1]))
    send0 = whole(
        last_back_kernel, out((8, 176, 128), BF),
        *da, x, dx1, p0, dx, m0, mid, sums, name="last_back",
    )

    g_near = to_owner(g_near0, g_near1.astype(F32))
    send0 = after(send0, g_near0)
    g_pair0 = add_up(after(g_pair0, send0))
    g_up = to_owner(g_pair0[:, :512], g_up1.astype(F32))
    g_down = to_owner(g_pair0[:, 512:], g_down1.astype(F32))

    got = lax.all_to_all(jnp.concatenate([send0, send1], 0), SS, 0, 0, tiled=True)
    ends_out = jnp.stack([got[s, :128] for s in SLOT]).reshape(9, 8, 16, 128)
    ends_out = jnp.transpose(ends_out, (2, 0, 1, 3)).reshape(16, 9, D)
    small = jnp.sum(got[:, 128:].astype(F32), 0)
    small = small[:24] + small[24:]
    both = move_core(small)
    vec = small[:8] + both[:8]
    vec = vec + move_x(vec, 1) + move_x(vec, -1) + move_x(vec, 2)
    g_vec = lax.dynamic_slice(vec, (0, ten * 16), (8, 16))
    bias = small[8:16] + both[16:24]
    qv = jnp.stack([bias[0].reshape(2, 64), bias[2].reshape(2, 64)], 1).reshape(4, 64)
    g_qvb = lax.dynamic_slice(qv, (0, seq * 8), (4, 8))
    g_upb = lax.dynamic_slice(bias[3:7].reshape(8, 64), (0, seq * 8), (8, 8))

    g_qkv = jnp.transpose(g_near[:, :384].reshape(128, 3, 2, HEAD), (0, 2, 1, 3)).reshape(128, 384)
    g_out = g_near[:, 384:].T
    return (
        ends_out[None],
        g_qkv[None],
        g_qvb[None],
        g_out[None],
        g_up[None],
        g_upb[None],
        g_down.T[None],
        g_vec[None],
    )


def solution(mesh):
    placed = (
        P("section", ("seq", "tensor"), None, None),
        P("section", "seq", "tensor"),
        P("section", "tensor", "seq"),
        P("section", "tensor", "seq"),
        P("section", "seq", "tensor"),
        P("section", "tensor", "seq"),
        P("section", "tensor", "seq"),
        P("section", None, ("seq", "tensor")),
    )
    return jax.shard_map(
        on_device, mesh=mesh, in_specs=placed, out_specs=placed, check_vma=False
    )
```

time: 704 us -> 577 us (0.82)
  starting transfers between devices: 291 us -> 115 us
  Pallas kernels: 31.3 us -> 128 us
  waiting for transfers between devices: 150 us -> 239 us
  local copies, waits for them, and re-layouts: 106 us -> 38.9 us
  matrix products: 58.8 us -> 20.4 us
  other arithmetic: 47.3 us -> 10.2 us
  between operations: 5.61 us -> 15.8 us
    ppermute x74 -> x0, starting transfers between devices: 190 us -> none  [the longest x56 153 us: scatter_grad(): piece = lax.ppermute(piece, 'seq', [(j, (j + d) % 8) for j in range(5)])]
    pallas_call x4 -> x26, Pallas kernels: 31.3 us -> 128 us  [the longest x22 90.3 us: whole(): pl.pallas_call(kernel, grid=(1,), out_shape=out_shape, in_specs=[entire(a...]
    ppermute x48 -> x54, waiting for transfers between devices: 94.7 us -> 180 us  [move_x(): return lax.ppermute(v, 'tensor', [(i, (i + 2 * d) % 8) for i in range(8)])]
    dot_general x24 -> x16, matrix products: 58.8 us -> 20.4 us  [dot(): lax.dot_general(a, b, (dims, ((), ())), preferred_element_type=F32)]
    ppermute x74 -> x0, waiting for transfers between devices: 29.2 us -> none  [the longest x18 27.7 us: move_yz(): lax.ppermute(v, SS, [(joint(y, z), joint((y + dy) % 4, (z + dz) % 4)) for...]
    slice x68 -> x14, local copies, waits for them, and re-layouts: 25.5 us -> 3.19 us  [the longest x2 1.43 us: on_device(): shards = [[v[:, 512 * k:512 * k + 512] for v in shards] for k in range(3)]]
    reduce_sum x19 -> x3, other arithmetic: 16 us -> 0.48 us  [the longest x2 0.45 us: add_up(): return jnp.sum(blocks.astype(F32), 0)]
    convert_element_type x22 -> x8, other arithmetic: 17.2 us -> 2.43 us  [the longest x2 1.61 us: core_sum(): return (own + move_core(other).astype(F32)).astype(BF)]
  transfers between devices with their start and end apart: 148 -> 89, of which waited for: 41 -> 55; matrix products, arithmetic and copies ran while one was open for 26% -> 7% of each run, Pallas kernels for 5% -> 17%
where the time goes in v2:
time: 577 us; the launch traced here: 567 us
  waiting for transfers between devices  239 us (41%)
  Pallas kernels  128 us (22%)
  starting transfers between devices  115 us (20%)
  local copies, waits for them, and re-layouts  38.9 us (7%)
  matrix products  20.4 us (4%)
  between operations  15.8 us (3%)
  other arithmetic  10.2 us (2%)
    ppermute x54, waiting for transfers between devices, move_x(): return lax.ppermute(v, 'tensor', [(i, (i + 2 * d) % 8) for i in range(8)])  180 us
    pallas_call x22, Pallas kernels, whole(): pl.pallas_call(kernel, grid=(1,), out_shape=out_shape, in_specs=[entire(a...  90.3 us
    ppermute x54, starting transfers between devices, move_x(): return lax.ppermute(v, 'tensor', [(i, (i + 2 * d) % 8) for i in range(8)])  71.8 us
    all_to_all x2, waiting for transfers between devices, scatter(): lax.all_to_all(after(g, *events), 'seq', 0, 0, tiled=True)  23.8 us
    unnamed x222, local copies, waits for them, and re-layouts  23.8 us
    pallas_call x2, Pallas kernels, attend_back(): pl.pallas_call(attend_back_kernel, grid=(2, n // rows), in_specs=[column(...  21.2 us
    dot_general x16, matrix products, dot(): lax.dot_general(a, b, (dims, ((), ())), preferred_element_type=F32)  20.4 us
    pallas_call x2, Pallas kernels, attend(): pl.pallas_call(attend_kernel, grid=(2, n // rows), in_specs=[column(rows,...  16.4 us
  transfers between devices with their start and end apart: 89, of which 55 were waited for; matrix products, arithmetic and copies ran while one was open for 7% of the time, Pallas kernels for 17%

profile of v2, /device:TPU:0, one launch (start us, length us, event | category | flops | bytes accessed | tf_op | source)
XLA Modules:
  0.0 566.9 jit_solution(11659629872261274699)
XLA Ops:
  14.0 4.0 collective-permute-start.4
  19.7 5.0 all-to-all-start
  29.6 11.1 %all-to-all-done = bf16[16,208,128]{2,1,0:T(8,128)(2,1)S(1)} async-done(((bf16[16,208,128]{2,1,0:T(8,128)(2,1)}), bf16[16,208,128]{2,1,0:T(8,128)(2,1)S(1)}, u32[]{:S(2)}, u32[]{:S(2)}) %all-to-all-start) | async-done | bytes 852000 | tf_op jit(solution)/shard_map/all_to_all | solution.py:574
  56.7 4.9 collective-permute-done.3.x3
  68.2 5.3 all-to-all-start.2
  74.5 4.3 first_qkv.1
  82.3 8.2 %attend.2 = (bf16[512,256]{1,0:T(8,128)(2,1)}, f32[2,8,512]{2,1,0:T(8,128)}) custom-call(bf16[512,768]{1,0:T(8,128)(2,1)} %get-tuple-element.144.q_ref.k0_ref.v0_ref, bf16[512,768]{1,0:T(8,128)(2,1)} %get-tuple-element.144.q_ref.k0_ref.v0_ref, bf16[512,768]{1,0:T(8,128)(2,1)} %get-tuple-element.144.q_ref.k0_ref.v0_ref, bf16[512,768]{1,0:T(8,128)(2,1)} %copy-done.3, ...), custom_call_target="tpu_custom_call" | custom-call | bytes 4096 | tf_op jit(solution)/shard_map/attend/pallas_call | solution.py:321
  94.3 5.7 %all-to-all-start.3 = ((bf16[8,128,512]{2,1,0:T(8,128)(2,1)}), bf16[8,128,512]{2,1,0:T(8,128)(2,1)S(1)}, u32[]{:S(2)}, u32[]{:S(2)}) async-start(bf16[8,128,512]{2,1,0:T(8,128)(2,1)} %broadcast_in_dim.70), calls=%async_computation.3 | async-start | bytes 2097152 | tf_op jit(solution)/shard_map/all_to_all | solution.py:450
  107.1 4.7 collective-permute-done.18.refs_3_
  116.6 4.8 collective-permute-done.10.back
  123.0 4.7 collective-permute-done.12.far
  134.3 7.2 %collective-permute-done.15.a3 = bf16[128,1024]{1,0:T(8,128)(2,1)S(1)} collective-permute-done((bf16[128,1024]{1,0:T(8,128)(2,1)}, bf16[128,1024]{1,0:T(8,128)(2,1)S(1)}, u32[]{:S(2)}, u32[]{:S(2)}) %collective-permute-start.15) | collective-permute-done | bytes 262176 | tf_op jit(solution)/shard_map/ppermute | solution.py:20
  148.3 8.1 %mlp.1 = (bf16[512,512]{1,0:T(8,128)(2,1)}, bf16[512,512]{1,0:T(8,128)(2,1)}, bf16[512,512]{1,0:T(8,128)(2,1)}, bf16[512,512]{1,0:T(8,128)(2,1)}, bf16[512,1024]...) custom-call(bf16[128,1024]{1,0:T(8,128)(2,1)} %get-tuple-element.150, ...), custom_call_target="tpu_custom_call" | custom-call | bytes 4096 | tf_op jit(solution)/shard_map/mlp/pallas_call | solution.py:59
  160.3 5.7 collective-permute-done.21.back
  166.0 7.2 %collective-permute-done.22.ahead = bf16[128,1024]{1,0:T(8,128)(2,1)S(1)} collective-permute-done((bf16[128,1024]{1,0:T(8,128)(2,1)}, bf16[128,1024]{1,0:T(8,128)(2,1)S(1)}, u32[]{:S(2)}, u32[]{:S(2)}) %collective-permute-start.22) | collective-permute-done | bytes 262176 | tf_op jit(solution)/shard_map/ppermute | solution.py:20
  179.7 7.8 %collective-permute-done.26.a3 = bf16[128,1024]{1,0:T(8,128)(2,1)S(1)} collective-permute-done((bf16[128,1024]{1,0:T(8,128)(2,1)}, bf16[128,1024]{1,0:T(8,128)(2,1)S(1)}, u32[]{:S(2)}, u32[]{:S(2)}) %collective-permute-start.26) | collective-permute-done | bytes 262176 | tf_op jit(solution)/shard_map/ppermute | solution.py:20
  192.4 4.2 qkv.1
  200.1 8.2 %attend.3 = (bf16[512,256]{1,0:T(8,128)(2,1)}, f32[2,8,512]{2,1,0:T(8,128)}) custom-call(bf16[512,768]{1,0:T(8,128)(2,1)} %get-tuple-element.164.q_ref.k0_ref.v0_ref, bf16[512,768]{1,0:T(8,128)(2,1)} %get-tuple-element.164.q_ref.k0_ref.v0_ref, bf16[512,768]{1,0:T(8,128)(2,1)} %get-tuple-element.164.q_ref.k0_ref.v0_ref, bf16[512,768]{1,0:T(8,128)(2,1)} %copy-done.4, ...), custom_call_target="tpu_custom_call" | custom-call | bytes 4096 | tf_op jit(solution)/shard_map/attend/pallas_call | solution.py:321
  215.2 5.1 collective-permute-done.29.back
  220.3 7.4 %collective-permute-done.30.ahead = bf16[128,1024]{1,0:T(8,128)(2,1)S(1)} collective-permute-done((bf16[128,1024]{1,0:T(8,128)(2,1)}, bf16[128,1024]{1,0:T(8,128)(2,1)S(1)}, u32[]{:S(2)}, u32[]{:S(2)}) %collective-permute-start.30) | collective-permute-done | bytes 262176 | tf_op jit(solution)/shard_map/ppermute | solution.py:20
  231.1 4.5 all-gather.6.cloned.1.call-done.w0
  246.5 5.2 collective-permute-done.35.a2
  253.5 5.3 up.1
  259.7 8.1 %mlp_back.2 = (bf16[512,512]{1,0:T(8,128)(2,1)}, bf16[512,512]{1,0:T(8,128)(2,1)}, f32[2,8,128]{2,1,0:T(8,128)}, bf16[512,1024]{1,0:T(8,128)(2,1)}, f32[128,1024...) custom-call(bf16[128,1024]{1,0:T(8,128)(2,1)} %get-tuple-element.165.d0, ...), custom_call_target="tpu_custom_call" | custom-call | bytes 4096 | tf_op jit(solution)/shard_map/mlp_back/pallas_call | solution.py:59
  277.0 3.8 collective-permute-done.39.far
  280.8 5.1 collective-permute-done.37.back
  291.8 5.4 down.1
  303.9 4.0 collective-permute-done.43.d3
  307.9 5.1 collective-permute-done.42.d2
  317.3 10.6 %attend_back.2 = (bf16[512,256]{1,0:T(8,128)(2,1)}, f32[512,512]{1,0:T(8,128)}, bf16[512,512]{1,0:T(8,128)(2,1)}) custom-call(bf16[512,768]{1,0:T(8,128)(2,1)} %get-tuple-element.164.q_ref.k0_ref.v0_ref, bf16[512,768]{1,0:T(8,128)(2,1)} %get-tuple-element.164.q_ref.k0_ref.v0_ref, bf16[512,768]{1,0:T(8,128)(2,1)} %get-tuple-element.164.q_ref.k0_ref.v0_ref, ...), custom_call_target="tpu_custom_call" | custom-call | bytes 4096 | tf_op jit(solution)/shard_map/attend_back/pallas_call | solution.py:399
  332.4 10.1 %collective-permute-done.46.back = bf16[128,1024]{1,0:T(8,128)(2,1)S(1)} collective-permute-done((bf16[128,1024]{1,0:T(8,128)(2,1)S(1)}, bf16[128,1024]{1,0:T(8,128)(2,1)S(1)}, u32[]{:S(2)}, u32[]{:S(2)}) %collective-permute-start.46) | collective-permute-done | bytes 262176 | tf_op jit(solution)/shard_map/ppermute | solution.py:20
  346.8 5.0 join_da.2
  377.2 8.3 %collective-permute-done.55.d3 = bf16[128,1024]{1,0:T(8,128)(2,1)S(1)} collective-permute-done((bf16[128,1024]{1,0:T(8,128)(2,1)}, bf16[128,1024]{1,0:T(8,128)(2,1)S(1)}, u32[]{:S(2)}, u32[]{:S(2)}) %collective-permute-start.55) | collective-permute-done | bytes 262176 | tf_op jit(solution)/shard_map/ppermute | solution.py:20
  390.9 8.0 %mlp_back.3 = (bf16[512,512]{1,0:T(8,128)(2,1)}, bf16[512,512]{1,0:T(8,128)(2,1)}, f32[2,8,128]{2,1,0:T(8,128)}, bf16[512,1024]{1,0:T(8,128)(2,1)}, f32[128,1024...) custom-call(bf16[128,1024]{1,0:T(8,128)(2,1)} %get-tuple-element.230.d0, ...), custom_call_target="tpu_custom_call" | custom-call | bytes 4096 | tf_op jit(solution)/shard_map/mlp_back/pallas_call | solution.py:59
  404.7 7.2 %collective-permute-done.58.far = bf16[128,1024]{1,0:T(8,128)(2,1)S(1)} collective-permute-done((bf16[128,1024]{1,0:T(8,128)(2,1)S(1)}, bf16[128,1024]{1,0:T(8,128)(2,1)S(1)}, u32[]{:S(2)}, u32[]{:S(2)}) %collective-permute-start.58) | collective-permute-done | bytes 262176 | tf_op jit(solution)/shard_map/ppermute | solution.py:20
  427.8 6.1 %collective-permute-done.62.d3 = bf16[128,1024]{1,0:T(8,128)(2,1)S(1)} collective-permute-done((bf16[128,1024]{1,0:T(8,128)(2,1)S(1)}, bf16[128,1024]{1,0:T(8,128)(2,1)S(1)}, u32[]{:S(2)}, u32[]{:S(2)}) %collective-permute-start.62) | collective-permute-done | bytes 262176 | tf_op jit(solution)/shard_map/ppermute | solution.py:20
  442.6 10.6 %attend_back.3 = (bf16[512,256]{1,0:T(8,128)(2,1)}, f32[512,512]{1,0:T(8,128)}, bf16[512,512]{1,0:T(8,128)(2,1)}) custom-call(bf16[512,768]{1,0:T(8,128)(2,1)} %get-tuple-element.144.q_ref.k0_ref.v0_ref, bf16[512,768]{1,0:T(8,128)(2,1)} %get-tuple-element.144.q_ref.k0_ref.v0_ref, bf16[512,768]{1,0:T(8,128)(2,1)} %get-tuple-element.144.q_ref.k0_ref.v0_ref, ...), custom_call_target="tpu_custom_call" | custom-call | bytes 4096 | tf_op jit(solution)/shard_map/attend_back/pallas_call | solution.py:399
  456.2 5.0 join_da.3
  466.4 5.7 %collective-permute-done.65.back = bf16[128,1024]{1,0:T(8,128)(2,1)S(1)} collective-permute-done((bf16[128,1024]{1,0:T(8,128)(2,1)S(1)}, bf16[128,1024]{1,0:T(8,128)(2,1)S(1)}, u32[]{:S(2)}, u32[]{:S(2)}) %collective-permute-start.65) | collective-permute-done | bytes 262176 | tf_op jit(solution)/shard_map/ppermute | solution.py:20
  473.3 3.6 all-to-all-start.4
  480.0 12.7 %all-to-all-done.4 = bf16[8,128,512]{1,2,0:T(8,128)(2,1)S(1)} async-done(((bf16[8,128,512]{1,2,0:T(8,128)(2,1)}), bf16[8,128,512]{1,2,0:T(8,128)(2,1)S(1)}, u32[]{:S(2)}, u32[]{:S(2)}) %all-to-all-start.4) | async-done | bytes 1048608 | tf_op jit(solution)/shard_map/all_to_all | solution.py:466
  492.7 3.6 all-to-all-start.6
  496.3 4.1 collective-permute-start.67
  500.4 5.7 %collective-permute-done.66.ahead = bf16[128,1024]{1,0:T(8,128)(2,1)S(1)} collective-permute-done((bf16[128,1024]{1,0:T(8,128)(2,1)}, bf16[128,1024]{1,0:T(8,128)(2,1)S(1)}, u32[]{:S(2)}, u32[]{:S(2)}) %collective-permute-start.66) | collective-permute-done | bytes 262176 | tf_op jit(solution)/shard_map/ppermute | solution.py:20
  506.2 5.3 collective-permute-done.67.far
  514.9 11.2 %all-to-all-done.6 = bf16[8,128,1024]{1,2,0:T(8,128)(2,1)S(1)} async-done(((bf16[8,128,1024]{1,2,0:T(8,128)(2,1)}), bf16[8,128,1024]{1,2,0:T(8,128)(2,1)S(1)}, u32[]{:S(2)}, u32[]{:S(2)}) %all-to-all-start.6) | async-done | bytes 2097184 | tf_op jit(solution)/shard_map/all_to_all | solution.py:466
  534.6 3.6 all-to-all-start.5
  541.7 8.3 %all-to-all-done.5 = bf16[16,176,128]{2,1,0:T(8,128)(2,1)S(1)} async-done(((bf16[16,176,128]{2,1,0:T(8,128)(2,1)}), bf16[16,176,128]{2,1,0:T(8,128)(2,1)S(1)}, u32[]{:S(2)}, u32[]{:S(2)}) %all-to-all-start.5) | async-done | bytes 720928 | tf_op jit(solution)/shard_map/all_to_all | solution.py:683
  (486 shorter events, 246.2 us)
Async XLA Ops:
  14.0 13.9 %collective-permute-start.4 = (bf16[128,1536]{1,0:T(8,128)(2,1)S(1)}, bf16[128,1536]{1,0:T(8,128)(2,1)S(1)}, u32[]{:S(2)}, u32[]{:S(2)}) collective-permute-start(bf16[128,1536]{1,0:T(8,128)(2,1)S(1)} %pad_maximum_fusion.5), channel_id=1, source_target_pairs={{0,64},{64,0},{1,65},{65,1},{2,66},{66,2},{3,67},{67,3},{4,68},{68... | collective-permute-start | bytes 1179656 | tf_op jit(solution)/shard_map/ppermute | solution.py:28
  19.7 21.0 %all-to-all-start = ((bf16[16,208,128]{2,1,0:T(8,128)(2,1)}), bf16[16,208,128]{2,1,0:T(8,128)(2,1)S(1)}, u32[]{:S(2)}, u32[]{:S(2)}) async-start(bf16[16,208,128]{2,1,0:T(8,128)(2,1)} %pad_maximum_fusion.3), calls=%async_computation | async-start | bytes 1703936 | tf_op jit(solution)/shard_map/all_to_all | solution.py:574
  41.7 23.8 %all-to-all-start.1 = ((bf16[8,128,512]{2,1,0:T(8,128)(2,1)}), bf16[8,128,512]{2,1,0:T(8,128)(2,1)S(1)}, u32[]{:S(2)}, u32[]{:S(2)}) async-start(bf16[8,128,512]{2,1,0:T(8,128)(2,1)} %broadcast_in_dim.68), calls=%async_computation.1 | async-start | bytes 2097152 | tf_op jit(solution)/shard_map/all_to_all | solution.py:450
  68.2 25.0 %all-to-all-start.2 = ((bf16[8,128,512]{2,1,0:T(8,128)(2,1)}), bf16[8,128,512]{2,1,0:T(8,128)(2,1)S(1)}, u32[]{:S(2)}, u32[]{:S(2)}) async-start(bf16[8,128,512]{2,1,0:T(8,128)(2,1)} %broadcast_in_dim.69), calls=%async_computation.2 | async-start | bytes 2097152 | tf_op jit(solution)/shard_map/all_to_all | solution.py:450
  94.3 36.1 %all-to-all-start.3 = ((bf16[8,128,512]{2,1,0:T(8,128)(2,1)}), bf16[8,128,512]{2,1,0:T(8,128)(2,1)S(1)}, u32[]{:S(2)}, u32[]{:S(2)}) async-start(bf16[8,128,512]{2,1,0:T(8,128)(2,1)} %broadcast_in_dim.70), calls=%async_computation.3 | async-start | bytes 2097152 | tf_op jit(solution)/shard_map/all_to_all | solution.py:450
  100.0 56.4 %all-gather.4.cloned.1.call-start = ((), (), s32[]{:S(2)}) async-start(), calls=%async_computation.10 | async-start | bytes 1179648 | tf_op jit(solution)/shard_map/all_gather | solution.py:454
  100.8 114.4 %all-gather.8.cloned.1.call-start = ((), (), s32[]{:S(2)}) async-start(), calls=%async_computation.12 | async-start | bytes 1179648 | tf_op jit(solution)/shard_map/all_gather | solution.py:454
  102.8 13.1 %collective-permute-start.17 = (bf16[128,1024]{1,0:T(8,128)(2,1)S(1)}, bf16[128,1024]{1,0:T(8,128)(2,1)S(1)}, u32[]{:S(2)}, u32[]{:S(2)}) collective-permute-start(bf16[128,1024]{1,0:T(8,128)(2,1)S(1)} %bitcast.138), channel_id=1, source_target_pairs={{0,6},{1,7},{2,0},{3,1},{4,2},{5,3},{6,4},{7,5},{8,14},{9,15},{10,... | collective-permute-start | bytes 786440 | tf_op jit(solution)/shard_map/ppermute | solution.py:20
  103.9 12.5 %collective-permute-start.16 = (bf16[128,1024]{1,0:T(8,128)(2,1)S(1)}, bf16[128,1024]{1,0:T(8,128)(2,1)S(1)}, u32[]{:S(2)}, u32[]{:S(2)}) collective-permute-start(bf16[128,1024]{1,0:T(8,128)(2,1)S(1)} %bitcast.139), channel_id=1, source_target_pairs={{0,2},{1,3},{2,4},{3,5},{4,6},{5,7},{6,0},{7,1},{8,10},{9,11},{10,... | collective-permute-start | bytes 786440 | tf_op jit(solution)/shard_map/ppermute | solution.py:20
  104.8 16.7 %collective-permute-start.10 = (bf16[128,1024]{1,0:T(8,128)(2,1)}, bf16[128,1024]{1,0:T(8,128)(2,1)S(1)}, u32[]{:S(2)}, u32[]{:S(2)}) collective-permute-start(bf16[128,1024]{1,0:T(8,128)(2,1)} %get-tuple-element.147), channel_id=1, source_target_pairs={{0,6},{1,7},{2,0},{3,1},{4,2},{5,3},{6,4},{7,5},{8,14},{9,15},{10,... | collective-permute-start | bytes 786440 | tf_op jit(solution)/shard_map/ppermute | solution.py:20
  107.1 15.9 %collective-permute-start.11 = (bf16[128,1024]{1,0:T(8,128)(2,1)}, bf16[128,1024]{1,0:T(8,128)(2,1)S(1)}, u32[]{:S(2)}, u32[]{:S(2)}) collective-permute-start(bf16[128,1024]{1,0:T(8,128)(2,1)} %get-tuple-element.148), channel_id=1, source_target_pairs={{0,2},{1,3},{2,4},{3,5},{4,6},{5,7},{6,0},{7,1},{8,10},{9,11},{10,... | collective-permute-start | bytes 786440 | tf_op jit(solution)/shard_map/ppermute | solution.py:20
  111.9 15.8 %collective-permute-start.12 = (bf16[128,1024]{1,0:T(8,128)(2,1)}, bf16[128,1024]{1,0:T(8,128)(2,1)}, u32[]{:S(2)}, u32[]{:S(2)}) collective-permute-start(bf16[128,1024]{1,0:T(8,128)(2,1)} %get-tuple-element.149), channel_id=1, source_target_pairs={{0,4},{1,5},{2,6},{3,7},{4,0},{5,1},{6,2},{7,3},{8,12},{9,13},{10,... | collective-permute-start | bytes 786440 | tf_op jit(solution)/shard_map/ppermute | solution.py:20
  116.4 30.2 %collective-permute-start.19 = (bf16[1024,512]{1,0:T(8,128)(2,1)S(1)}, bf16[1024,512]{1,0:T(8,128)(2,1)S(1)}, u32[]{:S(2)}, u32[]{:S(2)}) collective-permute-start(bf16[1024,512]{1,0:T(8,128)(2,1)S(1)} %bitcast.125), channel_id=1, source_target_pairs={{0,1},{1,0},{2,3},{3,2},{4,5},{5,4},{6,7},{7,6},{8,9},{9,8},{10,11... | collective-permute-start | bytes 3145736 | tf_op jit(solution)/shard_map/ppermute | solution.py:24
  130.5 16.9 %collective-permute-start.20 = (bf16[1024,512]{1,0:T(8,128)(2,1)S(1)}, bf16[1024,512]{1,0:T(8,128)(2,1)}, u32[]{:S(2)}, u32[]{:S(2)}) collective-permute-start(bf16[1024,512]{1,0:T(8,128)(2,1)S(1)} %bitcast.128), channel_id=1, source_target_pairs={{0,1},{1,0},{2,3},{3,2},{4,5},{5,4},{6,7},{7,6},{8,9},{9,8},{10,11... | collective-permute-start | bytes 3145736 | tf_op jit(solution)/shard_map/ppermute | solution.py:24
  132.3 12.7 %collective-permute-start.14 = (bf16[128,1024]{1,0:T(8,128)(2,1)}, bf16[128,1024]{1,0:T(8,128)(2,1)S(1)}, u32[]{:S(2)}, u32[]{:S(2)}) collective-permute-start(bf16[128,1024]{1,0:T(8,128)(2,1)} %get-tuple-element.150.a0), channel_id=1, source_target_pairs={{0,6},{1,7},{2,0},{3,1},{4,2},{5,3},{6,4},{7,5},{8,14},{9,15},{10,... | collective-permute-start | bytes 786440 | tf_op jit(solution)/shard_map/ppermute | solution.py:20
  133.4 13.2 %collective-permute-start.13 = (bf16[128,1024]{1,0:T(8,128)(2,1)}, bf16[128,1024]{1,0:T(8,128)(2,1)S(1)}, u32[]{:S(2)}, u32[]{:S(2)}) collective-permute-start(bf16[128,1024]{1,0:T(8,128)(2,1)} %get-tuple-element.150.a0), channel_id=1, source_target_pairs={{0,2},{1,3},{2,4},{3,5},{4,6},{5,7},{6,0},{7,1},{8,10},{9,11},{10,... | collective-permute-start | bytes 786440 | tf_op jit(solution)/shard_map/ppermute | solution.py:20
  156.4 79.2 %all-gather.6.cloned.1.call-start = ((), (), s32[]{:S(2)}) async-start(), calls=%async_computation.11 | async-start | bytes 1179648 | tf_op jit(solution)/shard_map/all_gather | solution.py:454
  156.5 34.3 %collective-permute-start.27 = (bf16[1024,512]{1,0:T(8,128)(2,1)}, bf16[1024,512]{1,0:T(8,128)(2,1)S(1)}, u32[]{:S(2)}, u32[]{:S(2)}) collective-permute-start(bf16[1024,512]{1,0:T(8,128)(2,1)} %all-gather.4.cloned.1.call-done.w0), channel_id=1, source_target_pairs={{0,1},{1,0},{2,3},{3,2},{4,5},{5,4},{6,7},{7,6},{8,9},{9,8},{10,11... | collective-permute-start | bytes 3145736 | tf_op jit(solution)/shard_map/ppermute | solution.py:24
  157.7 15.4 %collective-permute-start.22 = (bf16[128,1024]{1,0:T(8,128)(2,1)}, bf16[128,1024]{1,0:T(8,128)(2,1)S(1)}, u32[]{:S(2)}, u32[]{:S(2)}) collective-permute-start(bf16[128,1024]{1,0:T(8,128)(2,1)} %get-tuple-element.159), channel_id=1, source_target_pairs={{0,2},{1,3},{2,4},{3,5},{4,6},{5,7},{6,0},{7,1},{8,10},{9,11},{10,... | collective-permute-start | bytes 786440 | tf_op jit(solution)/shard_map/ppermute | solution.py:20
  158.7 14.5 %collective-permute-start.23 = (bf16[128,1024]{1,0:T(8,128)(2,1)}, bf16[128,1024]{1,0:T(8,128)(2,1)S(1)}, u32[]{:S(2)}, u32[]{:S(2)}) collective-permute-start(bf16[128,1024]{1,0:T(8,128)(2,1)} %get-tuple-element.160), channel_id=1, source_target_pairs={{0,4},{1,5},{2,6},{3,7},{4,0},{5,1},{6,2},{7,3},{8,12},{9,13},{10,... | collective-permute-start | bytes 786440 | tf_op jit(solution)/shard_map/ppermute | solution.py:20
  177.7 12.0 %collective-permute-start.25 = (bf16[128,1024]{1,0:T(8,128)(2,1)}, bf16[128,1024]{1,0:T(8,128)(2,1)S(1)}, u32[]{:S(2)}, u32[]{:S(2)}) collective-permute-start(bf16[128,1024]{1,0:T(8,128)(2,1)} %get-tuple-element.161.a0), channel_id=1, source_target_pairs={{0,6},{1,7},{2,0},{3,1},{4,2},{5,3},{6,4},{7,5},{8,14},{9,15},{10,... | collective-permute-start | bytes 786440 | tf_op jit(solution)/shard_map/ppermute | solution.py:20
  178.2 12.6 %collective-permute-start.24 = (bf16[128,1024]{1,0:T(8,128)(2,1)}, bf16[128,1024]{1,0:T(8,128)(2,1)S(1)}, u32[]{:S(2)}, u32[]{:S(2)}) collective-permute-start(bf16[128,1024]{1,0:T(8,128)(2,1)} %get-tuple-element.161.a0), channel_id=1, source_target_pairs={{0,2},{1,3},{2,4},{3,5},{4,6},{5,7},{6,0},{7,1},{8,10},{9,11},{10,... | collective-permute-start | bytes 786440 | tf_op jit(solution)/shard_map/ppermute | solution.py:20
  196.6 149.3 %reduce-scatter.4.cloned.1.call-start = ((), (), s32[]{:S(2)}) async-start(), calls=%async_computation.13 | async-start | bytes 1179648 | tf_op jit(solution)/shard_map/reduce_scatter | solution.py:458
  212.6 15.1 %collective-permute-start.30 = (bf16[128,1024]{1,0:T(8,128)(2,1)}, bf16[128,1024]{1,0:T(8,128)(2,1)S(1)}, u32[]{:S(2)}, u32[]{:S(2)}) collective-permute-start(bf16[128,1024]{1,0:T(8,128)(2,1)} %get-tuple-element.173), channel_id=1, source_target_pairs={{0,2},{1,3},{2,4},{3,5},{4,6},{5,7},{6,0},{7,1},{8,10},{9,11},{10,... | collective-permute-start | bytes 786440 | tf_op jit(solution)/shard_map/ppermute | solution.py:20
  213.0 14.8 %collective-permute-start.31 = (bf16[128,1024]{1,0:T(8,128)(2,1)}, bf16[128,1024]{1,0:T(8,128)(2,1)S(1)}, u32[]{:S(2)}, u32[]{:S(2)}) collective-permute-start(bf16[128,1024]{1,0:T(8,128)(2,1)} %get-tuple-element.174), channel_id=1, source_target_pairs={{0,4},{1,5},{2,6},{3,7},{4,0},{5,1},{6,2},{7,3},{8,12},{9,13},{10,... | collective-permute-start | bytes 786440 | tf_op jit(solution)/shard_map/ppermute | solution.py:20
  215.2 36.5 %collective-permute-start.33 = (bf16[1024,512]{1,0:T(8,128)(2,1)}, bf16[1024,512]{1,0:T(8,128)(2,1)S(1)}, u32[]{:S(2)}, u32[]{:S(2)}) collective-permute-start(bf16[1024,512]{1,0:T(8,128)(2,1)} %all-gather.8.cloned.1.call-done.w0.u0), channel_id=1, source_target_pairs={{0,1},{1,0},{2,3},{3,2},{4,5},{5,4},{6,7},{7,6},{8,9},{9,8},{10,11... | collective-permute-start | bytes 3145736 | tf_op jit(solution)/shard_map/ppermute | solution.py:24
  235.6 23.2 %collective-permute-start.32 = (bf16[1024,512]{1,0:T(8,128)(2,1)}, bf16[1024,512]{1,0:T(8,128)(2,1)S(1)}, u32[]{:S(2)}, u32[]{:S(2)}) collective-permute-start(bf16[1024,512]{1,0:T(8,128)(2,1)} %all-gather.6.cloned.1.call-done.w0), channel_id=1, source_target_pairs={{0,1},{1,0},{2,3},{3,2},{4,5},{5,4},{6,7},{7,6},{8,9},{9,8},{10,11... | collective-permute-start | bytes 3145736 | tf_op jit(solution)/shard_map/ppermute | solution.py:24
  238.7 13.0 %collective-permute-start.35 = (bf16[128,1024]{1,0:T(8,128)(2,1)}, bf16[128,1024]{1,0:T(8,128)(2,1)S(1)}, u32[]{:S(2)}, u32[]{:S(2)}) collective-permute-start(bf16[128,1024]{1,0:T(8,128)(2,1)} %get-tuple-element.180.a0), channel_id=1, source_target_pairs={{0,6},{1,7},{2,0},{3,1},{4,2},{5,3},{6,4},{7,5},{8,14},{9,15},{10,... | collective-permute-start | bytes 786440 | tf_op jit(solution)/shard_map/ppermute | solution.py:20
  273.1 12.8 %collective-permute-start.37 = (bf16[128,1024]{1,0:T(8,128)(2,1)S(1)}, bf16[128,1024]{1,0:T(8,128)(2,1)S(1)}, u32[]{:S(2)}, u32[]{:S(2)}) collective-permute-start(bf16[128,1024]{1,0:T(8,128)(2,1)S(1)} %copy-done.96), channel_id=1, source_target_pairs={{0,6},{1,7},{2,0},{3,1},{4,2},{5,3},{6,4},{7,5},{8,14},{9,15},{10,... | collective-permute-start | bytes 786440 | tf_op jit(solution)/shard_map/ppermute | solution.py:20
  277.0 100.2 %reduce-scatter.6.cloned.1.call-start = ((), (), s32[]{:S(2)}) async-start(), calls=%async_computation.14 | async-start | bytes 1179648 | tf_op jit(solution)/shard_map/reduce_scatter | solution.py:458
  300.1 12.9 %collective-permute-start.42 = (bf16[128,1024]{1,0:T(8,128)(2,1)S(1)}, bf16[128,1024]{1,0:T(8,128)(2,1)S(1)}, u32[]{:S(2)}, u32[]{:S(2)}) collective-permute-start(bf16[128,1024]{1,0:T(8,128)(2,1)S(1)} %copy-done.35), channel_id=1, source_target_pairs={{0,6},{1,7},{2,0},{3,1},{4,2},{5,3},{6,4},{7,5},{8,14},{9,15},{10,... | collective-permute-start | bytes 786440 | tf_op jit(solution)/shard_map/ppermute | solution.py:20
  328.0 17.9 %collective-permute-start.45 = (bf16[512,512]{1,0:T(8,128)(2,1)}, bf16[512,512]{1,0:T(8,128)(2,1)S(1)}, u32[]{:S(2)}, u32[]{:S(2)}) collective-permute-start(bf16[512,512]{1,0:T(8,128)(2,1)} %get-tuple-element.206), channel_id=1, source_target_pairs={{0,1},{1,0},{2,3},{3,2},{4,5},{5,4},{6,7},{7,6},{8,9},{9,8},{10,11... | collective-permute-start | bytes 1572872 | tf_op jit(solution)/shard_map/ppermute | solution.py:24
  328.0 14.5 %collective-permute-start.46 = (bf16[128,1024]{1,0:T(8,128)(2,1)S(1)}, bf16[128,1024]{1,0:T(8,128)(2,1)S(1)}, u32[]{:S(2)}, u32[]{:S(2)}) collective-permute-start(bf16[128,1024]{1,0:T(8,128)(2,1)S(1)} %copy-done.93), channel_id=1, source_target_pairs={{0,6},{1,7},{2,0},{3,1},{4,2},{5,3},{6,4},{7,5},{8,14},{9,15},{10,... | collective-permute-start | bytes 786440 | tf_op jit(solution)/shard_map/ppermute | solution.py:20
  330.7 15.2 %collective-permute-start.47 = (bf16[128,1024]{1,0:T(8,128)(2,1)S(1)}, bf16[128,1024]{1,0:T(8,128)(2,1)S(1)}, u32[]{:S(2)}, u32[]{:S(2)}) collective-permute-start(bf16[128,1024]{1,0:T(8,128)(2,1)S(1)} %copy-done.92), channel_id=1, source_target_pairs={{0,2},{1,3},{2,4},{3,5},{4,6},{5,7},{6,0},{7,1},{8,10},{9,11},{10,... | collective-permute-start | bytes 786440 | tf_op jit(solution)/shard_map/ppermute | solution.py:20
  330.7 15.2 %collective-permute-start.48 = (bf16[128,1024]{1,0:T(8,128)(2,1)S(1)}, bf16[128,1024]{1,0:T(8,128)(2,1)S(1)}, u32[]{:S(2)}, u32[]{:S(2)}) collective-permute-start(bf16[128,1024]{1,0:T(8,128)(2,1)S(1)} %copy-done.91), channel_id=1, source_target_pairs={{0,4},{1,5},{2,6},{3,7},{4,0},{5,1},{6,2},{7,3},{8,12},{9,13},{10,... | collective-permute-start | bytes 786440 | tf_op jit(solution)/shard_map/ppermute | solution.py:20
  332.3 79.6 %reduce-scatter.8.cloned.1.call-start = ((), (), s32[]{:S(2)}) async-start(), calls=%async_computation.15 | async-start | bytes 1179648 | tf_op jit(solution)/shard_map/reduce_scatter | solution.py:458
  354.9 13.1 %collective-permute-start.49 = (bf16[128,1024]{1,0:T(8,128)(2,1)}, bf16[128,1024]{1,0:T(8,128)(2,1)S(1)}, u32[]{:S(2)}, u32[]{:S(2)}) collective-permute-start(bf16[128,1024]{1,0:T(8,128)(2,1)} %get-tuple-element.217), channel_id=1, source_target_pairs={{0,6},{1,7},{2,0},{3,1},{4,2},{5,3},{6,4},{7,5},{8,14},{9,15},{10,... | collective-permute-start | bytes 786440 | tf_op jit(solution)/shard_map/ppermute | solution.py:20
  355.2 15.2 %collective-permute-start.50 = (bf16[128,1024]{1,0:T(8,128)(2,1)}, bf16[128,1024]{1,0:T(8,128)(2,1)S(1)}, u32[]{:S(2)}, u32[]{:S(2)}) collective-permute-start(bf16[128,1024]{1,0:T(8,128)(2,1)} %get-tuple-element.218), channel_id=1, source_target_pairs={{0,2},{1,3},{2,4},{3,5},{4,6},{5,7},{6,0},{7,1},{8,10},{9,11},{10,... | collective-permute-start | bytes 786440 | tf_op jit(solution)/shard_map/ppermute | solution.py:20
  375.1 12.7 %collective-permute-start.54 = (bf16[128,1024]{1,0:T(8,128)(2,1)}, bf16[128,1024]{1,0:T(8,128)(2,1)S(1)}, u32[]{:S(2)}, u32[]{:S(2)}) collective-permute-start(bf16[128,1024]{1,0:T(8,128)(2,1)} %get-tuple-element.230.d0), channel_id=1, source_target_pairs={{0,6},{1,7},{2,0},{3,1},{4,2},{5,3},{6,4},{7,5},{8,14},{9,15},{10,... | collective-permute-start | bytes 786440 | tf_op jit(solution)/shard_map/ppermute | solution.py:20
  376.4 13.8 %collective-permute-start.53 = (bf16[128,1024]{1,0:T(8,128)(2,1)}, bf16[128,1024]{1,0:T(8,128)(2,1)S(1)}, u32[]{:S(2)}, u32[]{:S(2)}) collective-permute-start(bf16[128,1024]{1,0:T(8,128)(2,1)} %get-tuple-element.230.d0), channel_id=1, source_target_pairs={{0,2},{1,3},{2,4},{3,5},{4,6},{5,7},{6,0},{7,1},{8,10},{9,11},{10,... | collective-permute-start | bytes 786440 | tf_op jit(solution)/shard_map/ppermute | solution.py:20
  401.9 13.1 %collective-permute-start.56 = (bf16[128,1024]{1,0:T(8,128)(2,1)}, bf16[128,1024]{1,0:T(8,128)(2,1)S(1)}, u32[]{:S(2)}, u32[]{:S(2)}) collective-permute-start(bf16[128,1024]{1,0:T(8,128)(2,1)} %get-tuple-element.235), channel_id=1, source_target_pairs={{0,6},{1,7},{2,0},{3,1},{4,2},{5,3},{6,4},{7,5},{8,14},{9,15},{10,... | collective-permute-start | bytes 786440 | tf_op jit(solution)/shard_map/ppermute | solution.py:20
  403.1 14.0 %collective-permute-start.57 = (bf16[128,1024]{1,0:T(8,128)(2,1)S(1)}, bf16[128,1024]{1,0:T(8,128)(2,1)S(1)}, u32[]{:S(2)}, u32[]{:S(2)}) collective-permute-start(bf16[128,1024]{1,0:T(8,128)(2,1)S(1)} %copy-done.95), channel_id=1, source_target_pairs={{0,2},{1,3},{2,4},{3,5},{4,6},{5,7},{6,0},{7,1},{8,10},{9,11},{10,... | collective-permute-start | bytes 786440 | tf_op jit(solution)/shard_map/ppermute | solution.py:20
  423.8 13.3 %collective-permute-start.61 = (bf16[128,1024]{1,0:T(8,128)(2,1)S(1)}, bf16[128,1024]{1,0:T(8,128)(2,1)S(1)}, u32[]{:S(2)}, u32[]{:S(2)}) collective-permute-start(bf16[128,1024]{1,0:T(8,128)(2,1)S(1)} %copy-done.39), channel_id=1, source_target_pairs={{0,6},{1,7},{2,0},{3,1},{4,2},{5,3},{6,4},{7,5},{8,14},{9,15},{10,... | collective-permute-start | bytes 786440 | tf_op jit(solution)/shard_map/ppermute | solution.py:20
  425.1 13.9 %collective-permute-start.60 = (bf16[128,1024]{1,0:T(8,128)(2,1)S(1)}, bf16[128,1024]{1,0:T(8,128)(2,1)S(1)}, u32[]{:S(2)}, u32[]{:S(2)}) collective-permute-start(bf16[128,1024]{1,0:T(8,128)(2,1)S(1)} %copy-done.39), channel_id=1, source_target_pairs={{0,2},{1,3},{2,4},{3,5},{4,6},{5,7},{6,0},{7,1},{8,10},{9,11},{10,... | collective-permute-start | bytes 786440 | tf_op jit(solution)/shard_map/ppermute | solution.py:20
  473.3 19.4 %all-to-all-start.4 = ((bf16[8,128,512]{1,2,0:T(8,128)(2,1)}), bf16[8,128,512]{1,2,0:T(8,128)(2,1)S(1)}, u32[]{:S(2)}, u32[]{:S(2)}) async-start(bf16[8,128,512]{1,2,0:T(8,128)(2,1)} %copy_bitcast_fusion.1), calls=%async_computation.7 | async-start | bytes 2097152 | tf_op jit(solution)/shard_map/all_to_all | solution.py:466
  492.7 33.4 %all-to-all-start.6 = ((bf16[8,128,1024]{1,2,0:T(8,128)(2,1)}), bf16[8,128,1024]{1,2,0:T(8,128)(2,1)S(1)}, u32[]{:S(2)}, u32[]{:S(2)}) async-start(bf16[8,128,1024]{1,2,0:T(8,128)(2,1)} %copy_bitcast_fusion), calls=%async_computation.9 | async-start | bytes 4194304 | tf_op jit(solution)/shard_map/all_to_all | solution.py:466
  496.3 15.1 %collective-permute-start.67 = (bf16[128,1024]{1,0:T(8,128)(2,1)}, bf16[128,1024]{1,0:T(8,128)(2,1)}, u32[]{:S(2)}, u32[]{:S(2)}) collective-permute-start(bf16[128,1024]{1,0:T(8,128)(2,1)} %get-tuple-element.262), channel_id=1, source_target_pairs={{0,4},{1,5},{2,6},{3,7},{4,0},{5,1},{6,2},{7,3},{8,12},{9,13},{10,... | collective-permute-start | bytes 786440 | tf_op jit(solution)/shard_map/ppermute | solution.py:20
  534.6 15.3 %all-to-all-start.5 = ((bf16[16,176,128]{2,1,0:T(8,128)(2,1)}), bf16[16,176,128]{2,1,0:T(8,128)(2,1)S(1)}, u32[]{:S(2)}, u32[]{:S(2)}) async-start(bf16[16,176,128]{2,1,0:T(8,128)(2,1)} %pad_maximum_fusion.4), calls=%async_computation.8 | async-start | bytes 1441792 | tf_op jit(solution)/shard_map/all_to_all | solution.py:683
  (141 other events, 954.2 us)
Sparse Core Ops, SparseCore 0:
  102.5 39.4 all-gather.3
  156.5 38.5 all-gather.7
  196.8 38.7 all-gather.5
  277.1 38.6 reduce-scatter.3
  332.4 38.5 reduce-scatter.5
  373.3 38.3 reduce-scatter.7

commit v3 on v2

--- a/solution.py
+++ b/solution.py
@@ -463,7 +463,7 @@
 
 
 def scatter(g, *events):
-    return lax.all_to_all(after(g, *events), "seq", 0, 0, tiled=True).reshape(8, 128, -1)
+    return lax.all_to_all(after(g, *events), "seq", 0, 0, tiled=True).reshape(8, 128, 512)
 
 
 def add_up(blocks):
@@ -602,10 +602,10 @@
     up0 = gather(shards[1][0], near0[0], p0)
     o0, lse0 = attend(qkv0, away0)
     dm_wide1 = whole(turn_kernel, [out((TOK, D), BF)] * 4, *cot_wide, p1, name="turn")
-    z = proj(o0, near0)
+    z = proj(after(o0, *cot_wide), near0)
     down0 = gather(shards[2][0], up0, z[3])
     near1 = gather_slow(shards[0][1], z[3])
-    up0 = sides(after(up0, z[3], *cot_wide))
+    up0 = sides(after(up0, z[3]))
     z0, x10, a2 = middle(narrow(z), x, p0)
     down0 = sides(after(down0, x10))
     a2_wide0 = widen(a2)
@@ -645,7 +645,7 @@
     m_parts = narrow(lax.optimization_barrier((*m_parts, do))[:4])
     dq, nearby, far = attend_back(qkv1, away1, do, lse1)
     g_up1 = scatter_slow(g_up1)
-    dqkv, sums, da = join_da(dq, nearby, after(move_core(far), g_down1, *m_parts), up_sums, near1)
+    dqkv, sums, da = join_da(dq, nearby, after(move_core(after(far, *m_parts)), g_down1), up_sums, near1)
     m1, y1 = whole(
         end_kernel, [out((TOK, D), F32), out((TOK, D), BF)], *m_parts, x11, p1, name="end"
     )
@@ -660,15 +660,16 @@
     du, up_sums, dm_all, da2 = mlp_back(dm_wide0, act0, w0)
     g_down0 = pair_grad(dm_all, after(act0[0], da2[3]), after(act0[1], da2[3]))
     dx1, dz, mid = middle_back(hold(narrow(da2), g_down0, g_near1), x10, dx, z0, p0)
+    g_down0 = scatter_slow(g_down0)
     dz_wide = widen(dz)
     g_up0 = pair_grad(act0[4], after(du[0], dz), after(du[1], dz))
     dz_wide = hold(dz_wide, g_up0)
     do, dz_all = back_to(dz_wide, near0)
-    g_pair0 = scatter(jnp.concatenate([g_up0, g_down0], 1), do)
+    g_up0 = scatter(g_up0, do)
     dq, nearby, far = attend_back(qkv0, away0, do, lse0)
-    dqkv, sums, da = join_da(dq, nearby, move_core(far), up_sums, near0)
+    dqkv, sums, da = join_da(dq, nearby, after(move_core(far), g_up0), up_sums, near0)
     da = narrow(da)
-    g_near0 = add_up(scatter(near_grad(a_all0, dqkv, dz_all, after(o0, da[0])), da[1]))
+    g_near0 = add_up(scatter(near_grad(a_all0, dqkv, dz_all, after(o0, da[0])), g_down0, *da[1:]))
     send0 = whole(
         last_back_kernel, out((8, 176, 128), BF),
         *da, x, dx1, p0, dx, m0, mid, sums, name="last_back",
@@ -676,9 +677,8 @@
 
     g_near = to_owner(g_near0, g_near1.astype(F32))
     send0 = after(send0, g_near0)
-    g_pair0 = add_up(after(g_pair0, send0))
-    g_up = to_owner(g_pair0[:, :512], g_up1.astype(F32))
-    g_down = to_owner(g_pair0[:, 512:], g_down1.astype(F32))
+    g_up = to_owner(add_up(after(g_up0, send0)), g_up1.astype(F32))
+    g_down = to_owner(after(g_down0, send0).astype(F32), g_down1.astype(F32))
 
     got = lax.all_to_all(jnp.concatenate([send0, send1], 0), SS, 0, 0, tiled=True)
     ends_out = jnp.stack([got[s, :128] for s in SLOT]).reshape(9, 8, 16, 128)

time: 577 us -> 555 us (0.962)
  waiting for transfers between devices: 239 us -> 222 us
    ppermute x54, waiting for transfers between devices: 180 us -> 141 us  [move_x(): return lax.ppermute(v, 'tensor', [(i, (i + 2 * d) % 8) for i in range(8)])]
    reduce_scatter x3 -> x4, waiting for transfers between devices: 0.02 us -> 35.1 us  [scatter_slow(): return lax.psum_scatter(g, 'seq', scatter_dimension=0, tiled=True)]
    all_to_all x2, waiting for transfers between devices: 23.8 us -> 11.1 us  [scatter(): lax.all_to_all(after(g, *events), 'seq', 0, 0, tiled=True)]
    unnamed x222 -> x224, local copies, waits for them, and re-layouts: 23.8 us -> 24.4 us
  transfers between devices with their start and end apart: 89 -> 90, of which waited for: 55 -> 50; matrix products, arithmetic and copies ran while one was open for 7% -> 7% of each run, Pallas kernels for 17% -> 21%
where the time goes in v3:
time: 555 us; the launch traced here: 545 us
  waiting for transfers between devices  222 us (40%)
  Pallas kernels  128 us (23%)
  starting transfers between devices  115 us (21%)
  local copies, waits for them, and re-layouts  36.3 us (7%)
  matrix products  20 us (4%)
  between operations  15.8 us (3%)
  other arithmetic  8.65 us (2%)
    ppermute x54, waiting for transfers between devices, move_x(): return lax.ppermute(v, 'tensor', [(i, (i + 2 * d) % 8) for i in range(8)])  141 us
    pallas_call x22, Pallas kernels, whole(): pl.pallas_call(kernel, grid=(1,), out_shape=out_shape, in_specs=[entire(a...  90.8 us
    ppermute x54, starting transfers between devices, move_x(): return lax.ppermute(v, 'tensor', [(i, (i + 2 * d) % 8) for i in range(8)])  71.5 us
    reduce_scatter x4, waiting for transfers between devices, scatter_slow(): return lax.psum_scatter(g, 'seq', scatter_dimension=0, tiled=True)  35.1 us
    unnamed x224, local copies, waits for them, and re-layouts  24.4 us
    pallas_call x2, Pallas kernels, attend_back(): pl.pallas_call(attend_back_kernel, grid=(2, n // rows), in_specs=[column(...  21.1 us
    dot_general x16, matrix products, dot(): lax.dot_general(a, b, (dims, ((), ())), preferred_element_type=F32)  20 us
    pallas_call x2, Pallas kernels, attend(): pl.pallas_call(attend_kernel, grid=(2, n // rows), in_specs=[column(rows,...  16.4 us
  transfers between devices with their start and end apart: 90, of which 50 were waited for; matrix products, arithmetic and copies ran while one was open for 7% of the time, Pallas kernels for 21%

profile of v3, /device:TPU:0, one launch (start us, length us, event | category | flops | bytes accessed | tf_op | source)
XLA Modules:
  0.0 545.2 jit_solution(11284049439498206966)
XLA Ops:
  14.0 4.0 collective-permute-start.4
  19.7 5.0 all-to-all-start
  28.9 11.7 %all-to-all-done = bf16[16,208,128]{2,1,0:T(8,128)(2,1)S(1)} async-done(((bf16[16,208,128]{2,1,0:T(8,128)(2,1)}), bf16[16,208,128]{2,1,0:T(8,128)(2,1)S(1)}, u32[]{:S(2)}, u32[]{:S(2)}) %all-to-all-start) | async-done | bytes 852000 | tf_op jit(solution)/shard_map/all_to_all | solution.py:574
  41.7 3.6 all-to-all-start.1
  56.7 4.9 collective-permute-done.3.x3
  67.0 5.3 all-to-all-start.2
  73.3 4.4 first_qkv.1
  82.5 8.2 %attend.2 = (bf16[512,256]{1,0:T(8,128)(2,1)}, f32[2,8,512]{2,1,0:T(8,128)}) custom-call(bf16[512,768]{1,0:T(8,128)(2,1)} %get-tuple-element.148.q_ref.k0_ref.v0_ref, bf16[512,768]{1,0:T(8,128)(2,1)} %get-tuple-element.148.q_ref.k0_ref.v0_ref, bf16[512,768]{1,0:T(8,128)(2,1)} %get-tuple-element.148.q_ref.k0_ref.v0_ref, bf16[512,768]{1,0:T(8,128)(2,1)} %copy-done.3, ...), custom_call_target="tpu_custom_call" | custom-call | bytes 4096 | tf_op jit(solution)/shard_map/attend/pallas_call | solution.py:321
  97.7 5.7 %all-to-all-start.3 = ((bf16[8,128,512]{2,1,0:T(8,128)(2,1)}), bf16[8,128,512]{2,1,0:T(8,128)(2,1)S(1)}, u32[]{:S(2)}, u32[]{:S(2)}) async-start(bf16[8,128,512]{2,1,0:T(8,128)(2,1)} %broadcast_in_dim.70), calls=%async_computation.3 | async-start | bytes 2097152 | tf_op jit(solution)/shard_map/all_to_all | solution.py:450
  108.2 5.5 %collective-permute-done.13.back = bf16[128,1024]{1,0:T(8,128)(2,1)S(1)} collective-permute-done((bf16[128,1024]{1,0:T(8,128)(2,1)}, bf16[128,1024]{1,0:T(8,128)(2,1)S(1)}, u32[]{:S(2)}, u32[]{:S(2)}) %collective-permute-start.13) | collective-permute-done | bytes 262176 | tf_op jit(solution)/shard_map/ppermute | solution.py:20
  113.7 7.0 %collective-permute-done.14.ahead = bf16[128,1024]{1,0:T(8,128)(2,1)S(1)} collective-permute-done((bf16[128,1024]{1,0:T(8,128)(2,1)}, bf16[128,1024]{1,0:T(8,128)(2,1)S(1)}, u32[]{:S(2)}, u32[]{:S(2)}) %collective-permute-start.14) | collective-permute-done | bytes 262176 | tf_op jit(solution)/shard_map/ppermute | solution.py:20
  127.0 8.3 %collective-permute-done.18.a3 = bf16[128,1024]{1,0:T(8,128)(2,1)S(1)} collective-permute-done((bf16[128,1024]{1,0:T(8,128)(2,1)}, bf16[128,1024]{1,0:T(8,128)(2,1)S(1)}, u32[]{:S(2)}, u32[]{:S(2)}) %collective-permute-start.18) | collective-permute-done | bytes 262176 | tf_op jit(solution)/shard_map/ppermute | solution.py:20
  141.4 8.1 %mlp.1 = (bf16[512,512]{1,0:T(8,128)(2,1)}, bf16[512,512]{1,0:T(8,128)(2,1)}, bf16[512,512]{1,0:T(8,128)(2,1)}, bf16[512,512]{1,0:T(8,128)(2,1)}, bf16[512,1024]...) custom-call(bf16[128,1024]{1,0:T(8,128)(2,1)} %get-tuple-element.156, ...), custom_call_target="tpu_custom_call" | custom-call | bytes 4096 | tf_op jit(solution)/shard_map/mlp/pallas_call | solution.py:59
  152.5 6.6 %collective-permute-done.21.back = bf16[128,1024]{1,0:T(8,128)(2,1)S(1)} collective-permute-done((bf16[128,1024]{1,0:T(8,128)(2,1)}, bf16[128,1024]{1,0:T(8,128)(2,1)S(1)}, u32[]{:S(2)}, u32[]{:S(2)}) %collective-permute-start.21) | collective-permute-done | bytes 262176 | tf_op jit(solution)/shard_map/ppermute | solution.py:20
  159.1 6.7 %collective-permute-done.22.ahead = bf16[128,1024]{1,0:T(8,128)(2,1)S(1)} collective-permute-done((bf16[128,1024]{1,0:T(8,128)(2,1)}, bf16[128,1024]{1,0:T(8,128)(2,1)S(1)}, u32[]{:S(2)}, u32[]{:S(2)}) %collective-permute-start.22) | collective-permute-done | bytes 262176 | tf_op jit(solution)/shard_map/ppermute | solution.py:20
  172.9 7.4 %collective-permute-done.26.a3 = bf16[128,1024]{1,0:T(8,128)(2,1)S(1)} collective-permute-done((bf16[128,1024]{1,0:T(8,128)(2,1)}, bf16[128,1024]{1,0:T(8,128)(2,1)S(1)}, u32[]{:S(2)}, u32[]{:S(2)}) %collective-permute-start.26) | collective-permute-done | bytes 262176 | tf_op jit(solution)/shard_map/ppermute | solution.py:20
  186.0 4.2 qkv.1
  193.8 8.2 %attend.3 = (bf16[512,256]{1,0:T(8,128)(2,1)}, f32[2,8,512]{2,1,0:T(8,128)}) custom-call(bf16[512,768]{1,0:T(8,128)(2,1)} %get-tuple-element.169.q_ref.k0_ref.v0_ref, bf16[512,768]{1,0:T(8,128)(2,1)} %get-tuple-element.169.q_ref.k0_ref.v0_ref, bf16[512,768]{1,0:T(8,128)(2,1)} %get-tuple-element.169.q_ref.k0_ref.v0_ref, bf16[512,768]{1,0:T(8,128)(2,1)} %copy-done.4, ...), custom_call_target="tpu_custom_call" | custom-call | bytes 4096 | tf_op jit(solution)/shard_map/attend/pallas_call | solution.py:321
  208.5 5.5 %collective-permute-done.29.back = bf16[128,1024]{1,0:T(8,128)(2,1)S(1)} collective-permute-done((bf16[128,1024]{1,0:T(8,128)(2,1)}, bf16[128,1024]{1,0:T(8,128)(2,1)S(1)}, u32[]{:S(2)}, u32[]{:S(2)}) %collective-permute-start.29) | collective-permute-done | bytes 262176 | tf_op jit(solution)/shard_map/ppermute | solution.py:20
  214.0 7.0 %collective-permute-done.30.ahead = bf16[128,1024]{1,0:T(8,128)(2,1)S(1)} collective-permute-done((bf16[128,1024]{1,0:T(8,128)(2,1)}, bf16[128,1024]{1,0:T(8,128)(2,1)S(1)}, u32[]{:S(2)}, u32[]{:S(2)}) %collective-permute-start.30) | collective-permute-done | bytes 262176 | tf_op jit(solution)/shard_map/ppermute | solution.py:20
  224.4 4.5 all-gather.6.cloned.1.call-done.w0
  236.2 3.5 collective-permute-done.36.a3
  239.7 5.4 collective-permute-done.35.a2
  247.0 5.3 up.1
  253.2 8.1 %mlp_back.2 = (bf16[512,512]{1,0:T(8,128)(2,1)}, bf16[512,512]{1,0:T(8,128)(2,1)}, f32[2,8,128]{2,1,0:T(8,128)}, bf16[512,1024]{1,0:T(8,128)(2,1)}, f32[128,1024...) custom-call(bf16[128,1024]{1,0:T(8,128)(2,1)} %get-tuple-element.170.d0, ...), custom_call_target="tpu_custom_call" | custom-call | bytes 4096 | tf_op jit(solution)/shard_map/mlp_back/pallas_call | solution.py:59
  270.3 4.0 collective-permute-done.39.far
  274.4 5.1 collective-permute-done.37.back
  285.3 5.4 down.1
  297.3 4.2 collective-permute-done.43.d3
  301.5 5.1 collective-permute-done.42.d2
  315.0 10.5 %attend_back.2 = (bf16[512,256]{1,0:T(8,128)(2,1)}, f32[512,512]{1,0:T(8,128)}, bf16[512,512]{1,0:T(8,128)(2,1)}) custom-call(bf16[512,768]{1,0:T(8,128)(2,1)} %get-tuple-element.169.q_ref.k0_ref.v0_ref, bf16[512,768]{1,0:T(8,128)(2,1)} %get-tuple-element.169.q_ref.k0_ref.v0_ref, bf16[512,768]{1,0:T(8,128)(2,1)} %get-tuple-element.169.q_ref.k0_ref.v0_ref, ...), custom_call_target="tpu_custom_call" | custom-call | bytes 4096 | tf_op jit(solution)/shard_map/attend_back/pallas_call | solution.py:399
  332.7 5.1 join_da.2
  357.0 3.6 next_back.1
  366.6 4.9 collective-permute-done.55.d3
  377.0 8.0 %mlp_back.3 = (bf16[512,512]{1,0:T(8,128)(2,1)}, bf16[512,512]{1,0:T(8,128)(2,1)}, f32[2,8,128]{2,1,0:T(8,128)}, bf16[512,1024]{1,0:T(8,128)(2,1)}, f32[128,1024...) custom-call(bf16[128,1024]{1,0:T(8,128)(2,1)} %get-tuple-element.236.d0, ...), custom_call_target="tpu_custom_call" | custom-call | bytes 4096 | tf_op jit(solution)/shard_map/mlp_back/pallas_call | solution.py:59
  391.8 6.2 %collective-permute-done.58.far = bf16[128,1024]{1,0:T(8,128)(2,1)S(1)} collective-permute-done((bf16[128,1024]{1,0:T(8,128)(2,1)S(1)}, bf16[128,1024]{1,0:T(8,128)(2,1)S(1)}, u32[]{:S(2)}, u32[]{:S(2)}) %collective-permute-start.58) | collective-permute-done | bytes 262176 | tf_op jit(solution)/shard_map/ppermute | solution.py:20
  398.0 9.6 %reduce-scatter.9.cloned.1.call-done = bf16[128,512]{1,0:T(8,128)(2,1)} async-done(((bf16[1024,512]{1,0:T(8,128)(2,1)}), bf16[128,512]{1,0:T(8,128)(2,1)}) %reduce-scatter.9.cloned.1.call-update) | async-done | bytes 131088 | tf_op jit(solution)/shard_map/reduce_scatter | solution.py:458
  419.3 3.9 collective-permute-done.62.d3
  423.2 4.9 collective-permute-done.61.d2
  432.5 3.6 all-to-all-start.4
  436.1 10.6 %attend_back.3 = (bf16[512,256]{1,0:T(8,128)(2,1)}, f32[512,512]{1,0:T(8,128)}, bf16[512,512]{1,0:T(8,128)(2,1)}) custom-call(bf16[512,768]{1,0:T(8,128)(2,1)} %get-tuple-element.148.q_ref.k0_ref.v0_ref, bf16[512,768]{1,0:T(8,128)(2,1)} %get-tuple-element.148.q_ref.k0_ref.v0_ref, bf16[512,768]{1,0:T(8,128)(2,1)} %get-tuple-element.148.q_ref.k0_ref.v0_ref, ...), custom_call_target="tpu_custom_call" | custom-call | bytes 4096 | tf_op jit(solution)/shard_map/attend_back/pallas_call | solution.py:399
  452.0 5.0 join_da.3
  459.2 3.6 collective-permute-start.65
  465.8 22.1 %reduce-scatter.11.cloned.1.call-done = bf16[128,512]{1,0:T(8,128)(2,1)} async-done(((bf16[1024,512]{1,0:T(8,128)(2,1)}), bf16[128,512]{1,0:T(8,128)(2,1)}) %reduce-scatter.11.cloned.1.call-update) | async-done | bytes 131088 | tf_op jit(solution)/shard_map/reduce_scatter | solution.py:458
  489.1 3.6 all-to-all-start.5
  495.9 7.9 %all-to-all-done.5 = bf16[8,128,512]{1,2,0:T(8,128)(2,1)S(1)} async-done(((bf16[8,128,512]{1,2,0:T(8,128)(2,1)}), bf16[8,128,512]{1,2,0:T(8,128)(2,1)S(1)}, u32[]{:S(2)}, u32[]{:S(2)}) %all-to-all-start.5) | async-done | bytes 1048608 | tf_op jit(solution)/shard_map/all_to_all | solution.py:466
  512.3 3.6 all-to-all-start.6
  520.5 6.5 %all-to-all-done.6 = bf16[16,176,128]{2,1,0:T(8,128)(2,1)S(1)} async-done(((bf16[16,176,128]{2,1,0:T(8,128)(2,1)}), bf16[16,176,128]{2,1,0:T(8,128)(2,1)S(1)}, u32[]{:S(2)}, u32[]{:S(2)}) %all-to-all-start.6) | async-done | bytes 720928 | tf_op jit(solution)/shard_map/all_to_all | solution.py:683
  (488 shorter events, 228.1 us)
Async XLA Ops:
  14.0 13.9 %collective-permute-start.4 = (bf16[128,1536]{1,0:T(8,128)(2,1)S(1)}, bf16[128,1536]{1,0:T(8,128)(2,1)S(1)}, u32[]{:S(2)}, u32[]{:S(2)}) collective-permute-start(bf16[128,1536]{1,0:T(8,128)(2,1)S(1)} %pad_maximum_fusion.4), channel_id=1, source_target_pairs={{0,64},{64,0},{1,65},{65,1},{2,66},{66,2},{3,67},{67,3},{4,68},{68... | collective-permute-start | bytes 1179656 | tf_op jit(solution)/shard_map/ppermute | solution.py:28
  19.7 21.0 %all-to-all-start = ((bf16[16,208,128]{2,1,0:T(8,128)(2,1)}), bf16[16,208,128]{2,1,0:T(8,128)(2,1)S(1)}, u32[]{:S(2)}, u32[]{:S(2)}) async-start(bf16[16,208,128]{2,1,0:T(8,128)(2,1)} %pad_maximum_fusion.2), calls=%async_computation | async-start | bytes 1703936 | tf_op jit(solution)/shard_map/all_to_all | solution.py:574
  41.7 23.8 %all-to-all-start.1 = ((bf16[8,128,512]{2,1,0:T(8,128)(2,1)}), bf16[8,128,512]{2,1,0:T(8,128)(2,1)S(1)}, u32[]{:S(2)}, u32[]{:S(2)}) async-start(bf16[8,128,512]{2,1,0:T(8,128)(2,1)} %broadcast_in_dim.68), calls=%async_computation.1 | async-start | bytes 2097152 | tf_op jit(solution)/shard_map/all_to_all | solution.py:450
  67.0 29.5 %all-to-all-start.2 = ((bf16[8,128,512]{2,1,0:T(8,128)(2,1)}), bf16[8,128,512]{2,1,0:T(8,128)(2,1)S(1)}, u32[]{:S(2)}, u32[]{:S(2)}) async-start(bf16[8,128,512]{2,1,0:T(8,128)(2,1)} %broadcast_in_dim.69), calls=%async_computation.2 | async-start | bytes 2097152 | tf_op jit(solution)/shard_map/all_to_all | solution.py:450
  77.8 12.9 %collective-permute-start.12 = (bf16[128,1024]{1,0:T(8,128)(2,1)S(1)}, bf16[128,1024]{1,0:T(8,128)(2,1)S(1)}, u32[]{:S(2)}, u32[]{:S(2)}) collective-permute-start(bf16[128,1024]{1,0:T(8,128)(2,1)S(1)} %bitcast.133), channel_id=1, source_target_pairs={{0,4},{1,5},{2,6},{3,7},{4,0},{5,1},{6,2},{7,3},{8,12},{9,13},{10,... | collective-permute-start | bytes 786440 | tf_op jit(solution)/shard_map/ppermute | solution.py:20
  79.5 12.6 %collective-permute-start.11 = (bf16[128,1024]{1,0:T(8,128)(2,1)S(1)}, bf16[128,1024]{1,0:T(8,128)(2,1)S(1)}, u32[]{:S(2)}, u32[]{:S(2)}) collective-permute-start(bf16[128,1024]{1,0:T(8,128)(2,1)S(1)} %bitcast.134), channel_id=1, source_target_pairs={{0,6},{1,7},{2,0},{3,1},{4,2},{5,3},{6,4},{7,5},{8,14},{9,15},{10,... | collective-permute-start | bytes 786440 | tf_op jit(solution)/shard_map/ppermute | solution.py:20
  80.6 13.1 %collective-permute-start.10 = (bf16[128,1024]{1,0:T(8,128)(2,1)S(1)}, bf16[128,1024]{1,0:T(8,128)(2,1)S(1)}, u32[]{:S(2)}, u32[]{:S(2)}) collective-permute-start(bf16[128,1024]{1,0:T(8,128)(2,1)S(1)} %bitcast.135), channel_id=1, source_target_pairs={{0,2},{1,3},{2,4},{3,5},{4,6},{5,7},{6,0},{7,1},{8,10},{9,11},{10,... | collective-permute-start | bytes 786440 | tf_op jit(solution)/shard_map/ppermute | solution.py:20
  97.7 26.6 %all-to-all-start.3 = ((bf16[8,128,512]{2,1,0:T(8,128)(2,1)}), bf16[8,128,512]{2,1,0:T(8,128)(2,1)S(1)}, u32[]{:S(2)}, u32[]{:S(2)}) async-start(bf16[8,128,512]{2,1,0:T(8,128)(2,1)} %broadcast_in_dim.70), calls=%async_computation.3 | async-start | bytes 2097152 | tf_op jit(solution)/shard_map/all_to_all | solution.py:450
  103.3 46.3 %all-gather.4.cloned.1.call-start = ((), (), s32[]{:S(2)}) async-start(), calls=%async_computation.11 | async-start | bytes 1179648 | tf_op jit(solution)/shard_map/all_gather | solution.py:454
  104.2 104.3 %all-gather.8.cloned.1.call-start = ((), (), s32[]{:S(2)}) async-start(), calls=%async_computation.13 | async-start | bytes 1179648 | tf_op jit(solution)/shard_map/all_gather | solution.py:454
  105.9 14.7 %collective-permute-start.14 = (bf16[128,1024]{1,0:T(8,128)(2,1)}, bf16[128,1024]{1,0:T(8,128)(2,1)S(1)}, u32[]{:S(2)}, u32[]{:S(2)}) collective-permute-start(bf16[128,1024]{1,0:T(8,128)(2,1)} %get-tuple-element.154), channel_id=1, source_target_pairs={{0,2},{1,3},{2,4},{3,5},{4,6},{5,7},{6,0},{7,1},{8,10},{9,11},{10,... | collective-permute-start | bytes 786440 | tf_op jit(solution)/shard_map/ppermute | solution.py:20
  106.3 14.4 %collective-permute-start.15 = (bf16[128,1024]{1,0:T(8,128)(2,1)}, bf16[128,1024]{1,0:T(8,128)(2,1)S(1)}, u32[]{:S(2)}, u32[]{:S(2)}) collective-permute-start(bf16[128,1024]{1,0:T(8,128)(2,1)} %get-tuple-element.155), channel_id=1, source_target_pairs={{0,4},{1,5},{2,6},{3,7},{4,0},{5,1},{6,2},{7,3},{8,12},{9,13},{10,... | collective-permute-start | bytes 786440 | tf_op jit(solution)/shard_map/ppermute | solution.py:20
  108.0 32.4 %collective-permute-start.19 = (bf16[1024,512]{1,0:T(8,128)(2,1)S(1)}, bf16[1024,512]{1,0:T(8,128)(2,1)S(1)}, u32[]{:S(2)}, u32[]{:S(2)}) collective-permute-start(bf16[1024,512]{1,0:T(8,128)(2,1)S(1)} %bitcast.121), channel_id=1, source_target_pairs={{0,1},{1,0},{2,3},{3,2},{4,5},{5,4},{6,7},{7,6},{8,9},{9,8},{10,11... | collective-permute-start | bytes 3145736 | tf_op jit(solution)/shard_map/ppermute | solution.py:24
  124.2 16.2 %collective-permute-start.20 = (bf16[1024,512]{1,0:T(8,128)(2,1)S(1)}, bf16[1024,512]{1,0:T(8,128)(2,1)}, u32[]{:S(2)}, u32[]{:S(2)}) collective-permute-start(bf16[1024,512]{1,0:T(8,128)(2,1)S(1)} %bitcast.124), channel_id=1, source_target_pairs={{0,1},{1,0},{2,3},{3,2},{4,5},{5,4},{6,7},{7,6},{8,9},{9,8},{10,11... | collective-permute-start | bytes 3145736 | tf_op jit(solution)/shard_map/ppermute | solution.py:24
  125.0 13.2 %collective-permute-start.17 = (bf16[128,1024]{1,0:T(8,128)(2,1)}, bf16[128,1024]{1,0:T(8,128)(2,1)S(1)}, u32[]{:S(2)}, u32[]{:S(2)}) collective-permute-start(bf16[128,1024]{1,0:T(8,128)(2,1)} %get-tuple-element.156.a0), channel_id=1, source_target_pairs={{0,6},{1,7},{2,0},{3,1},{4,2},{5,3},{6,4},{7,5},{8,14},{9,15},{10,... | collective-permute-start | bytes 786440 | tf_op jit(solution)/shard_map/ppermute | solution.py:20
  125.4 15.0 %collective-permute-start.16 = (bf16[128,1024]{1,0:T(8,128)(2,1)}, bf16[128,1024]{1,0:T(8,128)(2,1)S(1)}, u32[]{:S(2)}, u32[]{:S(2)}) collective-permute-start(bf16[128,1024]{1,0:T(8,128)(2,1)} %get-tuple-element.156.a0), channel_id=1, source_target_pairs={{0,2},{1,3},{2,4},{3,5},{4,6},{5,7},{6,0},{7,1},{8,10},{9,11},{10,... | collective-permute-start | bytes 786440 | tf_op jit(solution)/shard_map/ppermute | solution.py:20
  149.6 79.3 %all-gather.6.cloned.1.call-start = ((), (), s32[]{:S(2)}) async-start(), calls=%async_computation.12 | async-start | bytes 1179648 | tf_op jit(solution)/shard_map/all_gather | solution.py:454
  149.6 34.7 %collective-permute-start.27 = (bf16[1024,512]{1,0:T(8,128)(2,1)}, bf16[1024,512]{1,0:T(8,128)(2,1)S(1)}, u32[]{:S(2)}, u32[]{:S(2)}) collective-permute-start(bf16[1024,512]{1,0:T(8,128)(2,1)} %all-gather.4.cloned.1.call-done.w0), channel_id=1, source_target_pairs={{0,1},{1,0},{2,3},{3,2},{4,5},{5,4},{6,7},{7,6},{8,9},{9,8},{10,11... | collective-permute-start | bytes 3145736 | tf_op jit(solution)/shard_map/ppermute | solution.py:24
  150.4 15.4 %collective-permute-start.22 = (bf16[128,1024]{1,0:T(8,128)(2,1)}, bf16[128,1024]{1,0:T(8,128)(2,1)S(1)}, u32[]{:S(2)}, u32[]{:S(2)}) collective-permute-start(bf16[128,1024]{1,0:T(8,128)(2,1)} %get-tuple-element.164), channel_id=1, source_target_pairs={{0,2},{1,3},{2,4},{3,5},{4,6},{5,7},{6,0},{7,1},{8,10},{9,11},{10,... | collective-permute-start | bytes 786440 | tf_op jit(solution)/shard_map/ppermute | solution.py:20
  151.8 14.0 %collective-permute-start.23 = (bf16[128,1024]{1,0:T(8,128)(2,1)}, bf16[128,1024]{1,0:T(8,128)(2,1)S(1)}, u32[]{:S(2)}, u32[]{:S(2)}) collective-permute-start(bf16[128,1024]{1,0:T(8,128)(2,1)} %get-tuple-element.165), channel_id=1, source_target_pairs={{0,4},{1,5},{2,6},{3,7},{4,0},{5,1},{6,2},{7,3},{8,12},{9,13},{10,... | collective-permute-start | bytes 786440 | tf_op jit(solution)/shard_map/ppermute | solution.py:20
  170.9 13.4 %collective-permute-start.24 = (bf16[128,1024]{1,0:T(8,128)(2,1)}, bf16[128,1024]{1,0:T(8,128)(2,1)S(1)}, u32[]{:S(2)}, u32[]{:S(2)}) collective-permute-start(bf16[128,1024]{1,0:T(8,128)(2,1)} %get-tuple-element.166.a0), channel_id=1, source_target_pairs={{0,2},{1,3},{2,4},{3,5},{4,6},{5,7},{6,0},{7,1},{8,10},{9,11},{10,... | collective-permute-start | bytes 786440 | tf_op jit(solution)/shard_map/ppermute | solution.py:20
  190.3 141.6 %reduce-scatter.5.cloned.1.call-start = ((), (), s32[]{:S(2)}) async-start(), calls=%async_computation.14 | async-start | bytes 1179648 | tf_op jit(solution)/shard_map/reduce_scatter | solution.py:458
  205.9 15.1 %collective-permute-start.30 = (bf16[128,1024]{1,0:T(8,128)(2,1)}, bf16[128,1024]{1,0:T(8,128)(2,1)S(1)}, u32[]{:S(2)}, u32[]{:S(2)}) collective-permute-start(bf16[128,1024]{1,0:T(8,128)(2,1)} %get-tuple-element.178), channel_id=1, source_target_pairs={{0,2},{1,3},{2,4},{3,5},{4,6},{5,7},{6,0},{7,1},{8,10},{9,11},{10,... | collective-permute-start | bytes 786440 | tf_op jit(solution)/shard_map/ppermute | solution.py:20
  206.6 14.4 %collective-permute-start.31 = (bf16[128,1024]{1,0:T(8,128)(2,1)}, bf16[128,1024]{1,0:T(8,128)(2,1)S(1)}, u32[]{:S(2)}, u32[]{:S(2)}) collective-permute-start(bf16[128,1024]{1,0:T(8,128)(2,1)} %get-tuple-element.179), channel_id=1, source_target_pairs={{0,4},{1,5},{2,6},{3,7},{4,0},{5,1},{6,2},{7,3},{8,12},{9,13},{10,... | collective-permute-start | bytes 786440 | tf_op jit(solution)/shard_map/ppermute | solution.py:20
  208.5 36.7 %collective-permute-start.33 = (bf16[1024,512]{1,0:T(8,128)(2,1)}, bf16[1024,512]{1,0:T(8,128)(2,1)S(1)}, u32[]{:S(2)}, u32[]{:S(2)}) collective-permute-start(bf16[1024,512]{1,0:T(8,128)(2,1)} %all-gather.8.cloned.1.call-done.w0.u0), channel_id=1, source_target_pairs={{0,1},{1,0},{2,3},{3,2},{4,5},{5,4},{6,7},{7,6},{8,9},{9,8},{10,11... | collective-permute-start | bytes 3145736 | tf_op jit(solution)/shard_map/ppermute | solution.py:24
  228.9 23.4 %collective-permute-start.32 = (bf16[1024,512]{1,0:T(8,128)(2,1)}, bf16[1024,512]{1,0:T(8,128)(2,1)S(1)}, u32[]{:S(2)}, u32[]{:S(2)}) collective-permute-start(bf16[1024,512]{1,0:T(8,128)(2,1)} %all-gather.6.cloned.1.call-done.w0), channel_id=1, source_target_pairs={{0,1},{1,0},{2,3},{3,2},{4,5},{5,4},{6,7},{7,6},{8,9},{9,8},{10,11... | collective-permute-start | bytes 3145736 | tf_op jit(solution)/shard_map/ppermute | solution.py:24
  232.0 13.2 %collective-permute-start.35 = (bf16[128,1024]{1,0:T(8,128)(2,1)}, bf16[128,1024]{1,0:T(8,128)(2,1)S(1)}, u32[]{:S(2)}, u32[]{:S(2)}) collective-permute-start(bf16[128,1024]{1,0:T(8,128)(2,1)} %get-tuple-element.185.a0), channel_id=1, source_target_pairs={{0,6},{1,7},{2,0},{3,1},{4,2},{5,3},{6,4},{7,5},{8,14},{9,15},{10,... | collective-permute-start | bytes 786440 | tf_op jit(solution)/shard_map/ppermute | solution.py:20
  266.5 13.0 %collective-permute-start.37 = (bf16[128,1024]{1,0:T(8,128)(2,1)S(1)}, bf16[128,1024]{1,0:T(8,128)(2,1)S(1)}, u32[]{:S(2)}, u32[]{:S(2)}) collective-permute-start(bf16[128,1024]{1,0:T(8,128)(2,1)S(1)} %copy-done.98), channel_id=1, source_target_pairs={{0,6},{1,7},{2,0},{3,1},{4,2},{5,3},{6,4},{7,5},{8,14},{9,15},{10,... | collective-permute-start | bytes 786440 | tf_op jit(solution)/shard_map/ppermute | solution.py:20
  270.3 96.3 %reduce-scatter.7.cloned.1.call-start = ((), (), s32[]{:S(2)}) async-start(), calls=%async_computation.15 | async-start | bytes 1179648 | tf_op jit(solution)/shard_map/reduce_scatter | solution.py:458
  293.5 13.1 %collective-permute-start.42 = (bf16[128,1024]{1,0:T(8,128)(2,1)S(1)}, bf16[128,1024]{1,0:T(8,128)(2,1)S(1)}, u32[]{:S(2)}, u32[]{:S(2)}) collective-permute-start(bf16[128,1024]{1,0:T(8,128)(2,1)S(1)} %copy-done.36), channel_id=1, source_target_pairs={{0,6},{1,7},{2,0},{3,1},{4,2},{5,3},{6,4},{7,5},{8,14},{9,15},{10,... | collective-permute-start | bytes 786440 | tf_op jit(solution)/shard_map/ppermute | solution.py:20
  310.8 14.7 %collective-permute-start.45 = (bf16[128,1024]{1,0:T(8,128)(2,1)S(1)}, bf16[128,1024]{1,0:T(8,128)(2,1)S(1)}, u32[]{:S(2)}, u32[]{:S(2)}) collective-permute-start(bf16[128,1024]{1,0:T(8,128)(2,1)S(1)} %copy-done.95), channel_id=1, source_target_pairs={{0,6},{1,7},{2,0},{3,1},{4,2},{5,3},{6,4},{7,5},{8,14},{9,15},{10,... | collective-permute-start | bytes 786440 | tf_op jit(solution)/shard_map/ppermute | solution.py:20
  313.5 14.9 %collective-permute-start.46 = (bf16[128,1024]{1,0:T(8,128)(2,1)S(1)}, bf16[128,1024]{1,0:T(8,128)(2,1)S(1)}, u32[]{:S(2)}, u32[]{:S(2)}) collective-permute-start(bf16[128,1024]{1,0:T(8,128)(2,1)S(1)} %copy-done.93), channel_id=1, source_target_pairs={{0,2},{1,3},{2,4},{3,5},{4,6},{5,7},{6,0},{7,1},{8,10},{9,11},{10,... | collective-permute-start | bytes 786440 | tf_op jit(solution)/shard_map/ppermute | solution.py:20
  313.5 14.9 %collective-permute-start.47 = (bf16[128,1024]{1,0:T(8,128)(2,1)S(1)}, bf16[128,1024]{1,0:T(8,128)(2,1)S(1)}, u32[]{:S(2)}, u32[]{:S(2)}) collective-permute-start(bf16[128,1024]{1,0:T(8,128)(2,1)S(1)} %copy-done.92), channel_id=1, source_target_pairs={{0,4},{1,5},{2,6},{3,7},{4,0},{5,1},{6,2},{7,3},{8,12},{9,13},{10,... | collective-permute-start | bytes 786440 | tf_op jit(solution)/shard_map/ppermute | solution.py:20
  329.8 77.8 %reduce-scatter.9.cloned.1.call-start = ((), (), s32[]{:S(2)}) async-start(), calls=%async_computation.16 | async-start | bytes 1179648 | tf_op jit(solution)/shard_map/reduce_scatter | solution.py:458
  340.4 13.6 %collective-permute-start.49 = (bf16[128,1024]{1,0:T(8,128)(2,1)}, bf16[128,1024]{1,0:T(8,128)(2,1)S(1)}, u32[]{:S(2)}, u32[]{:S(2)}) collective-permute-start(bf16[128,1024]{1,0:T(8,128)(2,1)} %get-tuple-element.223), channel_id=1, source_target_pairs={{0,6},{1,7},{2,0},{3,1},{4,2},{5,3},{6,4},{7,5},{8,14},{9,15},{10,... | collective-permute-start | bytes 786440 | tf_op jit(solution)/shard_map/ppermute | solution.py:20
  342.9 13.4 %collective-permute-start.50 = (bf16[128,1024]{1,0:T(8,128)(2,1)S(1)}, bf16[128,1024]{1,0:T(8,128)(2,1)S(1)}, u32[]{:S(2)}, u32[]{:S(2)}) collective-permute-start(bf16[128,1024]{1,0:T(8,128)(2,1)S(1)} %copy-done.94), channel_id=1, source_target_pairs={{0,2},{1,3},{2,4},{3,5},{4,6},{5,7},{6,0},{7,1},{8,10},{9,11},{10,... | collective-permute-start | bytes 786440 | tf_op jit(solution)/shard_map/ppermute | solution.py:20
  361.1 12.8 %collective-permute-start.54 = (bf16[128,1024]{1,0:T(8,128)(2,1)}, bf16[128,1024]{1,0:T(8,128)(2,1)S(1)}, u32[]{:S(2)}, u32[]{:S(2)}) collective-permute-start(bf16[128,1024]{1,0:T(8,128)(2,1)} %get-tuple-element.236.d0), channel_id=1, source_target_pairs={{0,6},{1,7},{2,0},{3,1},{4,2},{5,3},{6,4},{7,5},{8,14},{9,15},{10,... | collective-permute-start | bytes 786440 | tf_op jit(solution)/shard_map/ppermute | solution.py:20
  363.2 13.1 %collective-permute-start.53 = (bf16[128,1024]{1,0:T(8,128)(2,1)}, bf16[128,1024]{1,0:T(8,128)(2,1)S(1)}, u32[]{:S(2)}, u32[]{:S(2)}) collective-permute-start(bf16[128,1024]{1,0:T(8,128)(2,1)} %get-tuple-element.236.d0), channel_id=1, source_target_pairs={{0,2},{1,3},{2,4},{3,5},{4,6},{5,7},{6,0},{7,1},{8,10},{9,11},{10,... | collective-permute-start | bytes 786440 | tf_op jit(solution)/shard_map/ppermute | solution.py:20
  388.0 19.6 %collective-permute-start.56 = (bf16[128,1024]{1,0:T(8,128)(2,1)S(1)}, bf16[128,1024]{1,0:T(8,128)(2,1)S(1)}, u32[]{:S(2)}, u32[]{:S(2)}) collective-permute-start(bf16[128,1024]{1,0:T(8,128)(2,1)S(1)} %copy-done.99), channel_id=1, source_target_pairs={{0,6},{1,7},{2,0},{3,1},{4,2},{5,3},{6,4},{7,5},{8,14},{9,15},{10,... | collective-permute-start | bytes 786440 | tf_op jit(solution)/shard_map/ppermute | solution.py:20
  390.1 17.6 %collective-permute-start.57 = (bf16[128,1024]{1,0:T(8,128)(2,1)S(1)}, bf16[128,1024]{1,0:T(8,128)(2,1)S(1)}, u32[]{:S(2)}, u32[]{:S(2)}) collective-permute-start(bf16[128,1024]{1,0:T(8,128)(2,1)S(1)} %copy-done.97), channel_id=1, source_target_pairs={{0,2},{1,3},{2,4},{3,5},{4,6},{5,7},{6,0},{7,1},{8,10},{9,11},{10,... | collective-permute-start | bytes 786440 | tf_op jit(solution)/shard_map/ppermute | solution.py:20
  415.3 12.8 %collective-permute-start.61 = (bf16[128,1024]{1,0:T(8,128)(2,1)S(1)}, bf16[128,1024]{1,0:T(8,128)(2,1)S(1)}, u32[]{:S(2)}, u32[]{:S(2)}) collective-permute-start(bf16[128,1024]{1,0:T(8,128)(2,1)S(1)} %copy-done.40), channel_id=1, source_target_pairs={{0,6},{1,7},{2,0},{3,1},{4,2},{5,3},{6,4},{7,5},{8,14},{9,15},{10,... | collective-permute-start | bytes 786440 | tf_op jit(solution)/shard_map/ppermute | solution.py:20
  432.5 19.5 %all-to-all-start.4 = ((bf16[8,128,512]{2,1,0:T(8,128)(2,1)}), bf16[8,128,512]{2,1,0:T(8,128)(2,1)S(1)}, u32[]{:S(2)}, u32[]{:S(2)}) async-start(bf16[8,128,512]{2,1,0:T(8,128)(2,1)} %bitcast.31), calls=%async_computation.7 | async-start | bytes 2097152 | tf_op jit(solution)/shard_map/all_to_all | solution.py:466
  436.0 51.9 %reduce-scatter.11.cloned.1.call-start = ((), (), s32[]{:S(2)}) async-start(), calls=%async_computation.17 | async-start | bytes 1179648 | tf_op jit(solution)/shard_map/reduce_scatter | solution.py:458
  459.2 28.7 %collective-permute-start.65 = (bf16[128,1024]{1,0:T(8,128)(2,1)}, bf16[128,1024]{1,0:T(8,128)(2,1)S(1)}, u32[]{:S(2)}, u32[]{:S(2)}) collective-permute-start(bf16[128,1024]{1,0:T(8,128)(2,1)} %get-tuple-element.268), channel_id=1, source_target_pairs={{0,6},{1,7},{2,0},{3,1},{4,2},{5,3},{6,4},{7,5},{8,14},{9,15},{10,... | collective-permute-start | bytes 786440 | tf_op jit(solution)/shard_map/ppermute | solution.py:20
  462.8 25.1 %collective-permute-start.66 = (bf16[128,1024]{1,0:T(8,128)(2,1)}, bf16[128,1024]{1,0:T(8,128)(2,1)}, u32[]{:S(2)}, u32[]{:S(2)}) collective-permute-start(bf16[128,1024]{1,0:T(8,128)(2,1)} %get-tuple-element.269), channel_id=1, source_target_pairs={{0,2},{1,3},{2,4},{3,5},{4,6},{5,7},{6,0},{7,1},{8,10},{9,11},{10,... | collective-permute-start | bytes 786440 | tf_op jit(solution)/shard_map/ppermute | solution.py:20
  462.8 25.1 %collective-permute-start.67 = (bf16[128,1024]{1,0:T(8,128)(2,1)}, bf16[128,1024]{1,0:T(8,128)(2,1)}, u32[]{:S(2)}, u32[]{:S(2)}) collective-permute-start(bf16[128,1024]{1,0:T(8,128)(2,1)} %get-tuple-element.270), channel_id=1, source_target_pairs={{0,4},{1,5},{2,6},{3,7},{4,0},{5,1},{6,2},{7,3},{8,12},{9,13},{10,... | collective-permute-start | bytes 786440 | tf_op jit(solution)/shard_map/ppermute | solution.py:20
  489.1 14.7 %all-to-all-start.5 = ((bf16[8,128,512]{1,2,0:T(8,128)(2,1)}), bf16[8,128,512]{1,2,0:T(8,128)(2,1)S(1)}, u32[]{:S(2)}, u32[]{:S(2)}) async-start(bf16[8,128,512]{1,2,0:T(8,128)(2,1)} %copy_bitcast_fusion), calls=%async_computation.9 | async-start | bytes 2097152 | tf_op jit(solution)/shard_map/all_to_all | solution.py:466
  512.3 14.7 %all-to-all-start.6 = ((bf16[16,176,128]{2,1,0:T(8,128)(2,1)}), bf16[16,176,128]{2,1,0:T(8,128)(2,1)S(1)}, u32[]{:S(2)}, u32[]{:S(2)}) async-start(bf16[16,176,128]{2,1,0:T(8,128)(2,1)} %pad_maximum_fusion.3), calls=%async_computation.10 | async-start | bytes 1441792 | tf_op jit(solution)/shard_map/all_to_all | solution.py:683
  (144 other events, 862.1 us)
Sparse Core Ops, SparseCore 0:
  105.8 39.8 all-gather.3
  149.7 37.7 all-gather.7
  190.4 38.4 all-gather.5
  270.4 38.3 reduce-scatter.4
  329.9 36.6 reduce-scatter.6
  368.8 38.7 reduce-scatter.8
  446.8 41.0 reduce-scatter.10
